TPU v7x, 32 devices: a whole 2x2x4 slice. The times are simulated.
32 devices in a mesh: wide: 8 (over y, x, core), narrow: 4 (over z).
Axes of the slice: x: 2, y: 2, z: 4, core: 2. Of those that a mesh axis runs over, the one named last changes fastest.
Arguments:
- views: bfloat16 [8, 4, 256, 576], P('wide', None, 'narrow'), may hold values from -6 to 6
- render_w: float32 [8, 12, 4, 64, 64], P('wide'), may hold values from 0.02 to 0.3
- targets: bfloat16 [8, 12, 3, 16384], P('wide', None, None, 'narrow'), may hold values from 0 to 1
- pix_mask: int32 [8, 12, 16384], P('wide', None, 'narrow'), may hold values 0 or 1
- pairs: int32 [8, 2, 8192], P('wide', None, 'narrow'), may hold values from 0 to 49151
- view_count: int32 [8], P('wide'), may hold values from 1 to 12, as said below
- pair_total: int32 [1], replicated, may hold values from 8192 to 65536
- embed_weight: float32 [576, 1024], P(None, ('wide', 'narrow')), may hold values from -0.25 to 0.25
- embed_first: float32 [576, 1024], P(None, ('wide', 'narrow')), may hold values from -1.9073486e-06 to 1.9073486e-06
- embed_second: float32 [576, 1024], P(None, ('wide', 'narrow')), may hold values from 3.766475e-13 to 1.50659e-12
- mixer_weight: float32 [1024, 3072], P(('wide', 'narrow')), may hold values from -0.1875 to 0.1875
- mixer_first: float32 [1024, 3072], P(('wide', 'narrow')), may hold values from -1.9073486e-06 to 1.9073486e-06
- mixer_second: float32 [1024, 3072], P(('wide', 'narrow')), may hold values from 3.766475e-13 to 1.50659e-12
- merge_weight: float32 [1024, 1024], P(('wide', 'narrow')), may hold values from -0.75 to 0.75
- merge_first: float32 [1024, 1024], P(('wide', 'narrow')), may hold values from -1.9073486e-06 to 1.9073486e-06
- merge_second: float32 [1024, 1024], P(('wide', 'narrow')), may hold values from 3.766475e-13 to 1.50659e-12
- expand_weight: float32 [1024, 4096], P(('wide', 'narrow')), may hold values from -0.1875 to 0.1875
- expand_first: float32 [1024, 4096], P(('wide', 'narrow')), may hold values from -1.9073486e-06 to 1.9073486e-06
- expand_second: float32 [1024, 4096], P(('wide', 'narrow')), may hold values from 3.766475e-13 to 1.50659e-12
- shrink_weight: float32 [4096, 1024], P(('wide', 'narrow')), may hold values from -0.09375 to 0.09375
- shrink_first: float32 [4096, 1024], P(('wide', 'narrow')), may hold values from -1.9073486e-06 to 1.9073486e-06
- shrink_second: float32 [4096, 1024], P(('wide', 'narrow')), may hold values from 3.766475e-13 to 1.50659e-12
- unpatch_weight: float32 [1024, 768], P(('wide', 'narrow')), may hold values from -0.1875 to 0.1875
- unpatch_first: float32 [1024, 768], P(('wide', 'narrow')), may hold values from -1.9073486e-06 to 1.9073486e-06
- unpatch_second: float32 [1024, 768], P(('wide', 'narrow')), may hold values from 3.766475e-13 to 1.50659e-12
- norm_params: float32 [6, 1024], P(None, ('wide', 'narrow')), may hold values from 0.5 to 1.5
- norm_first: float32 [6, 1024], P(None, ('wide', 'narrow')), may hold values from -1.9073486e-06 to 1.9073486e-06
- norm_second: float32 [6, 1024], P(None, ('wide', 'narrow')), may hold values from 3.766475e-13 to 1.50659e-12
Outputs:
- embed_new: float32 [576, 1024], P(None, ('wide', 'narrow'))
- embed_first_new: float32 [576, 1024], P(None, ('wide', 'narrow'))
- embed_second_new: float32 [576, 1024], P(None, ('wide', 'narrow'))
- mixer_new: float32 [1024, 3072], P(('wide', 'narrow'))
- mixer_first_new: float32 [1024, 3072], P(('wide', 'narrow'))
- mixer_second_new: float32 [1024, 3072], P(('wide', 'narrow'))
- merge_new: float32 [1024, 1024], P(('wide', 'narrow'))
- merge_first_new: float32 [1024, 1024], P(('wide', 'narrow'))
- merge_second_new: float32 [1024, 1024], P(('wide', 'narrow'))
- expand_new: float32 [1024, 4096], P(('wide', 'narrow'))
- expand_first_new: float32 [1024, 4096], P(('wide', 'narrow'))
- expand_second_new: float32 [1024, 4096], P(('wide', 'narrow'))
- shrink_new: float32 [4096, 1024], P(('wide', 'narrow'))
- shrink_first_new: float32 [4096, 1024], P(('wide', 'narrow'))
- shrink_second_new: float32 [4096, 1024], P(('wide', 'narrow'))
- unpatch_new: float32 [1024, 768], P(('wide', 'narrow'))
- unpatch_first_new: float32 [1024, 768], P(('wide', 'narrow'))
- unpatch_second_new: float32 [1024, 768], P(('wide', 'narrow'))
- norm_new: float32 [6, 1024], P(None, ('wide', 'narrow'))
- norm_first_new: float32 [6, 1024], P(None, ('wide', 'narrow'))
- norm_second_new: float32 [6, 1024], P(None, ('wide', 'narrow'))
- loss: float32 [], replicated
- grad_norm: float32 [], replicated
Inputs may be any that keep to these rules, and one draw needn't show every extreme that they name: `view_count`: mostly few views; some scene has 12.
All inputs are finite; a program needn't handle non-finite values. No bound on the sum of `pix_mask` on one device may be relied on, other than what follows from the above.
Results may differ from a plain program's by a relative error of at most 0.02.
Values may be sent and summed in bfloat16 or wider, within the bound.
A program may use at most 192 MiB of HBM per device.

v0:
```python
import jax
import jax.numpy as jnp
from jax import lax
from jax.sharding import PartitionSpec as P

D = 1024
HD = 64
P_SIZE = 8
NVIEW = 4
TMAX = 12
STEP = 10


HIGHEST = lax.Precision.HIGHEST
DEPTH_WEIGHT = 1.0
CLIP_NORM = 0.01
BETA_ONE = 0.9
BETA_TWO = 0.95
ADAM_EPS = 1e-08
DECAY = 0.05
RATES = (0.05, 0.05, 0.5, 0.05, 0.05, 0.05, 0.8)


def matmul(left, right):
    return jnp.dot(left, right, preferred_element_type=jnp.float32)


def outer_sum(left, right):
    return lax.dot_general(
        left, right, (((0,), (0,)), ((), ())), preferred_element_type=jnp.float32
    )


def back_mul(grad, weight):
    return lax.dot_general(
        grad, weight, (((1,), (1,)), ((), ())), preferred_element_type=jnp.float32
    )


def layer_norm(values, gain, shift):
    centred = values - jnp.mean(values, -1, keepdims=True)
    spread = jnp.mean(centred * centred, -1, keepdims=True)
    return centred * lax.rsqrt(spread + 1e-05) * gain + shift


def exact_gelu(values):
    return jax.nn.gelu(values, approximate=False)


def render_terms(gaussians, render_weights, target_image, pixel_mask, pair_index, view_total):
    colour = jax.nn.sigmoid(gaussians[:, :, 0:3])
    opacity = jax.nn.sigmoid(gaussians[:, :, 3])
    depth = jax.nn.softplus(gaussians[:, :, 4])
    extent = jax.nn.sigmoid(gaussians[:, :, 5] + gaussians[:, :, 6] + gaussians[:, :, 7])
    rotation = gaussians[:, :, 8:12]
    facing = rotation[:, :, 0] * rotation[:, :, 0] / (1.0 + jnp.sum(rotation * rotation, 2))
    footprint = opacity * extent * facing
    features = jnp.concatenate(
        [colour * footprint[:, :, None], footprint[:, :, None], (depth * footprint)[:, :, None]], 2
    )
    rendered = jnp.einsum("tvap,vqca->tcqp", render_weights, features, precision=HIGHEST)
    pixels = target_image.shape[-1]
    colour_out = rendered[:, 0:3].reshape(TMAX, 3, pixels)
    depth_out = (rendered[:, 4] / (1.0 + rendered[:, 3])).reshape(TMAX * pixels)
    live = (pixel_mask * (jnp.arange(TMAX)[:, None] < view_total)).astype(jnp.float32)
    colour_error = colour_out - target_image
    colour_term = jnp.sum(live[:, None, :] * colour_error * colour_error)
    flat_live = live.reshape(TMAX * pixels)
    pair_live = flat_live[pair_index[0]] * flat_live[pair_index[1]]
    depth_gap = depth_out[pair_index[0]] - depth_out[pair_index[1]]
    return colour_term + DEPTH_WEIGHT * jnp.sum(pair_live * depth_gap * depth_gap)


def attention_forward(queries, keys, values):
    length, heads = (queries.shape[0], queries.shape[1])
    blocked = min(512, length)
    scale = HD ** (-0.5)

    def one_block(query_block):
        scores = (
            jnp.einsum("qhd,khd->hqk", query_block, keys, preferred_element_type=jnp.float32)
            * scale
        )
        highest = jnp.max(scores, -1, keepdims=True)
        exponentials = jnp.exp(scores - highest)
        summed = jnp.sum(exponentials, -1, keepdims=True)
        softmaxed = (exponentials / summed).astype(jnp.bfloat16)
        output = jnp.einsum("hqk,khd->qhd", softmaxed, values, preferred_element_type=jnp.float32)
        return (output.astype(jnp.bfloat16), (highest + jnp.log(summed))[:, :, 0])

    output, logsum = lax.map(one_block, queries.reshape(length // blocked, blocked, heads, HD))
    return (output.reshape(length, heads * HD), logsum)


def attention_backward(queries, keys, values, logsum, out_grad):
    length, heads = (queries.shape[0], queries.shape[1])
    blocked = min(512, length)
    scale = HD ** (-0.5)

    def one_block(carry, inputs):
        key_grad, value_grad = carry
        query_block, logsum_block, grad_block = inputs
        scores = (
            jnp.einsum("qhd,khd->hqk", query_block, keys, preferred_element_type=jnp.float32)
            * scale
        )
        softmaxed = jnp.exp(scores - logsum_block[:, :, None])
        value_grad = value_grad + jnp.einsum(
            "hqk,qhd->khd",
            softmaxed.astype(jnp.bfloat16),
            grad_block,
            preferred_element_type=jnp.float32,
        )
        prob_grad = jnp.einsum(
            "qhd,khd->hqk", grad_block, values, preferred_element_type=jnp.float32
        )
        score_grad = softmaxed * (prob_grad - jnp.sum(softmaxed * prob_grad, -1, keepdims=True))
        score_low = score_grad.astype(jnp.bfloat16)
        query_grad = (
            jnp.einsum("hqk,khd->qhd", score_low, keys, preferred_element_type=jnp.float32) * scale
        )
        key_grad = (
            key_grad
            + jnp.einsum("hqk,qhd->khd", score_low, query_block, preferred_element_type=jnp.float32)
            * scale
        )
        return ((key_grad, value_grad), query_grad)

    zeros = jnp.zeros((length, heads, HD), jnp.float32)
    shaped = (
        queries.reshape(length // blocked, blocked, heads, HD),
        logsum,
        out_grad.reshape(length // blocked, blocked, heads, HD),
    )
    (key_grad, value_grad), query_grad = lax.scan(one_block, (zeros, zeros), shaped)
    return (query_grad.reshape(length, heads, HD), key_grad, value_grad)


def adamw(weight, first, second, grad, rate):
    first = BETA_ONE * first + (1.0 - BETA_ONE) * grad
    second = BETA_TWO * second + (1.0 - BETA_TWO) * grad * grad
    first_hat = first / (1.0 - BETA_ONE**STEP)
    second_hat = second / (1.0 - BETA_TWO**STEP)
    weight = weight - rate * (first_hat / (jnp.sqrt(second_hat) + ADAM_EPS) + DECAY * weight)
    return (weight, first, second)


def body(
    views,
    render_w,
    targets,
    pix_mask,
    pairs,
    view_count,
    pair_total,
    embed_weight,
    embed_first,
    embed_second,
    mixer_weight,
    mixer_first,
    mixer_second,
    merge_weight,
    merge_first,
    merge_second,
    expand_weight,
    expand_first,
    expand_second,
    shrink_weight,
    shrink_first,
    shrink_second,
    unpatch_weight,
    unpatch_first,
    unpatch_second,
    norm_params,
    norm_first,
    norm_second,
):
    masters = (
        embed_weight,
        mixer_weight,
        merge_weight,
        expand_weight,
        shrink_weight,
        unpatch_weight,
        norm_params,
    )
    firsts = (
        embed_first,
        mixer_first,
        merge_first,
        expand_first,
        shrink_first,
        unpatch_first,
        norm_first,
    )
    seconds = (
        embed_second,
        mixer_second,
        merge_second,
        expand_second,
        shrink_second,
        unpatch_second,
        norm_second,
    )
    lowered = [weight.astype(jnp.bfloat16) for weight in masters]
    fetched = (
        lax.all_gather(lowered[0], ("wide", "narrow"), axis=1, tiled=True),
        lax.all_gather(lowered[1], ("wide", "narrow"), axis=0, tiled=True),
        lax.all_gather(lowered[2], ("wide", "narrow"), axis=0, tiled=True),
        lax.all_gather(lowered[3], ("wide", "narrow"), axis=0, tiled=True),
        lax.all_gather(lowered[4], ("wide", "narrow"), axis=0, tiled=True),
        lax.all_gather(lowered[5], ("wide", "narrow"), axis=0, tiled=True),
        lax.all_gather(lowered[6], ("wide", "narrow"), axis=1, tiled=True),
    )
    groups = lax.axis_size("narrow")
    wide_count = lax.axis_size("wide")
    patches = views.reshape(-1, views.shape[-1])
    rows = patches.shape[0]
    gains = fetched[6].astype(jnp.float32)
    embedded = matmul(patches, fetched[0])
    normed_one, norm_back_one = jax.vjp(layer_norm, embedded, gains[0], gains[3])
    normed_one = normed_one.astype(jnp.bfloat16)
    mixed = matmul(normed_one, fetched[1]).astype(jnp.bfloat16).reshape(rows, 3, groups, -1)
    spread = lax.all_to_all(mixed, "narrow", split_axis=2, concat_axis=0, tiled=True)
    length, width = (spread.shape[0], spread.shape[-1])
    local_heads = width // HD
    queries = spread[:, 0, 0].reshape(length, local_heads, HD)
    keys_all = spread[:, 1, 0].reshape(length, local_heads, HD)
    values_all = spread[:, 2, 0].reshape(length, local_heads, HD)
    attended, logsum = attention_forward(queries, keys_all, values_all)
    returned = lax.all_to_all(
        attended.reshape(length, 1, width), "narrow", split_axis=0, concat_axis=1, tiled=True
    ).reshape(rows, D)
    residual_one = embedded + matmul(returned, fetched[2])
    normed_two, norm_back_two = jax.vjp(layer_norm, residual_one, gains[1], gains[4])
    normed_two = normed_two.astype(jnp.bfloat16)
    expanded = matmul(normed_two, fetched[3])
    activated, gelu_back = jax.vjp(exact_gelu, expanded)
    activated = activated.astype(jnp.bfloat16)
    residual_two = residual_one + matmul(activated, fetched[4])
    normed_three, norm_back_three = jax.vjp(layer_norm, residual_two, gains[2], gains[5])
    normed_three = normed_three.astype(jnp.bfloat16)
    gaussians = matmul(normed_three, fetched[5])
    divisor = pair_total[0].astype(jnp.float32)

    def local_loss(values):
        return render_terms(
            values.reshape(NVIEW, -1, 12, P_SIZE * P_SIZE),
            render_w[0],
            targets[0].astype(jnp.float32),
            pix_mask[0],
            pairs[0],
            view_count[0],
        )

    term, render_back = jax.vjp(local_loss, gaussians)
    (gauss_grad,) = render_back(jnp.ones((), jnp.float32) / divisor)
    gauss_grad, relowered = lax.optimization_barrier((gauss_grad, tuple(lowered)))
    weights = (
        lax.all_gather(relowered[0], ("wide", "narrow"), axis=1, tiled=True),
        lax.all_gather(relowered[1], ("wide", "narrow"), axis=0, tiled=True),
        lax.all_gather(relowered[2], ("wide", "narrow"), axis=0, tiled=True),
        lax.all_gather(relowered[3], ("wide", "narrow"), axis=0, tiled=True),
        lax.all_gather(relowered[4], ("wide", "narrow"), axis=0, tiled=True),
        lax.all_gather(relowered[5], ("wide", "narrow"), axis=0, tiled=True),
        lax.all_gather(relowered[6], ("wide", "narrow"), axis=1, tiled=True),
    )
    gauss_low = gauss_grad.astype(jnp.bfloat16)
    grad_unpatch = outer_sum(normed_three, gauss_low)
    residual_grad, gain_three, shift_three = norm_back_three(back_mul(gauss_low, weights[5]))
    shrink_low = residual_grad.astype(jnp.bfloat16)
    grad_shrink = outer_sum(activated, shrink_low)
    (expand_grad,) = gelu_back(back_mul(shrink_low, weights[4]))
    expand_low = expand_grad.astype(jnp.bfloat16)
    grad_expand = outer_sum(normed_two, expand_low)
    through_two, gain_two, shift_two = norm_back_two(back_mul(expand_low, weights[3]))
    residual_grad = residual_grad + through_two
    merge_low = residual_grad.astype(jnp.bfloat16)
    grad_merge = outer_sum(returned, merge_low)
    out_grad = back_mul(merge_low, weights[2]).astype(jnp.bfloat16).reshape(rows, groups, width)
    head_grad = lax.all_to_all(out_grad, "narrow", split_axis=1, concat_axis=0, tiled=True).reshape(
        length, local_heads, HD
    )
    query_grad, key_grad, value_grad = attention_backward(
        queries, keys_all, values_all, logsum, head_grad
    )
    stacked = (
        jnp.stack([query_grad, key_grad, value_grad], 1)
        .astype(jnp.bfloat16)
        .reshape(length, 3, 1, width)
    )
    mixed_grad = lax.all_to_all(stacked, "narrow", split_axis=0, concat_axis=2, tiled=True).reshape(
        rows, 3 * D
    )
    grad_mixer = outer_sum(normed_one, mixed_grad)
    through_one, gain_one, shift_one = norm_back_one(back_mul(mixed_grad, weights[1]))
    embed_grad = (residual_grad + through_one).astype(jnp.bfloat16)
    grad_embed = outer_sum(patches, embed_grad)
    grad_norms = jnp.stack([gain_one, gain_two, gain_three, shift_one, shift_two, shift_three])

    def split_rows(grad):
        return grad.reshape(wide_count, groups, -1, grad.shape[1])

    def split_cols(grad):
        return grad.reshape(grad.shape[0], wide_count, groups, -1)

    partial_sums = (
        lax.psum_scatter(
            split_cols(grad_embed).astype(jnp.bfloat16), "narrow", scatter_dimension=2, tiled=True
        ).astype(jnp.float32),
        lax.psum_scatter(
            split_rows(grad_mixer).astype(jnp.bfloat16), "narrow", scatter_dimension=1, tiled=True
        ).astype(jnp.float32),
        lax.psum_scatter(
            split_rows(grad_merge).astype(jnp.bfloat16), "narrow", scatter_dimension=1, tiled=True
        ).astype(jnp.float32),
        lax.psum_scatter(
            split_rows(grad_expand).astype(jnp.bfloat16), "narrow", scatter_dimension=1, tiled=True
        ).astype(jnp.float32),
        lax.psum_scatter(
            split_rows(grad_shrink).astype(jnp.bfloat16), "narrow", scatter_dimension=1, tiled=True
        ).astype(jnp.float32),
        lax.psum_scatter(
            split_rows(grad_unpatch).astype(jnp.bfloat16), "narrow", scatter_dimension=1, tiled=True
        ).astype(jnp.float32),
        lax.psum_scatter(
            split_cols(grad_norms).astype(jnp.bfloat16), "narrow", scatter_dimension=2, tiled=True
        ).astype(jnp.float32),
    )
    reduced = (
        lax.psum_scatter(
            partial_sums[0].astype(jnp.bfloat16), "wide", scatter_dimension=1, tiled=True
        ).astype(jnp.float32),
        lax.psum_scatter(
            partial_sums[1].astype(jnp.bfloat16), "wide", scatter_dimension=0, tiled=True
        ).astype(jnp.float32),
        lax.psum_scatter(
            partial_sums[2].astype(jnp.bfloat16), "wide", scatter_dimension=0, tiled=True
        ).astype(jnp.float32),
        lax.psum_scatter(
            partial_sums[3].astype(jnp.bfloat16), "wide", scatter_dimension=0, tiled=True
        ).astype(jnp.float32),
        lax.psum_scatter(
            partial_sums[4].astype(jnp.bfloat16), "wide", scatter_dimension=0, tiled=True
        ).astype(jnp.float32),
        lax.psum_scatter(
            partial_sums[5].astype(jnp.bfloat16), "wide", scatter_dimension=0, tiled=True
        ).astype(jnp.float32),
        lax.psum_scatter(
            partial_sums[6].astype(jnp.bfloat16), "wide", scatter_dimension=1, tiled=True
        ).astype(jnp.float32),
    )
    shards = [reduced[which].reshape(masters[which].shape) for which in range(7)]
    squares = sum((jnp.sum(shard * shard) for shard in shards))
    loss_sum, square_sum = lax.psum((term, squares), ("wide", "narrow"))
    loss = loss_sum / divisor
    grad_norm = jnp.sqrt(square_sum)
    factor = jnp.minimum(1.0, CLIP_NORM / (grad_norm + 1e-06))
    updated = [
        adamw(masters[which], firsts[which], seconds[which], shards[which] * factor, RATES[which])
        for which in range(7)
    ]
    return (
        updated[0][0],
        updated[0][1],
        updated[0][2],
        updated[1][0],
        updated[1][1],
        updated[1][2],
        updated[2][0],
        updated[2][1],
        updated[2][2],
        updated[3][0],
        updated[3][1],
        updated[3][2],
        updated[4][0],
        updated[4][1],
        updated[4][2],
        updated[5][0],
        updated[5][1],
        updated[5][2],
        updated[6][0],
        updated[6][1],
        updated[6][2],
        loss,
        grad_norm,
    )


def solution(mesh):
    return jax.shard_map(
        body,
        mesh=mesh,
        in_specs=(
            P("wide", None, "narrow", None),
            P("wide", None, None, None, None),
            P("wide", None, None, "narrow"),
            P("wide", None, "narrow"),
            P("wide", None, "narrow"),
            P("wide"),
            P(),
            P(None, ("wide", "narrow")),
            P(None, ("wide", "narrow")),
            P(None, ("wide", "narrow")),
            P(("wide", "narrow"), None),
            P(("wide", "narrow"), None),
            P(("wide", "narrow"), None),
            P(("wide", "narrow"), None),
            P(("wide", "narrow"), None),
            P(("wide", "narrow"), None),
            P(("wide", "narrow"), None),
            P(("wide", "narrow"), None),
            P(("wide", "narrow"), None),
            P(("wide", "narrow"), None),
            P(("wide", "narrow"), None),
            P(("wide", "narrow"), None),
            P(("wide", "narrow"), None),
            P(("wide", "narrow"), None),
            P(("wide", "narrow"), None),
            P(None, ("wide", "narrow")),
            P(None, ("wide", "narrow")),
            P(None, ("wide", "narrow")),
        ),
        out_specs=(
            P(None, ("wide", "narrow")),
            P(None, ("wide", "narrow")),
            P(None, ("wide", "narrow")),
            P(("wide", "narrow"), None),
            P(("wide", "narrow"), None),
            P(("wide", "narrow"), None),
            P(("wide", "narrow"), None),
            P(("wide", "narrow"), None),
            P(("wide", "narrow"), None),
            P(("wide", "narrow"), None),
            P(("wide", "narrow"), None),
            P(("wide", "narrow"), None),
            P(("wide", "narrow"), None),
            P(("wide", "narrow"), None),
            P(("wide", "narrow"), None),
            P(("wide", "narrow"), None),
            P(("wide", "narrow"), None),
            P(("wide", "narrow"), None),
            P(None, ("wide", "narrow")),
            P(None, ("wide", "narrow")),
            P(None, ("wide", "narrow")),
            P(),
            P(),
        ),
        check_vma=False,
    )
```

profile of v0, /device:TPU:0, one launch (start us, length us, event | category | flops | bytes accessed | tf_op | source)
XLA Modules:
  0.0 2210.4 jit_solution(13537875796928789561)
XLA Ops:
  18.3 70.4 %all-gather = bf16[32,32,6]{1,2,0:T(8,128)(2,1)S(1)} all-gather(bf16[1,32,6]{1,2,0:T(8,128)(2,1)S(1)} %convert_bitcast_fusion), channel_id=1, replica_groups=mesh['wide'=8,'narrow'=4] {'wide','narrow'}, dimensions={0}, use_global_device_ids=true | all-gather | bytes 12672 | tf_op jit(solution)/shard_map/all_gather | solution.py:213
  93.9 46.7 %all-gather.15.cloned.1.call-done = bf16[1024,3072]{1,0:T(8,128)(2,1)} async-done(((bf16[32,3072]{1,0:T(8,128)(2,1)}), bf16[1024,3072]{1,0:T(8,128)(2,1)}) %all-gather.15.cloned.1.call-update) | async-done | bytes 6291472 | tf_op jit(solution)/shard_map/all_gather | solution.py:208
  161.2 36.7 %all-to-all-done = bf16[256,3,4,256]{3,0,1,2:T(8,128)(2,1)S(1)} async-done(((bf16[256,3,4,256]{3,0,1,2:T(8,128)(2,1)}), bf16[256,3,4,256]{3,0,1,2:T(8,128)(2,1)S(1)}, u32[]{:S(2)}, u32[]{:S(2)}) %all-to-all-start) | async-done | bytes 1572896 | tf_op jit(solution)/shard_map/all_to_all | solution.py:224
  202.6 12.3 while.27
  242.0 20.9 gather_fusion
  262.9 20.5 gather_fusion.1
  297.6 16.2 multiply_convert_fusion.1
  313.8 60.1 %all-gather.21.cloned.1.call-done = bf16[4096,1024]{1,0:T(8,128)(2,1)} async-done(((bf16[128,1024]{1,0:T(8,128)(2,1)}), bf16[4096,1024]{1,0:T(8,128)(2,1)}) %all-gather.21.cloned.1.call-update) | async-done | bytes 8388624 | tf_op jit(solution)/shard_map/all_gather | solution.py:211
  373.9 6.6 fusion.169
  381.8 49.1 %all-gather.23.cloned.1.call-done = bf16[1024,768]{1,0:T(8,128)(2,1)} async-done(((bf16[32,768]{1,0:T(8,128)(2,1)}), bf16[1024,768]{1,0:T(8,128)(2,1)}) %all-gather.23.cloned.1.call-update) | async-done | bytes 1572880 | tf_op jit(solution)/shard_map/all_gather | solution.py:212
  464.5 11.8 gather_fusion.2
  476.3 11.8 gather_fusion.3
  488.7 22.1 scatter_custom_fusion
  528.1 51.3 %all-gather.25.cloned.1.call-done = bf16[1024,768]{1,0:T(8,128)(2,1)} async-done(((bf16[32,768]{1,0:T(8,128)(2,1)}), bf16[1024,768]{1,0:T(8,128)(2,1)}) %all-gather.25.cloned.1.call-update) | async-done | bytes 1572880 | tf_op jit(solution)/shard_map/all_gather | solution.py:265
  583.6 75.6 %all-gather.27.cloned.1.call-done = bf16[4096,1024]{1,0:T(8,128)(2,1)} async-done(((bf16[128,1024]{1,0:T(8,128)(2,1)}), bf16[4096,1024]{1,0:T(8,128)(2,1)}) %all-gather.27.cloned.1.call-update) | async-done | bytes 8388624 | tf_op jit(solution)/shard_map/all_gather | solution.py:264
  659.2 11.0 add_convert_fusion
  670.2 68.5 %all-gather.29.cloned.1.call-done = bf16[1024,4096]{1,0:T(8,128)(2,1)} async-done(((bf16[32,4096]{1,0:T(8,128)(2,1)}), bf16[1024,4096]{1,0:T(8,128)(2,1)}) %all-gather.29.cloned.1.call-update) | async-done | bytes 8388624 | tf_op jit(solution)/shard_map/all_gather | solution.py:263
  738.7 7.3 multiply_reduce_fusion.3
  746.6 50.5 %all-gather.31.cloned.1.call-done = bf16[1024,1024]{1,0:T(8,128)(2,1)} async-done(((bf16[32,1024]{1,0:T(8,128)(2,1)}), bf16[1024,1024]{1,0:T(8,128)(2,1)}) %all-gather.31.cloned.1.call-update) | async-done | bytes 2097168 | tf_op jit(solution)/shard_map/all_gather | solution.py:262
  804.2 18.3 all-to-all-done.2
  827.4 35.4 %while.28 = (s32[]{:T(128)}, f32[1024,4,64]{0,2,1:T(8,128)S(1)}, f32[1024,4,64]{0,2,1:T(8,128)}, bf16[2,512,4,64]{1,3,2,0:T(8,128)(2,1)}, bf16[2,512,4,64]{1,3,2...) while((s32[]{:T(128)}, f32[1024,4,64]{0,2,1:T(8,128)S(1)}, ...), condition=%wide.region_19.20_spmd.clone, body=%wide.region_17.19_spmd.clone.sunk | while | flops 1368782848 | bytes 166781296 | solution.py:135
  877.9 7.1 convolution_convert_fusion
  893.2 29.9 %all-to-all-done.3 = bf16[1024,3,1,256]{3,1,2,0:T(4,128)(2,1)} async-done(((bf16[1024,3,1,256]{3,1,2,0:T(4,128)(2,1)}), bf16[1024,3,1,256]{3,1,2,0:T(4,128)(2,1)}, u32[]{:S(2)}, u32[]{:S(2)}) %all-to-all-start.3) | async-done | bytes 1572896 | tf_op jit(solution)/shard_map/all_to_all | solution.py:292
  953.0 928.2 %all-reduce.22.cloned.1.call-done = (bf16[576,8,4,32]{0,3,2,1:T(8,128)(2,1)}, bf16[8,4,32,3072]{3,2,1,0:T(8,128)(2,1)}, bf16[8,4,32,1024]{3,2,1,0:T(8,128)(2,1)}...) async-done(((bf16[576,8,4,32]{0,3,2,1:T(8,128)(2,1)}, bf16[8,4,32,3072]{3,2,1,0:T(8,128)(2,1)}, ...) | async-done | bytes 27918352
  1902.7 24.0 %all-reduce.17 = bf16[6,8,1,32]{3,0,2,1:T(8,128)(2,1)S(1)} all-reduce(bf16[6,8,1,32]{3,0,2,1:T(8,128)(2,1)S(1)} %copy.223), channel_id=15, replica_groups=mesh['wide'=8,'narrow'=4] {'wide'}, use_global_device_ids=true, to_apply=%region_47.48.clone | all-reduce | flops 1536 | bytes 6144
  1928.0 9.5 reduce-scatter.24.cloned.1.call-done
  1938.9 35.9 %reduce-scatter.34.cloned.1.call-done = bf16[1,1,32,768]{3,2,1,0:T(8,128)(2,1)} async-done(((bf16[8,1,32,768]{3,2,1,0:T(8,128)(2,1)}), bf16[1,1,32,768]{3,2,1,0:T(8,128)(2,1)}) %reduce-scatter.34.cloned.1.call-update) | async-done | bytes 49168 | tf_op jit(solution)/shard_map/reduce_scatter | solution.py:346
  1976.2 36.2 %reduce-scatter.28.cloned.1.call-done = bf16[1,1,32,1024]{3,2,1,0:T(8,128)(2,1)} async-done(((bf16[8,1,32,1024]{3,2,1,0:T(8,128)(2,1)}), bf16[1,1,32,1024]{3,2,1,0:T(8,128)(2,1)}) %reduce-scatter.28.cloned.1.call-update) | async-done | bytes 65552 | tf_op jit(solution)/shard_map/reduce_scatter | solution.py:337
  2014.0 40.5 %reduce-scatter.26.cloned.1.call-done = bf16[1,1,32,3072]{3,2,1,0:T(8,128)(2,1)} async-done(((bf16[8,1,32,3072]{3,2,1,0:T(8,128)(2,1)}), bf16[1,1,32,3072]{3,2,1,0:T(8,128)(2,1)}) %reduce-scatter.26.cloned.1.call-update) | async-done | bytes 196624 | tf_op jit(solution)/shard_map/reduce_scatter | solution.py:334
  2058.0 41.1 %reduce-scatter.30.cloned.1.call-done = bf16[1,1,32,4096]{3,2,1,0:T(8,128)(2,1)} async-done(((bf16[8,1,32,4096]{3,2,1,0:T(8,128)(2,1)}), bf16[1,1,32,4096]{3,2,1,0:T(8,128)(2,1)}) %reduce-scatter.30.cloned.1.call-update) | async-done | bytes 262160 | tf_op jit(solution)/shard_map/reduce_scatter | solution.py:340
  2101.6 42.1 %reduce-scatter.32.cloned.1.call-done = bf16[1,1,128,1024]{3,2,1,0:T(8,128)(2,1)} async-done(((bf16[8,1,128,1024]{3,2,1,0:T(8,128)(2,1)}), bf16[1,1,128,1024]{3,2,1,0:T(8,128)(2,1)}) %reduce-scatter.32.cloned.1.call-update) | async-done | bytes 262160 | tf_op jit(solution)/shard_map/reduce_scatter | solution.py:343
  2147.4 39.4 %all-reduce.18 = (f32[]{:T(128)}, f32[]{:T(128)}) all-reduce(f32[]{:T(128)S(6)} %add.428, f32[]{:T(128)S(6)} %add.465), channel_id=1, replica_groups=mesh['wide'=8,'narrow'=4] {'wide','narrow'}, use_global_device_ids=true, to_apply=%region_49.50 | all-reduce | flops 2 | bytes 16 | tf_op jit(solution)/shard_map/psum | solution.py:355
  (441 shorter events, 294.9 us)
Async XLA Ops:
  7.2 452.2 %copy-start = (f32[1,12,4,64,64]{4,3,2,1,0:T(8,128)S(1)}, f32[1,12,4,64,64]{4,3,2,1,0:T(8,128)}, u32[]{:S(2)}) copy-start(f32[1,12,4,64,64]{4,3,2,1,0:T(8,128)} %param.33) | copy-start | bytes 2359300
  7.2 84.3 %all-gather.13.cloned.1.call-start = ((), (), s32[]{:S(2)}) async-start(), calls=%async_computation.11 | async-start | bytes 1351680 | tf_op jit(solution)/shard_map/all_gather | solution.py:207
  8.9 131.6 %all-gather.15.cloned.1.call-start = ((), (), s32[]{:S(2)}) async-start(), calls=%async_computation.12 | async-start | bytes 6488064 | tf_op jit(solution)/shard_map/all_gather | solution.py:208
  10.7 282.8 %all-gather.17.cloned.1.call-start = ((), (), s32[]{:S(2)}) async-start(), calls=%async_computation.13 | async-start | bytes 2162688 | tf_op jit(solution)/shard_map/all_gather | solution.py:209
  12.3 285.3 %all-gather.19.cloned.1.call-start = ((), (), s32[]{:S(2)}) async-start(), calls=%async_computation.14 | async-start | bytes 8650752 | tf_op jit(solution)/shard_map/all_gather | solution.py:210
  14.2 359.7 %all-gather.21.cloned.1.call-start = ((), (), s32[]{:S(2)}) async-start(), calls=%async_computation.15 | async-start | bytes 8650752 | tf_op jit(solution)/shard_map/all_gather | solution.py:211
  16.0 414.8 %all-gather.23.cloned.1.call-start = ((), (), s32[]{:S(2)}) async-start(), calls=%async_computation.16 | async-start | bytes 1622016 | tf_op jit(solution)/shard_map/all_gather | solution.py:212
  153.4 44.4 %all-to-all-start = ((bf16[256,3,4,256]{3,0,1,2:T(8,128)(2,1)}), bf16[256,3,4,256]{3,0,1,2:T(8,128)(2,1)S(1)}, u32[]{:S(2)}, u32[]{:S(2)}) async-start(bf16[256,3,4,256]{3,0,1,2:T(8,128)(2,1)} %copy.191), calls=%async_computation | async-start | bytes 3145728 | tf_op jit(solution)/shard_map/all_to_all | solution.py:224
  230.1 55.8 %all-to-all-start.1 = ((bf16[4,2,32768]{2,1,0:T(2,128)(2,1)}), bf16[4,2,32768]{2,1,0:T(2,128)(2,1)}, u32[]{:S(2)}, u32[]{:S(2)}) async-start(bf16[4,2,32768]{2,1,0:T(2,128)(2,1)} %reshape.528), calls=%async_computation.1 | async-start | bytes 1048576 | tf_op jit(solution)/shard_map/all_to_all | solution.py:231
  234.2 345.1 %all-gather.25.cloned.1.call-start = ((), (), s32[]{:S(2)}) async-start(), calls=%async_computation.17 | async-start | bytes 1622016 | tf_op jit(solution)/shard_map/all_gather | solution.py:265
  525.2 133.9 %all-gather.27.cloned.1.call-start = ((), (), s32[]{:S(2)}) async-start(), calls=%async_computation.18 | async-start | bytes 8650752 | tf_op jit(solution)/shard_map/all_gather | solution.py:264
  526.0 212.7 %all-gather.29.cloned.1.call-start = ((), (), s32[]{:S(2)}) async-start(), calls=%async_computation.19 | async-start | bytes 8650752 | tf_op jit(solution)/shard_map/all_gather | solution.py:263
  526.7 270.4 %all-gather.31.cloned.1.call-start = ((), (), s32[]{:S(2)}) async-start(), calls=%async_computation.20 | async-start | bytes 2162688 | tf_op jit(solution)/shard_map/all_gather | solution.py:262
  527.3 408.4 %all-gather.33.cloned.1.call-start = ((), (), s32[]{:S(2)}) async-start(), calls=%async_computation.21 | async-start | bytes 6488064 | tf_op jit(solution)/shard_map/all_gather | solution.py:261
  800.5 22.0 all-to-all-start.2
  870.8 52.2 %all-to-all-start.3 = ((bf16[1024,3,1,256]{3,1,2,0:T(4,128)(2,1)}), bf16[1024,3,1,256]{3,1,2,0:T(4,128)(2,1)}, u32[]{:S(2)}, u32[]{:S(2)}) async-start(bf16[1024,3,1,256]{3,1,2,0:T(4,128)(2,1)} %copy.217), calls=%async_computation.3 | async-start | bytes 4194304 | tf_op jit(solution)/shard_map/all_to_all | solution.py:292
  875.4 1005.7 %all-reduce.22.cloned.1.call-start = ((), (), s32[]{:S(2)}) async-start(), calls=%async_computation.29 | async-start | bytes 56098816
  950.5 951.5 %reduce-scatter.36.cloned.1.call-start = ((), (), s32[]{:S(2)}) async-start(), calls=%async_computation.28 | async-start | bytes 61440 | tf_op jit(solution)/shard_map/reduce_scatter | solution.py:326
  952.9 984.5 %reduce-scatter.24.cloned.1.call-start = ((), (), s32[]{:S(2)}) async-start(), calls=%async_computation.22 | async-start | bytes 368640 | tf_op jit(solution)/shard_map/reduce_scatter | solution.py:331
  1883.6 91.2 %reduce-scatter.34.cloned.1.call-start = ((), (), s32[]{:S(2)}) async-start(), calls=%async_computation.27 | async-start | bytes 442368 | tf_op jit(solution)/shard_map/reduce_scatter | solution.py:346
  1886.1 126.4 %reduce-scatter.28.cloned.1.call-start = ((), (), s32[]{:S(2)}) async-start(), calls=%async_computation.24 | async-start | bytes 589824 | tf_op jit(solution)/shard_map/reduce_scatter | solution.py:337
  1888.7 165.8 %reduce-scatter.26.cloned.1.call-start = ((), (), s32[]{:S(2)}) async-start(), calls=%async_computation.23 | async-start | bytes 1769472 | tf_op jit(solution)/shard_map/reduce_scatter | solution.py:334
  1892.1 207.0 %reduce-scatter.30.cloned.1.call-start = ((), (), s32[]{:S(2)}) async-start(), calls=%async_computation.25 | async-start | bytes 2359296 | tf_op jit(solution)/shard_map/reduce_scatter | solution.py:340
  1896.0 292.2 %copy-start.89 = (f32[6,32]{1,0:T(8,128)S(1)}, f32[6,32]{1,0:T(8,128)}, u32[]{:S(2)}) copy-start(f32[6,32]{1,0:T(8,128)} %param.58) | copy-start | bytes 2308
  1896.0 292.2 %copy-start.90 = (f32[6,32]{1,0:T(8,128)S(1)}, f32[6,32]{1,0:T(8,128)}, u32[]{:S(2)}) copy-start(f32[6,32]{1,0:T(8,128)} %param.59) | copy-start | bytes 2308
  1896.0 293.5 %copy-start.43 = (f32[576,32]{0,1:T(8,128)S(1)}, f32[576,32]{0,1:T(8,128)}, u32[]{:S(2)}) copy-start(f32[576,32]{0,1:T(8,128)} %param.39) | copy-start | bytes 221188
  1896.0 293.5 %copy-start.49 = (f32[576,32]{0,1:T(8,128)S(1)}, f32[576,32]{0,1:T(8,128)}, u32[]{:S(2)}) copy-start(f32[576,32]{0,1:T(8,128)} %param.40) | copy-start | bytes 221188
  1896.0 293.5 %copy-start.50 = (f32[576,32]{0,1:T(8,128)S(1)}, f32[576,32]{0,1:T(8,128)}, u32[]{:S(2)}) copy-start(f32[576,32]{0,1:T(8,128)} %param.41) | copy-start | bytes 221188
  1896.0 295.0 %copy-start.32 = (f32[32,3072]{1,0:T(8,128)S(1)}, f32[32,3072]{1,0:T(8,128)}, u32[]{:S(2)}) copy-start(f32[32,3072]{1,0:T(8,128)} %param.42) | copy-start | bytes 1179652
  1896.1 247.7 %reduce-scatter.32.cloned.1.call-start = ((), (), s32[]{:S(2)}) async-start(), calls=%async_computation.26 | async-start | bytes 2359296 | tf_op jit(solution)/shard_map/reduce_scatter | solution.py:343
  1900.0 295.4 %copy-start.30 = (f32[32,4096]{1,0:T(8,128)S(1)}, f32[32,4096]{1,0:T(8,128)}, u32[]{:S(2)}) copy-start(f32[32,4096]{1,0:T(8,128)} %param.48) | copy-start | bytes 1572868
  1900.1 298.0 %copy-start.31 = (f32[128,1024]{1,0:T(8,128)S(1)}, f32[128,1024]{1,0:T(8,128)}, u32[]{:S(2)}) copy-start(f32[128,1024]{1,0:T(8,128)} %param.51) | copy-start | bytes 1572868
  (98 other events, 2532.6 us)
Sparse Core Ops, SparseCore 0:
  11.5 57.1 all-gather.12
  72.1 68.4 all-gather.14
  144.0 68.9 all-gather.16
  216.4 78.0 all-gather.18
  297.8 75.9 all-gather.20
  377.2 53.6 all-gather.22
  525.4 53.9 all-gather.24
  582.8 76.2 all-gather.26
  662.7 75.9 all-gather.28
  742.0 55.0 all-gather.30
  800.6 72.6 all-gather.32
  950.6 930.4 all-reduce.21
  1884.1 17.9 reduce-scatter.35
  1905.5 31.9 reduce-scatter.23
  1940.9 33.8 reduce-scatter.33
  1978.3 34.1 reduce-scatter.27
  2016.0 38.4 reduce-scatter.25
  2057.9 41.1 reduce-scatter.29
  2102.4 41.2 reduce-scatter.31
where the time goes:
time: 2220 us; the launch traced here: 2210 us
  waiting for transfers between devices  1620 us (73%)
  local copies, waits for them, and re-layouts  185 us (8%)
  blocking collectives  134 us (6%)
  matrix products  123 us (6%)
  other arithmetic  102 us (5%)
  between operations  26.2 us (1%)
    unnamed x20, waiting for transfers between devices  931 us
    all_gather x1, waiting for transfers between devices, body(): lax.all_gather(relowered[4], ('wide', 'narrow'), axis=0, tiled=True)  75.6 us
    all_gather x1, blocking collectives, body(): lax.all_gather(lowered[6], ('wide', 'narrow'), axis=1, tiled=True)  70.4 us
    all_gather x1, waiting for transfers between devices, body(): lax.all_gather(relowered[3], ('wide', 'narrow'), axis=0, tiled=True)  68.5 us
    all_gather x1, waiting for transfers between devices, body(): lax.all_gather(lowered[4], ('wide', 'narrow'), axis=0, tiled=True)  60.1 us
    all_gather x1, waiting for transfers between devices, body(): lax.all_gather(relowered[5], ('wide', 'narrow'), axis=0, tiled=True)  51.3 us
    all_gather x1, waiting for transfers between devices, body(): lax.all_gather(relowered[2], ('wide', 'narrow'), axis=0, tiled=True)  50.5 us
    all_gather x1, waiting for transfers between devices, body(): lax.all_gather(lowered[5], ('wide', 'narrow'), axis=0, tiled=True)  49.1 us
  transfers between devices with their start and end apart: 23, of which 18 were waited for; matrix products, arithmetic and copies ran while one was open for 12% of the time, Pallas kernels for 0%

commit v1 on v0

v1 whole, which is shorter than its diff:
```python
import functools

import jax
import jax.numpy as jnp
from jax import lax
from jax.experimental import pallas as pl
from jax.experimental.pallas import tpu as pltpu
from jax.sharding import PartitionSpec as P

D = 1024
HD = 64
P_SIZE = 8
PP = 64
NVIEW = 4
TMAX = 12
STEP = 10
LANES = 128
MIB = 1024 * 1024

DEPTH_WEIGHT = 1.0
CLIP_NORM = 0.01
BETA_ONE = 0.9
BETA_TWO = 0.95
ADAM_EPS = 1e-08
DECAY = 0.05
RATES = (0.05, 0.05, 0.5, 0.05, 0.05, 0.05, 0.8)
MESH = pl.DeviceIdType.MESH
HIGHEST = lax.Precision.HIGHEST
F32 = jnp.float32
BF16 = jnp.bfloat16


def matmul(left, right):
    return jnp.dot(left, right, preferred_element_type=F32)


def outer_sum(left, right):
    return lax.dot_general(left, right, (((0,), (0,)), ((), ())), preferred_element_type=F32)


def back_mul(grad, weight):
    return lax.dot_general(grad, weight, (((1,), (1,)), ((), ())), preferred_element_type=F32)


def layer_norm(values, gain, shift):
    centred = values - jnp.mean(values, -1, keepdims=True)
    spread = jnp.mean(centred * centred, -1, keepdims=True)
    return centred * lax.rsqrt(spread + 1e-05) * gain + shift


def exact_gelu(values):
    return jax.nn.gelu(values, approximate=False)


def attention_forward(queries, keys, values):
    length, heads = (queries.shape[0], queries.shape[1])
    blocked = min(512, length)
    scale = HD ** (-0.5)

    def one_block(query_block):
        scores = (
            jnp.einsum("qhd,khd->hqk", query_block, keys, preferred_element_type=jnp.float32)
            * scale
        )
        highest = jnp.max(scores, -1, keepdims=True)
        exponentials = jnp.exp(scores - highest)
        summed = jnp.sum(exponentials, -1, keepdims=True)
        softmaxed = (exponentials / summed).astype(jnp.bfloat16)
        output = jnp.einsum("hqk,khd->qhd", softmaxed, values, preferred_element_type=jnp.float32)
        return (output.astype(jnp.bfloat16), (highest + jnp.log(summed))[:, :, 0])

    output, logsum = lax.map(one_block, queries.reshape(length // blocked, blocked, heads, HD))
    return (output.reshape(length, heads * HD), logsum)


def attention_backward(queries, keys, values, logsum, out_grad):
    length, heads = (queries.shape[0], queries.shape[1])
    blocked = min(512, length)
    scale = HD ** (-0.5)

    def one_block(carry, inputs):
        key_grad, value_grad = carry
        query_block, logsum_block, grad_block = inputs
        scores = (
            jnp.einsum("qhd,khd->hqk", query_block, keys, preferred_element_type=jnp.float32)
            * scale
        )
        softmaxed = jnp.exp(scores - logsum_block[:, :, None])
        value_grad = value_grad + jnp.einsum(
            "hqk,qhd->khd",
            softmaxed.astype(jnp.bfloat16),
            grad_block,
            preferred_element_type=jnp.float32,
        )
        prob_grad = jnp.einsum(
            "qhd,khd->hqk", grad_block, values, preferred_element_type=jnp.float32
        )
        score_grad = softmaxed * (prob_grad - jnp.sum(softmaxed * prob_grad, -1, keepdims=True))
        score_low = score_grad.astype(jnp.bfloat16)
        query_grad = (
            jnp.einsum("hqk,khd->qhd", score_low, keys, preferred_element_type=jnp.float32) * scale
        )
        key_grad = (
            key_grad
            + jnp.einsum("hqk,qhd->khd", score_low, query_block, preferred_element_type=jnp.float32)
            * scale
        )
        return ((key_grad, value_grad), query_grad)

    zeros = jnp.zeros((length, heads, HD), jnp.float32)
    shaped = (
        queries.reshape(length // blocked, blocked, heads, HD),
        logsum,
        out_grad.reshape(length // blocked, blocked, heads, HD),
    )
    (key_grad, value_grad), query_grad = lax.scan(one_block, (zeros, zeros), shaped)
    return (query_grad.reshape(length, heads, HD), key_grad, value_grad)


def adamw(weight, first, second, grad, rate):
    first = BETA_ONE * first + (1.0 - BETA_ONE) * grad
    second = BETA_TWO * second + (1.0 - BETA_TWO) * grad * grad
    first_hat = first / (1.0 - BETA_ONE**STEP)
    second_hat = second / (1.0 - BETA_TWO**STEP)
    weight = weight - rate * (first_hat / (jnp.sqrt(second_hat) + ADAM_EPS) + DECAY * weight)
    return (weight, first, second)


def chip_bits(chips):
    bits, step = [], 1
    while step < chips:
        bits.append(step)
        step *= 2
    return bits


def flip(chip, mask):
    for bit in chip_bits(mask + 1):
        if mask & bit:
            chip = chip + (1 - 2 * (chip // bit % 2)) * bit
    return chip


def column_halves(width):
    first = -(-width // (2 * LANES)) * LANES
    return ((0, first), (first, width - first))


def work_items(widths, order):
    return [(which,) + half + (side,) for which in order for side, half in enumerate(column_halves(widths[which]))]


class Place:
    def __init__(self, wide, narrow):
        self.wide, self.narrow = wide, narrow
        self.chips = wide // 2
        self.bits = chip_bits(self.chips)
        self.w = lax.axis_index("wide")
        self.n = lax.axis_index("narrow")
        self.chip = self.w // 2
        self.core = self.w % 2
        self.twin = (2 * self.chip + 1 - self.core, self.n)

    def across(self, mask):
        return (2 * flip(self.chip, mask) + self.core, self.n)

    def along(self, step):
        return (self.w, lax.rem(self.n + step, self.narrow))

    def neighbours(self):
        return (
            [self.twin]
            + [self.across(bit) for bit in self.bits]
            + [self.along(step) for step in range(1, self.narrow)]
        )


def greet(peers):
    barrier = pltpu.get_barrier_semaphore()
    for peer in peers:
        pl.semaphore_signal(barrier, inc=1, device_id=peer, device_id_type=MESH)
    pl.semaphore_wait(barrier, len(peers))


def gather_kernel(items, wide, narrow, count, *refs):
    ins, outs = refs[:count], refs[count : 2 * count]
    own_sem, send_sem, recv_sem = refs[2 * count :]
    place = Place(wide, narrow)
    chips = place.chips
    greet(place.neighbours())

    own = []
    for which in range(count):
        copy = pltpu.make_async_copy(
            ins[which], outs[which].at[place.chip, place.core, place.n], own_sem.at[which]
        )
        copy.start()
        own.append(copy)

    def remote(item, src, dst, slot, peer):
        return pltpu.make_async_remote_copy(
            src_ref=src,
            dst_ref=dst,
            send_sem=send_sem.at[item, slot],
            recv_sem=recv_sem.at[item, slot],
            device_id=peer,
            device_id_type=MESH,
        )

    def group(item, mask):
        which, start, width, _ = items[item]
        return outs[which].at[flip(place.chip, mask), place.core, :, :, pl.ds(start, width)]

    def along(item, step):
        which, start, width, _ = items[item]
        return remote(
            item,
            ins[which].at[:, pl.ds(start, width)],
            outs[which].at[place.chip, place.core, place.n, :, pl.ds(start, width)],
            2 * chips + step - 1,
            place.along(step),
        )

    def bits_of(item):
        return place.bits if items[item][3] == 0 else place.bits[::-1]

    def across(item, mask, bit):
        return remote(item, group(item, mask), group(item, mask), mask ^ bit, place.across(bit))

    def to_twin(item, mask):
        return remote(item, group(item, mask), group(item, mask), chips + mask, place.twin)

    started = []

    def start(copy):
        copy.start()
        started.append(copy)

    def start_along(item):
        for step in range(1, narrow):
            start(along(item, step))

    def stage(item, number):
        bits = bits_of(item)
        if number == 0:
            if item % 2 == 0:
                own[items[item][0]].wait()
            for step in range(1, narrow):
                along(item, step).wait_recv()
            held = [0]
            fresh = [0]
        else:
            held = [0]
            for bit in bits[: number - 1]:
                held = held + [mask ^ bit for mask in held]
            fresh = [mask ^ bits[number - 1] for mask in held]
            for mask in fresh:
                across(item, mask ^ bits[number - 1], bits[number - 1]).wait_recv()
            held = held + fresh
        if number < len(bits):
            for mask in held:
                start(across(item, mask, bits[number]))
        for mask in fresh:
            start(to_twin(item, mask))

    total = len(items)
    ahead = 4
    for item in range(min(ahead, total)):
        start_along(item)
    depth = len(place.bits) + 1
    for tick in range(0, total + 2 * (depth - 1), 2):
        for number in reversed(range(depth)):
            for item in (tick - 2 * number, tick - 2 * number + 1):
                if 0 <= item < total:
                    stage(item, number)
        for item in (tick + ahead, tick + ahead + 1):
            if item < total:
                start_along(item)
    for item in range(total):
        for mask in range(chips):
            to_twin(item, mask).wait_recv()
    for copy in started:
        copy.wait_send()


def gather_all(shards, wide, narrow):
    count = len(shards)
    widths = [shard.shape[1] for shard in shards]
    items = work_items(widths, range(count))
    slots = wide + narrow - 1
    shapes = [
        jax.ShapeDtypeStruct((wide // 2, 2, narrow) + shard.shape, shard.dtype) for shard in shards
    ]
    whole = pl.pallas_call(
        functools.partial(gather_kernel, items, wide, narrow, count),
        out_shape=shapes,
        in_specs=[pl.BlockSpec(memory_space=pl.ANY)] * count,
        out_specs=[pl.BlockSpec(memory_space=pl.ANY)] * count,
        scratch_shapes=[
            pltpu.SemaphoreType.DMA((count,)),
            pltpu.SemaphoreType.DMA((len(items), slots)),
            pltpu.SemaphoreType.DMA((len(items), slots)),
        ],
        compiler_params=pltpu.CompilerParams(collective_id=0, has_side_effects=True),
        name="gather_weights",
    )(*shards)
    return [full.reshape(-1, width) for full, width in zip(whole, widths)]


def tile_of(width):
    for tile in (512, 384, 256, 128):
        if width % tile == 0:
            return tile
    return width


def reduce_kernel(items, wide, narrow, count, *refs):
    lefts, rights = refs[:count], refs[count : 2 * count]
    extra, term = refs[2 * count : 2 * count + 2]
    outs = refs[2 * count + 2 : 3 * count + 2]
    sums = refs[3 * count + 2]
    scratch = list(refs[3 * count + 3 :])
    place = Place(wide, narrow)
    chips = place.chips
    total = len(items)
    sent = [scratch.pop(0) for _ in items]
    held = [scratch.pop(0) for _ in items]
    passed = [[scratch.pop(0) for _ in place.bits] for _ in items]
    last = [scratch.pop(0) for _ in items]
    wide_tiles, narrow_tiles, send_sem, recv_sem, tile_send, tile_recv = scratch
    peers = [place.twin]
    for step in range(1, wide):
        peers.append((lax.rem(place.w + step, wide), place.n))
    for step in range(1, narrow):
        peers.append(place.along(step))
    greet(peers[1:])

    started = []

    def start(copy):
        copy.start()
        started.append(copy)

    def remote(item, src, dst, slot, peer):
        return pltpu.make_async_remote_copy(
            src_ref=src,
            dst_ref=dst,
            send_sem=send_sem.at[item, slot],
            recv_sem=recv_sem.at[item, slot],
            device_id=peer,
            device_id_type=MESH,
        )

    def bits_of(item):
        return place.bits[::-1] if items[item][3] == 0 else place.bits

    def product(item, mask, core, into, plus):
        which, begin, width, _ = items[item]
        left, right = lefts[which], rights[which]
        rows = into.shape[2]
        tile = tile_of(width)
        together = max(1, min(narrow, 128 // rows))
        owner = flip(place.chip, mask)
        with_extra = which == 0 and begin + width == right.shape[1]

        def one(step, carry):
            across, down = step % (width // tile), step // (width // tile)
            offset = pl.multiple_of(begin + across * tile, LANES)
            local = pl.multiple_of(across * tile, LANES)
            ns = pl.ds(down * together, together)
            lhs = left[owner, core, ns].reshape(together * rows, left.shape[-1])
            value = jnp.dot(lhs, right[:, pl.ds(offset, tile)], preferred_element_type=F32)
            if with_extra:
                more = extra[owner, core, ns].reshape(together * rows, LANES)
                more = jnp.concatenate([jnp.zeros((together * rows, tile - LANES), F32), more], 1)
                value = value + more
            value = value.reshape(together, rows, tile)
            if plus is not None:
                value = value + plus[mask, ns, :, pl.ds(local, tile)].astype(F32)
            into[mask, ns, :, pl.ds(local, tile)] = value.astype(BF16)
            return carry

        assert not with_extra or tile == width
        lax.fori_loop(0, (width // tile) * (narrow // together), one, 0)

    def to_twin(item, mask):
        return remote(item, sent[item].at[mask], held[item].at[mask], mask, place.twin)

    def across(item, mask, bit, number, slot):
        return remote(
            item, held[item].at[mask], passed[item][number].at[slot], chips + mask, place.across(bit)
        )

    def along(item, step):
        target = place.along(step)
        return remote(
            item,
            held[item].at[0, target[1]],
            last[item].at[narrow - step - 1],
            2 * chips + narrow - step - 1,
            target,
        )

    def split(item, number):
        bits = bits_of(item)
        keep = list(range(chips))
        for bit in bits[:number]:
            keep = [mask for mask in keep if not mask & bit]
        if number < len(bits):
            return [m for m in keep if m & bits[number]], [m for m in keep if not m & bits[number]]
        return [], keep

    def add_into(dest, dest_at, src, src_at):
        rows, width = dest.shape[-2:]

        def one(step, carry):
            a = dest[dest_at, step].astype(F32) + src[src_at, step].astype(F32)
            dest[dest_at, step] = a.astype(BF16)
            return carry

        lax.fori_loop(0, narrow, one, 0)

    def send_on(item, number, ready):
        bits = bits_of(item)
        away, keep = split(item, number)
        if number < len(bits):
            for mask in away:
                ready(mask)
                start(across(item, mask, bits[number], number, keep.index(mask ^ bits[number])))
            for mask in keep:
                ready(mask)
        else:
            ready(0)
            for step in range(1, narrow):
                start(along(item, step))

    def stage(item, number):
        bits = bits_of(item)
        if number == 0:

            def ready(mask):
                to_twin(item, mask).wait_recv()
                product(item, mask, place.core, held[item], held[item])

            send_on(item, 0, ready)
        else:
            bit = bits[number - 1]
            _, kept = split(item, number - 1)

            def ready(mask):
                slot = kept.index(mask)
                across(item, mask ^ bit, bit, number - 1, slot).wait_recv()
                add_into(held[item], mask, passed[item][number - 1], slot)

            send_on(item, number, ready)

    def finish(item):
        which, begin, width, _ = items[item]
        value = held[item][0, place.n].astype(F32)
        for step in range(1, narrow):
            along(item, step).wait_recv()
        for slot in range(narrow - 1):
            value = value + last[item][slot].astype(F32)
        outs[which][:, pl.ds(begin, width)] = value
        return jnp.sum(value * value)

    for item in range(total):
        for mask in range(chips):
            product(item, mask, 1 - place.core, sent[item], None)
            start(to_twin(item, mask))
    squares = jnp.zeros((), F32)
    depth = len(place.bits) + 1
    for tick in range(0, total + 2 * depth, 2):
        for number in reversed(range(depth + 1)):
            for item in (tick - 2 * number, tick - 2 * number + 1):
                if 0 <= item < total:
                    if number < depth:
                        stage(item, number)
                    else:
                        squares = squares + finish(item)

    rows = lax.broadcasted_iota(jnp.int32, (8, LANES), 0)
    wide_tiles[place.w] = jnp.where(rows == 0, term[...], squares)

    def tile_copy(buffer, at, slot, peer):
        return pltpu.make_async_remote_copy(
            src_ref=buffer.at[at],
            dst_ref=buffer.at[at],
            send_sem=tile_send.at[slot],
            recv_sem=tile_recv.at[slot],
            device_id=peer,
            device_id_type=MESH,
        )

    for step in range(1, wide):
        start(tile_copy(wide_tiles, place.w, step - 1, (lax.rem(place.w + step, wide), place.n)))
    for step in range(1, wide):
        tile_copy(wide_tiles, place.w, step - 1, (lax.rem(place.w + step, wide), place.n)).wait_recv()
    whole = wide_tiles[0]
    for index in range(1, wide):
        whole = whole + wide_tiles[index]
    narrow_tiles[place.n] = whole
    for step in range(1, narrow):
        start(tile_copy(narrow_tiles, place.n, wide + step - 1, place.along(step)))
    for step in range(1, narrow):
        tile_copy(narrow_tiles, place.n, wide + step - 1, place.along(step)).wait_recv()
    whole = narrow_tiles[0]
    for index in range(1, narrow):
        whole = whole + narrow_tiles[index]
    sums[...] = whole
    for copy in started:
        copy.wait_send()


def reduce_all(lefts, rights, extra, term, wide, narrow, order):
    count = len(lefts)
    chips = wide // 2
    shaped = [left.reshape(chips, 2, narrow, -1, left.shape[1]) for left in lefts]
    extra = extra.reshape(chips, 2, narrow, -1, LANES)
    widths = [right.shape[1] for right in rights]
    rows = [left.shape[3] for left in shaped]
    items = work_items(widths, order)
    slots = 2 * chips + narrow - 1
    scratch = []
    for which, _, width, _ in items:
        scratch.append(pltpu.VMEM((chips, narrow, rows[which], width), BF16))
    for which, _, width, _ in items:
        scratch.append(pltpu.VMEM((chips, narrow, rows[which], width), BF16))
    for which, _, width, _ in items:
        size = chips
        while size > 1:
            size //= 2
            scratch.append(pltpu.VMEM((size, narrow, rows[which], width), BF16))
    for which, _, width, _ in items:
        scratch.append(pltpu.VMEM((narrow - 1, rows[which], width), BF16))
    scratch += [
        pltpu.VMEM((wide, 8, LANES), F32),
        pltpu.VMEM((narrow, 8, LANES), F32),
        pltpu.SemaphoreType.DMA((len(items), slots)),
        pltpu.SemaphoreType.DMA((len(items), slots)),
        pltpu.SemaphoreType.DMA((wide + narrow,)),
        pltpu.SemaphoreType.DMA((wide + narrow,)),
    ]
    vmem = pl.BlockSpec(memory_space=pltpu.VMEM)
    return pl.pallas_call(
        functools.partial(reduce_kernel, items, wide, narrow, count),
        out_shape=[jax.ShapeDtypeStruct((rows[i], widths[i]), F32) for i in range(count)]
        + [jax.ShapeDtypeStruct((8, LANES), F32)],
        in_specs=[vmem] * (2 * count + 2),
        out_specs=[vmem] * (count + 1),
        scratch_shapes=scratch,
        compiler_params=pltpu.CompilerParams(
            collective_id=1, has_side_effects=True, vmem_limit_bytes=60 * MIB
        ),
        name="reduce_grads",
    )(*shaped, *rights, extra, term)


def render_kernel(
    gauss_ref, weight_ref, target_ref, mask_ref, pair_ref, view_ref, total_ref, grad_ref, term_ref, feat, dfeat
):
    quads = gauss_ref.shape[0] // NVIEW
    span = weight_ref.shape[1]
    pairs = pair_ref.shape[1]
    scale = 1.0 / total_ref[0].astype(F32)

    def channel(index):
        return gauss_ref[:, index * PP : (index + 1) * PP]

    def shared():
        opacity = jax.nn.sigmoid(channel(3))
        extent = jax.nn.sigmoid(channel(5) + channel(6) + channel(7))
        lead = channel(8)
        denom = 1.0 + lead * lead + channel(9) * channel(9) + channel(10) * channel(10) + channel(11) * channel(11)
        facing = lead * lead / denom
        raw = channel(4)
        depth = jnp.maximum(raw, 0.0) + jnp.log1p(jnp.exp(-jnp.abs(raw)))
        return opacity, extent, lead, denom, facing, raw, depth

    opacity, extent, lead, denom, facing, raw, depth = shared()
    footprint = opacity * extent * facing
    channels = [jax.nn.sigmoid(channel(index)) * footprint for index in range(3)]
    channels += [footprint, depth * footprint]
    for index, value in enumerate(channels):
        for view in range(NVIEW):
            feat[index * quads : (index + 1) * quads, view * PP : (view + 1) * PP] = value[
                view * quads : (view + 1) * quads
            ]
    rendered = jnp.dot(feat[...], weight_ref[...], precision=HIGHEST, preferred_element_type=F32)
    parts = [rendered[index * quads : (index + 1) * quads] for index in range(5)]
    lane = lax.broadcasted_iota(jnp.int32, (quads, span), 1)
    live = jnp.where(lane < view_ref[0] * PP, mask_ref[...], 0).astype(F32)
    term = jnp.zeros((quads, span), F32)
    slopes = []
    for index in range(3):
        error = parts[index] - target_ref[index * quads : (index + 1) * quads, :].astype(F32)
        term = term + live * error * error
        slopes.append(2.0 * scale * live * error)
    below = 1.0 + parts[3]
    depth_out = parts[4] / below

    first, second = pair_ref[0:1, :], pair_ref[1:2, :]
    least = jnp.minimum(first, second)
    down = (jnp.abs(first - second) == P_SIZE).astype(jnp.int32)
    place = quads * PP
    slot, local = least // place, least % place
    high = down * quads + local // PP
    low = slot * PP + local % PP
    high_hot = (lax.broadcasted_iota(jnp.int32, (2 * quads, pairs), 0) == high).astype(F32).astype(BF16)
    low_hot = (lax.broadcasted_iota(jnp.int32, (span, pairs), 0) == low).astype(F32).astype(BF16)
    counts = back_mul(high_hot, low_hot)
    slope = jnp.zeros((quads, span), F32)
    for which, shift in enumerate((1, P_SIZE)):
        count = counts[which * quads : (which + 1) * quads]
        weight = DEPTH_WEIGHT * count * live * pltpu.roll(live, span - shift, 1)
        gap = depth_out - pltpu.roll(depth_out, span - shift, 1)
        term = term + weight * gap * gap
        pull = 2.0 * scale * weight * gap
        slope = slope + pull - pltpu.roll(pull, shift, 1)
    term_ref[...] = jnp.full(term_ref.shape, jnp.sum(term), F32)
    over = slope / below
    slopes += [-over * depth_out, over]
    stacked = jnp.concatenate(slopes, 0)
    dfeat[...] = lax.dot_general(
        stacked, weight_ref[...], (((1,), (1,)), ((), ())), precision=HIGHEST, preferred_element_type=F32
    )

    def feature_grad(index):
        return jnp.concatenate(
            [
                dfeat[index * quads : (index + 1) * quads, view * PP : (view + 1) * PP]
                for view in range(NVIEW)
            ],
            0,
        )

    def put(index, value):
        grad_ref[:, index * PP : (index + 1) * PP] = value.astype(BF16)

    d_foot = feature_grad(3)
    for index in range(3):
        tint = jax.nn.sigmoid(channel(index))
        upper = feature_grad(index)
        d_foot = d_foot + upper * tint
        put(index, upper * footprint * tint * (1.0 - tint))
    d_last = feature_grad(4)
    d_foot = d_foot + d_last * depth
    put(3, d_foot * extent * facing * opacity * (1.0 - opacity))
    put(4, d_last * footprint * jax.nn.sigmoid(raw))
    d_extent = d_foot * opacity * facing * extent * (1.0 - extent)
    for index in (5, 6, 7):
        put(index, d_extent)
    d_facing = d_foot * opacity * extent
    put(8, d_facing * 2.0 * lead / denom * (1.0 - facing))
    for index in (9, 10, 11):
        put(index, -2.0 * d_facing * facing / denom * channel(index))


def render(gaussians, weights, targets, mask, pairs, view_count, pair_total):
    rows = gaussians.shape[0]
    quads = rows // NVIEW
    slots, views = weights.shape[:2]
    spread = weights.transpose(1, 2, 0, 3).reshape(views * PP, slots * PP)
    wanted = targets.reshape(slots, 3, quads, PP).transpose(1, 2, 0, 3).reshape(3 * quads, slots * PP)
    valid = mask.reshape(slots, quads, PP).transpose(1, 0, 2).reshape(quads, slots * PP)
    vmem = pl.BlockSpec(memory_space=pltpu.VMEM)
    smem = pl.BlockSpec(memory_space=pltpu.SMEM)
    return pl.pallas_call(
        render_kernel,
        out_shape=[
            jax.ShapeDtypeStruct(gaussians.shape, BF16),
            jax.ShapeDtypeStruct((8, LANES), F32),
        ],
        in_specs=[vmem] * 5 + [smem] * 2,
        out_specs=[vmem] * 2,
        scratch_shapes=[pltpu.VMEM((5 * quads, views * PP), F32)] * 2,
        compiler_params=pltpu.CompilerParams(vmem_limit_bytes=48 * MIB),
        name="render",
    )(gaussians, spread, wanted, valid, pairs, view_count, pair_total)


def body(
    views,
    render_w,
    targets,
    pix_mask,
    pairs,
    view_count,
    pair_total,
    embed_weight,
    embed_first,
    embed_second,
    mixer_weight,
    mixer_first,
    mixer_second,
    merge_weight,
    merge_first,
    merge_second,
    expand_weight,
    expand_first,
    expand_second,
    shrink_weight,
    shrink_first,
    shrink_second,
    unpatch_weight,
    unpatch_first,
    unpatch_second,
    norm_params,
    norm_first,
    norm_second,
):
    masters = (embed_weight, mixer_weight, merge_weight, expand_weight, shrink_weight, unpatch_weight, norm_params)
    firsts = (embed_first, mixer_first, merge_first, expand_first, shrink_first, unpatch_first, norm_first)
    seconds = (embed_second, mixer_second, merge_second, expand_second, shrink_second, unpatch_second, norm_second)
    groups = lax.axis_size("narrow")
    wide_count = lax.axis_size("wide")
    features = embed_weight.shape[0]
    kinds = norm_params.shape[0]
    padded = -(-(features + kinds) // LANES) * LANES
    fill = padded - features - kinds
    by_kernel = mixer_weight.shape[0] % 16 == 0

    first_shard = jnp.concatenate([embed_weight.T, norm_params.T], 1)
    first_shard = jnp.pad(first_shard.astype(BF16), ((0, 0), (0, fill)))
    shards = [first_shard] + [weight.astype(BF16) for weight in masters[1:6]]
    if by_kernel:
        weights = gather_all(shards, wide_count, groups)
    else:
        weights = [lax.all_gather(shard, ("wide", "narrow"), axis=0, tiled=True) for shard in shards]
    gains = weights[0][:, features : features + kinds].T.astype(F32)

    patches = views.reshape(-1, features)
    rows = patches.shape[0]
    patches = jnp.pad(patches, ((0, 0), (0, padded - features)))
    embedded = back_mul(patches[:, :features], weights[0][:, :features])
    normed_one, norm_back_one = jax.vjp(layer_norm, embedded, gains[0], gains[3])
    normed_one = normed_one.astype(BF16)
    mixed = matmul(normed_one, weights[1]).astype(BF16).reshape(rows, 3, groups, -1)
    spread = lax.all_to_all(mixed, "narrow", split_axis=2, concat_axis=0, tiled=True)
    length, width = (spread.shape[0], spread.shape[-1])
    local_heads = width // HD
    queries = spread[:, 0, 0].reshape(length, local_heads, HD)
    keys_all = spread[:, 1, 0].reshape(length, local_heads, HD)
    values_all = spread[:, 2, 0].reshape(length, local_heads, HD)
    attended, logsum = attention_forward(queries, keys_all, values_all)
    returned = lax.all_to_all(
        attended.reshape(length, 1, width), "narrow", split_axis=0, concat_axis=1, tiled=True
    ).reshape(rows, D)
    residual_one = embedded + matmul(returned, weights[2])
    normed_two, norm_back_two = jax.vjp(layer_norm, residual_one, gains[1], gains[4])
    normed_two = normed_two.astype(BF16)
    expanded = matmul(normed_two, weights[3])
    activated, gelu_back = jax.vjp(exact_gelu, expanded)
    activated = activated.astype(BF16)
    residual_two = residual_one + matmul(activated, weights[4])
    normed_three, norm_back_three = jax.vjp(layer_norm, residual_two, gains[2], gains[5])
    normed_three = normed_three.astype(BF16)
    gaussians = matmul(normed_three, weights[5])
    divisor = pair_total[0].astype(F32)

    gauss_low, term = render(
        gaussians, render_w[0], targets[0], pix_mask[0], pairs[0], view_count, pair_total
    )
    residual_grad, gain_three, shift_three = norm_back_three(back_mul(gauss_low, weights[5]))
    shrink_low = residual_grad.astype(BF16)
    (expand_grad,) = gelu_back(back_mul(shrink_low, weights[4]))
    expand_low = expand_grad.astype(BF16)
    through_two, gain_two, shift_two = norm_back_two(back_mul(expand_low, weights[3]))
    residual_grad = residual_grad + through_two
    merge_low = residual_grad.astype(BF16)
    out_grad = back_mul(merge_low, weights[2]).astype(BF16).reshape(rows, groups, width)
    head_grad = lax.all_to_all(out_grad, "narrow", split_axis=1, concat_axis=0, tiled=True).reshape(
        length, local_heads, HD
    )
    query_grad, key_grad, value_grad = attention_backward(queries, keys_all, values_all, logsum, head_grad)
    stacked = jnp.stack([query_grad, key_grad, value_grad], 1).astype(BF16).reshape(length, 3, 1, width)
    mixed_grad = lax.all_to_all(stacked, "narrow", split_axis=0, concat_axis=2, tiled=True).reshape(
        rows, 3 * D
    )
    through_one, gain_one, shift_one = norm_back_one(back_mul(mixed_grad, weights[1]))
    embed_grad = (residual_grad + through_one).astype(BF16)
    grad_norms = jnp.stack([gain_one, gain_two, gain_three, shift_one, shift_two, shift_three])

    lefts = [embed_grad.T, normed_one.T, returned.T, normed_two.T, activated.T, normed_three.T]
    rights = [patches, mixed_grad, merge_low, expand_low, shrink_low, gauss_low]
    at = features % LANES
    extra = jnp.pad(grad_norms.T, ((0, 0), (at, LANES - at - kinds)))
    if by_kernel:
        *sums, totals = reduce_all(
            lefts, rights, extra, term, wide_count, groups, (5, 4, 3, 2, 1, 0)
        )
        loss_sum, square_sum = totals[0, 0], totals[1, 0]
    else:
        products = [matmul(left, right) for left, right in zip(lefts, rights)]
        products[0] = products[0].at[:, -LANES:].add(extra)
        sums = [
            lax.psum_scatter(
                product.astype(BF16), ("wide", "narrow"), scatter_dimension=0, tiled=True
            ).astype(F32)
            for product in products
        ]
        squares = sum(jnp.sum(part * part) for part in sums)
        loss_sum, square_sum = lax.psum((term[0, 0], squares), ("wide", "narrow"))
    first_sum = sums[0].T
    grads = [first_sum[:features]] + list(sums[1:]) + [first_sum[features : features + kinds]]
    loss = loss_sum / divisor
    grad_norm = jnp.sqrt(square_sum)
    factor = jnp.minimum(1.0, CLIP_NORM / (grad_norm + 1e-06))
    results = []
    for which in range(7):
        results += adamw(masters[which], firsts[which], seconds[which], grads[which] * factor, RATES[which])
    return tuple(results) + (loss, grad_norm)


def solution(mesh):
    columns = P(None, ("wide", "narrow"))
    rows = P(("wide", "narrow"), None)
    weights = (columns,) * 3 + (rows,) * 15 + (columns,) * 3
    return jax.shard_map(
        body,
        mesh=mesh,
        in_specs=(
            P("wide", None, "narrow", None),
            P("wide", None, None, None, None),
            P("wide", None, None, "narrow"),
            P("wide", None, "narrow"),
            P("wide", None, "narrow"),
            P("wide"),
            P(),
        )
        + weights,
        out_specs=weights + (P(), P()),
        check_vma=False,
    )
```

time: 2220 us -> 680 us (0.31)
  waiting for transfers between devices: 1620 us -> 75 us
  Pallas kernels: 0 us -> 323 us
  blocking collectives: 134 us -> 0 us
  local copies, waits for them, and re-layouts: 185 us -> 94.9 us
  other arithmetic: 102 us -> 59.4 us
  matrix products: 123 us -> 87.3 us
    unnamed x20 -> x0, waiting for transfers between devices: 931 us -> none
    all_gather x11 -> x0, waiting for transfers between devices: 402 us -> none  [the longest x1 75.6 us: body(): lax.all_gather(relowered[4], ('wide', 'narrow'), axis=0, tiled=True)]
    pallas_call x0 -> x3, Pallas kernels: none -> 323 us  [the longest x1 174 us: reduce_all(): pl.pallas_call(functools.partial(reduce_kernel, items, wide, narrow, coun...]
    reduce_scatter x7 -> x0, waiting for transfers between devices: 205 us -> none  [the longest x1 42.1 us: body(): lax.psum_scatter(partial_sums[4].astype(jnp.bfloat16), 'wide', scatter_di...]
    all_gather x1 -> x0, blocking collectives: 70.4 us -> none  [body(): lax.all_gather(lowered[6], ('wide', 'narrow'), axis=1, tiled=True)]
    gather x4 -> x0, local copies, waits for them, and re-layouts: 64.9 us -> none  [the longest x2 41.4 us: render_terms(): pair_live = flat_live[pair_index[0]] * flat_live[pair_index[1]]]
    psum x1 -> x0, blocking collectives: 39.4 us -> none  [body(): loss_sum, square_sum = lax.psum((term, squares), ('wide', 'narrow'))]
    dot_general x14 -> x5, matrix products: 65 us -> 27.3 us  [matmul(): return jnp.dot(left, right, preferred_element_type=F32)]
  transfers between devices with their start and end apart: 23 -> 4, of which waited for: 18 -> 3; matrix products, arithmetic and copies ran while one was open for 12% -> 6% of each run, Pallas kernels for 0% -> 0%
where the time goes in v1:
time: 680 us; the launch traced here: 672 us
  Pallas kernels  323 us (48%)
  local copies, waits for them, and re-layouts  94.9 us (14%)
  matrix products  87.3 us (13%)
  waiting for transfers between devices  75 us (11%)
  other arithmetic  59.4 us (9%)
  starting transfers between devices  24.8 us (4%)
  between operations  6.93 us (1%)
    pallas_call x1, Pallas kernels, reduce_all(): pl.pallas_call(functools.partial(reduce_kernel, items, wide, narrow, coun...  174 us
    pallas_call x1, Pallas kernels, gather_all(): pl.pallas_call(functools.partial(gather_kernel, items, wide, narrow, coun...  144 us
    all_to_all x1, waiting for transfers between devices, body(): lax.all_to_all(mixed, 'narrow', split_axis=2, concat_axis=0, tiled=True)  37.8 us
    all_to_all x1, waiting for transfers between devices, body(): lax.all_to_all(stacked, 'narrow', split_axis=0, concat_axis=2, tiled=True)  35.1 us
    dot_general x5, matrix products, matmul(): return jnp.dot(left, right, preferred_element_type=F32)  27.3 us
    dot_general x6, matrix products, back_mul(): lax.dot_general(grad, weight, (((1,), (1,)), ((), ())), preferred_element...  26 us
    unnamed x163, local copies, waits for them, and re-layouts  17.1 us
  transfers between devices with their start and end apart: 4, of which 3 were waited for; matrix products, arithmetic and copies ran while one was open for 6% of the time, Pallas kernels for 0%

profile of v1, /device:TPU:0, one launch (start us, length us, event | category | flops | bytes accessed | tf_op | source)
XLA Modules:
  0.0 671.8 jit_solution(7705805498856905565)
XLA Ops:
  11.4 143.9 %gather_weights.1 = (bf16[4,2,4,32,640]{4,3,2,1,0:T(8,128)(2,1)}, bf16[4,2,4,32,3072]{4,3,2,1,0:T(8,128)(2,1)}, bf16[4,2,4,32,1024]{4,3,2,1,0:T(8,128)(2,1)}, bf...) custom-call(bf16[32,640]{1,0:T(8,128)(2,1)} %fusion.97.refs_0_, ...), custom_call_target="tpu_custom_call" | custom-call | tf_op jit(solution)/shard_map/gather_weights/pallas_call | solution.py:294
  160.4 5.9 convolution_convert_fusion
  166.3 4.3 reshape.294
  173.4 10.6 %all-to-all-start = ((bf16[256,3,4,256]{3,0,1,2:T(8,128)(2,1)}), bf16[256,3,4,256]{3,0,1,2:T(8,128)(2,1)}, u32[]{:S(2)}, u32[]{:S(2)}) async-start(bf16[256,3,4,256]{3,0,1,2:T(8,128)(2,1)} %copy.228), calls=%async_computation | async-start | bytes 3145728 | tf_op jit(solution)/shard_map/all_to_all | solution.py:739
  184.1 37.8 %all-to-all-done = bf16[256,3,4,256]{3,0,1,2:T(8,128)(2,1)} async-done(((bf16[256,3,4,256]{3,0,1,2:T(8,128)(2,1)}), bf16[256,3,4,256]{3,0,1,2:T(8,128)(2,1)}, u32[]{:S(2)}, u32[]{:S(2)}) %all-to-all-start) | async-done | bytes 1572896 | tf_op jit(solution)/shard_map/all_to_all | solution.py:739
  228.0 12.4 %while.27 = (s32[]{:T(128)}, bf16[2,512,4,64]{1,3,2,0:T(8,128)(2,1)}, f32[2,4,512]{2,1,0:T(4,128)S(1)}, bf16[2,512,4,64]{1,3,2,0:T(8,128)(2,1)S(1)}, bf16[1024,4...) while((s32[]{:T(128)}, bf16[2,512,4,64]{1,3,2,0:T(8,128)(2,1)}, ...), condition=%wide.region_5.6_spmd, body=%wide.region_2.5_spmd.sunk | while | flops 555874304 | bytes 30998672 | solution.py:72
  242.8 4.8 reshape.318
  248.1 4.8 reduce.2
  253.8 4.5 all-to-all-start.1
  259.0 3.7 copy.267
  276.4 3.5 reshape.323
  284.1 3.6 fusion.114
  288.0 13.6 %fusion.40 = (f32[256,4096]{1,0:T(8,128)S(1)}, f32[256,4096]{1,0:T(8,128)S(1)}) fusion(bf16[1024,4096]{1,0:T(8,128)(2,1)} %bitcast.336, f32[256,1024]{1,0:T(8,128)S(1)} %get-tuple-element.451, f32[1024]{0:T(1024)S(1)} %bitcast.328, f32[1024]{0:T(1024)S(1)} %bitcast.313, f32[256]{0:T(256)S(1)} %fusion.100, f32[256]{0:T(256)S(1)} %broadcast_multiply_fusion.1), kind=kOutput, calls=%fused_computation.47 | convolution fusion | flops 2213806080 | bytes 17836032 | tf_op jit(solution)/shard_map/dot_general | solution.py:34
  301.6 3.6 fusion.113
  306.2 4.9 render.1
  315.2 7.2 %add_convert_fusion.refs_9_ = bf16[256,4096]{1,0:T(8,128)(2,1)S(1)} fusion(f32[256,4096]{1,0:T(8,128)S(1)} %get-tuple-element.473, f32[256,4096]{1,0:T(8,128)S(1)} %get-tuple-element.474, bf16[256,1024]{1,0:T(8,128)(2,1)S(1)} %add_convert_fusion.8.refs_10_, bf16[4096,1024]{1,0:T(8,128)(2,1)} %bitcast.279), kind=kOutput, calls=%fused_computation.68 | convolution fusion | flops 2162163712 | bytes 19398656 | tf_op jit(solution)/shard_map/dot_general | solution.py:42
  322.4 7.8 %multiply_reduce_fusion.3 = (f32[1024]{0:T(1024)}, f32[256]{0:T(256)S(1)}, f32[1024]{0:T(1024)}, f32[256,1024]{1,0:T(8,128)S(1)}) fusion(f32[256,1024]{1,0:T(8,128)S(1)} %get-tuple-element.451, f32[256]{0:T(256)S(1)} %fusion.100, f32[256]{0:T(256)S(1)} %broadcast_multiply_fusion.1, f32[1024]{0:T(1024)S(1)} %bitcast.314, ...), kind=kOutput, calls=%fused_computation.110 | convolution fusion | flops 2149578496 | bytes 12598272 | tf_op jit(solution)/shard_map/dot_general | solution.py:42
  333.9 5.1 all-to-all-start.2
  340.7 4.0 add_convert_fusion.1
  359.7 36.2 %while.28 = (s32[]{:T(128)}, f32[1024,4,64]{0,2,1:T(8,128)S(1)}, f32[1024,4,64]{0,2,1:T(8,128)S(1)}, bf16[2,512,4,64]{1,3,2,0:T(8,128)(2,1)}, bf16[2,512,4,64]{1...) while((s32[]{:T(128)}, f32[1024,4,64]{0,2,1:T(8,128)S(1)}, ...), condition=%wide.region_16.17_spmd.clone, body=%wide.region_14.16_spmd.clone.sunk | while | flops 1368782848 | bytes 147906928 | solution.py:116
  364.3 3.4 multiply_convert_fusion.4
  367.7 3.3 fusion.174
  371.0 4.1 fusion.176
  382.4 3.4 multiply_convert_fusion.4
  385.8 3.3 fusion.174
  389.1 4.1 fusion.176
  402.6 4.6 all-to-all-start.3
  407.2 10.2 %fusion.43 = bf16[4096,256]{0,1:T(8,128)(2,1)S(1)} fusion(f32[256,4096]{1,0:T(8,128)} %copy-done.11), kind=kLoop, calls=%fused_computation.50 | loop fusion | flops 68157440 | bytes 6291456 | tf_op jit(solution)/shard_map/convert_element_type | solution.py:754
  419.9 35.1 %all-to-all-done.3 = bf16[1024,3,1,256]{3,1,2,0:T(4,128)(2,1)} async-done(((bf16[1024,3,1,256]{3,1,2,0:T(4,128)(2,1)}), bf16[1024,3,1,256]{3,1,2,0:T(4,128)(2,1)}, u32[]{:S(2)}, u32[]{:S(2)}) %all-to-all-start.3) | async-done | bytes 1572896 | tf_op jit(solution)/shard_map/all_to_all | solution.py:777
  459.1 4.1 reshape.304.refs_7_
  463.4 5.4 fusion.103
  478.8 174.3 %reduce_grads.1 = (f32[32,640]{1,0:T(8,128)}, f32[32,3072]{1,0:T(8,128)}, f32[32,1024]{1,0:T(8,128)}, f32[32,4096]{1,0:T(8,128)}, f32[128,1024]{1,0:T(8,128)}, /*index=5*/f32[32,768]{1,0:T(8,128)}, f32[8,128]{1,0:T(8,128)}) custom-call(bf16[4,2,4,32,256]{4,3,2,1,0:T(8,128)(2,1)} %bitcast.294, bf16[4,2,4,32,256]{4,3,2,1,0:T(8,128)(2,1)} %bitcast.291, ...), custom_call_target="tpu_custom_call" | custom-call | tf_op jit(solution)/shard_map/reduce_grads/pallas_call | solution.py:545
  (305 shorter events, 136.0 us)
Async XLA Ops:
  0.7 155.8 %copy-start.24 = (bf16[1,4,64,576]{3,2,1,0:T(8,128)(2,1)S(1)}, bf16[1,4,64,576]{3,2,1,0:T(8,128)(2,1)}, u32[]{:S(2)}) copy-start(bf16[1,4,64,576]{3,2,1,0:T(8,128)(2,1)} %param.32) | copy-start | bytes 884740
  158.7 125.3 %copy-start.5 = (f32[1024,256]{0,1:T(8,128)}, f32[1024,256]{0,1:T(8,128)S(1)}, u32[]{:S(2)}) copy-start(f32[1024,256]{0,1:T(8,128)S(1)} %copy.226) | copy-start | bytes 3145732
  173.4 48.4 %all-to-all-start = ((bf16[256,3,4,256]{3,0,1,2:T(8,128)(2,1)}), bf16[256,3,4,256]{3,0,1,2:T(8,128)(2,1)}, u32[]{:S(2)}, u32[]{:S(2)}) async-start(bf16[256,3,4,256]{3,0,1,2:T(8,128)(2,1)} %copy.228), calls=%async_computation | async-start | bytes 3145728 | tf_op jit(solution)/shard_map/all_to_all | solution.py:739
  240.3 18.7 %copy-start.9 = (bf16[1024,4,64]{0,2,1:T(8,128)(2,1)}, bf16[1024,4,64]{0,2,1:T(8,128)(2,1)S(1)}, u32[]{:S(2)}) copy-start(bf16[1024,4,64]{0,2,1:T(8,128)(2,1)S(1)} %get-tuple-element.635) | copy-start | bytes 1572868
  252.9 11.9 %copy-start.35 = (bf16[1,12,3,4096]{3,2,1,0:T(4,128)(2,1)S(1)}, bf16[1,12,3,4096]{3,2,1,0:T(4,128)(2,1)}, u32[]{:S(2)}) copy-start(bf16[1,12,3,4096]{3,2,1,0:T(4,128)(2,1)} %param.34) | copy-start | bytes 884740
  253.8 22.6 %all-to-all-start.1 = ((bf16[4,2,32768]{2,1,0:T(2,128)(2,1)}), bf16[4,2,32768]{2,1,0:T(2,128)(2,1)}, u32[]{:S(2)}, u32[]{:S(2)}) async-start(bf16[4,2,32768]{2,1,0:T(2,128)(2,1)} %reshape.322), calls=%async_computation.1 | async-start | bytes 1048576 | tf_op jit(solution)/shard_map/all_to_all | solution.py:746
  284.1 17.5 %slice-start = ((s8[8388608]{0:T(1024)(128)(4,1)}), s8[4194304]{0:T(1024)(128)(4,1)S(1)}, s32[]{:S(2)}) async-start(s8[8388608]{0:T(1024)(128)(4,1)} %bitcast.280), calls=%async_computation.4 | async-start | bytes 8388608
  287.7 42.5 %copy-start.52 = (f32[256]{0:T(256)}, f32[256]{0:T(256)S(1)}, u32[]{:S(2)}) copy-start(f32[256]{0:T(256)S(1)} %broadcast_multiply_fusion.1) | copy-start | bytes 3076
  288.0 42.3 %copy-start.62 = (f32[256]{0:T(256)}, f32[256]{0:T(256)S(1)}, u32[]{:S(2)}) copy-start(f32[256]{0:T(256)S(1)} %fusion.100) | copy-start | bytes 3076
  288.0 13.6 %slice-start.1 = ((s8[8388608]{0:T(1024)(128)(4,1)}), s8[4194304]{0:T(1024)(128)(4,1)S(1)}, s32[]{:S(2)}) async-start(s8[8388608]{0:T(1024)(128)(4,1)} %bitcast.280), calls=%async_computation.5 | async-start | bytes 8388608
  301.6 13.6 %copy-start.11 = (f32[256,4096]{1,0:T(8,128)}, f32[256,4096]{1,0:T(8,128)S(1)}, u32[]{:S(2)}) copy-start(f32[256,4096]{1,0:T(8,128)S(1)} %get-tuple-element.474) | copy-start | bytes 12582916
  305.2 8.8 %copy-start.54 = (f32[256]{0:T(256)}, f32[256]{0:T(256)S(1)}, u32[]{:S(2)}) copy-start(f32[256]{0:T(256)S(1)} %broadcast_multiply_fusion) | copy-start | bytes 3076
  315.0 16.0 %copy-start.66 = (f32[256]{0:T(256)}, f32[256]{0:T(256)S(1)}, u32[]{:S(2)}) copy-start(f32[256]{0:T(256)S(1)} %negate_multiply_fusion.3) | copy-start | bytes 3076
  331.0 8.9 %copy-start.80 = (f32[6,32]{1,0:T(8,128)S(1)}, f32[6,32]{1,0:T(8,128)}, u32[]{:S(2)}) copy-start(f32[6,32]{1,0:T(8,128)} %param.58) | copy-start | bytes 2308
  331.0 9.7 %copy-start.49 = (f32[1,1024]{1,0:T(1,128)S(1)}, f32[1,1024]{1,0:T(1,128)}, u32[]{:S(2)}) copy-start(f32[1,1024]{1,0:T(1,128)} %copy-done.48) | copy-start | bytes 12292
  331.0 9.7 %copy-start.51 = (f32[256]{0:T(256)S(1)}, f32[256]{0:T(256)}, u32[]{:S(2)}) copy-start(f32[256]{0:T(256)} %copy-done.50) | copy-start | bytes 3076
  333.9 19.0 %all-to-all-start.2 = ((bf16[256,4,256]{0,2,1:T(8,128)(2,1)}), bf16[256,4,256]{0,2,1:T(8,128)(2,1)}, u32[]{:S(2)}, u32[]{:S(2)}) async-start(bf16[256,4,256]{0,2,1:T(8,128)(2,1)} %bitcast.39), calls=%async_computation.2 | async-start | bytes 1048576 | tf_op jit(solution)/shard_map/all_to_all | solution.py:772
  402.6 52.4 %all-to-all-start.3 = ((bf16[1024,3,1,256]{3,1,2,0:T(4,128)(2,1)}), bf16[1024,3,1,256]{3,1,2,0:T(4,128)(2,1)}, u32[]{:S(2)}, u32[]{:S(2)}) async-start(bf16[1024,3,1,256]{3,1,2,0:T(4,128)(2,1)} %copy.248), calls=%async_computation.3 | async-start | bytes 4194304 | tf_op jit(solution)/shard_map/all_to_all | solution.py:777
  419.9 43.3 %copy-start.6 = (f32[1024,256]{0,1:T(8,128)S(1)}, f32[1024,256]{0,1:T(8,128)}, u32[]{:S(2)}) copy-start(f32[1024,256]{0,1:T(8,128)} %copy-done.5) | copy-start | bytes 3145732
  478.7 179.3 %copy-start.40 = (f32[576,32]{0,1:T(8,128)S(1)}, f32[576,32]{0,1:T(8,128)}, u32[]{:S(2)}) copy-start(f32[576,32]{0,1:T(8,128)} %param.39) | copy-start | bytes 221188
  478.7 181.7 %copy-start.36 = (f32[32,768]{1,0:T(8,128)S(1)}, f32[32,768]{1,0:T(8,128)}, u32[]{:S(2)}) copy-start(f32[32,768]{1,0:T(8,128)} %param.54) | copy-start | bytes 294916
  478.7 181.7 %copy-start.44 = (f32[32,768]{1,0:T(8,128)S(1)}, f32[32,768]{1,0:T(8,128)}, u32[]{:S(2)}) copy-start(f32[32,768]{1,0:T(8,128)} %param.55) | copy-start | bytes 294916
  478.7 181.7 %copy-start.45 = (f32[32,768]{1,0:T(8,128)S(1)}, f32[32,768]{1,0:T(8,128)}, u32[]{:S(2)}) copy-start(f32[32,768]{1,0:T(8,128)} %param.56) | copy-start | bytes 294916
  478.7 183.4 %copy-start.21 = (f32[128,1024]{1,0:T(8,128)S(1)}, f32[128,1024]{1,0:T(8,128)}, u32[]{:S(2)}) copy-start(f32[128,1024]{1,0:T(8,128)} %param.51) | copy-start | bytes 1572868
  478.8 183.4 %copy-start.31 = (f32[128,1024]{1,0:T(8,128)S(1)}, f32[128,1024]{1,0:T(8,128)}, u32[]{:S(2)}) copy-start(f32[128,1024]{1,0:T(8,128)} %param.52) | copy-start | bytes 1572868
  478.8 183.4 %copy-start.32 = (f32[128,1024]{1,0:T(8,128)S(1)}, f32[128,1024]{1,0:T(8,128)}, u32[]{:S(2)}) copy-start(f32[128,1024]{1,0:T(8,128)} %param.53) | copy-start | bytes 1572868
  653.1 11.6 %copy-start.22 = (f32[32,4096]{1,0:T(8,128)S(1)}, f32[32,4096]{1,0:T(8,128)}, u32[]{:S(2)}) copy-start(f32[32,4096]{1,0:T(8,128)} %param.48) | copy-start | bytes 1572868
  653.1 11.6 %copy-start.33 = (f32[32,4096]{1,0:T(8,128)S(1)}, f32[32,4096]{1,0:T(8,128)}, u32[]{:S(2)}) copy-start(f32[32,4096]{1,0:T(8,128)} %param.49) | copy-start | bytes 1572868
  658.0 9.2 %copy-start.28 = (f32[32,1024]{1,0:T(8,128)S(1)}, f32[32,1024]{1,0:T(8,128)}, u32[]{:S(2)}) copy-start(f32[32,1024]{1,0:T(8,128)} %param.45) | copy-start | bytes 393220
  658.0 9.2 %copy-start.41 = (f32[32,1024]{1,0:T(8,128)S(1)}, f32[32,1024]{1,0:T(8,128)}, u32[]{:S(2)}) copy-start(f32[32,1024]{1,0:T(8,128)} %param.46) | copy-start | bytes 393220
  658.0 9.2 %copy-start.42 = (f32[32,1024]{1,0:T(8,128)S(1)}, f32[32,1024]{1,0:T(8,128)}, u32[]{:S(2)}) copy-start(f32[32,1024]{1,0:T(8,128)} %param.47) | copy-start | bytes 393220
  658.0 9.2 %copy-start.43 = (f32[32,1024]{1,0:T(8,128)S(1)}, f32[32,1024]{1,0:T(8,128)}, u32[]{:S(2)}) copy-start(f32[32,1024]{1,0:T(8,128)} %get-tuple-element.136) | copy-start | bytes 393220
  (65 other events, 323.4 us)

commit v2 on v1

--- a/solution.py
+++ b/solution.py
@@ -182,17 +182,52 @@
     pl.semaphore_wait(barrier, len(peers))
 
 
-def gather_kernel(items, wide, narrow, count, *refs):
-    ins, outs = refs[:count], refs[count : 2 * count]
-    own_sem, send_sem, recv_sem = refs[2 * count :]
+def normalize(values, gain, shift):
+    centred = values - jnp.mean(values, -1, keepdims=True)
+    spread = jnp.mean(centred * centred, -1, keepdims=True)
+    return centred * lax.rsqrt(spread + 1e-05) * gain + shift
+
+
+def forward_plan(widths):
+    items = []
+    for which, cuts in ((0, 1), (1, 3), (2, 1), (3, 4), (5, 1), (4, 4)):
+        size = widths[which] // cuts
+        for cut in range(cuts):
+            for side, (start, width) in enumerate(column_halves(size)):
+                items.append((which, cut * size + start, width, side))
+    return items
+
+
+def forward_kernel(items, wide, narrow, lead, ins, outs, scratch, *refs):
+    at = dict(zip(ins + outs + scratch, refs))
+    buf = {name: at["v_" + name] for name in outs}
+    weights = [at["first_weight"]] + [buf["w%d" % which] for which in range(1, 6)]
+    shards = [at["s%d" % which] for which in range(6)]
+    own_sem, send_sem, recv_sem, swap_send, swap_recv, out_sem = (at[name] for name in SEMS)
     place = Place(wide, narrow)
-    chips = place.chips
+    chips, me = place.chips, place.n
+    tokens = at["patches"].shape[0]
+    head_width = D // narrow
+    total = len(items)
+    started = []
+
+    def start(copy):
+        copy.start()
+        started.append(copy)
+
     greet(place.neighbours())
+    rows_of = [shard.shape[0] for shard in shards]
+
+    def rows_at(which, chip, core, node=None):
+        rows = rows_of[which]
+        if node is None:
+            return pl.ds(pl.multiple_of((chip * 2 + core) * narrow * rows, rows), narrow * rows)
+        return pl.ds(pl.multiple_of(((chip * 2 + core) * narrow + node) * rows, rows), rows)
 
     own = []
-    for which in range(count):
+    for which in range(6):
         copy = pltpu.make_async_copy(
-            ins[which], outs[which].at[place.chip, place.core, place.n], own_sem.at[which]
+            shards[which], weights[which].at[rows_at(which, place.chip, place.core, me), :], own_sem.at[which]
         )
         copy.start()
         own.append(copy)
@@ -208,15 +243,15 @@
         )
 
     def group(item, mask):
-        which, start, width, _ = items[item]
-        return outs[which].at[flip(place.chip, mask), place.core, :, :, pl.ds(start, width)]
+        which, begin, width, _ = items[item]
+        return weights[which].at[rows_at(which, flip(place.chip, mask), place.core), pl.ds(begin, width)]
 
     def along(item, step):
-        which, start, width, _ = items[item]
+        which, begin, width, _ = items[item]
         return remote(
             item,
-            ins[which].at[:, pl.ds(start, width)],
-            outs[which].at[place.chip, place.core, place.n, :, pl.ds(start, width)],
+            shards[which].at[:, pl.ds(begin, width)],
+            weights[which].at[rows_at(which, place.chip, place.core, me), pl.ds(begin, width)],
             2 * chips + step - 1,
             place.along(step),
         )
@@ -230,27 +265,23 @@
     def to_twin(item, mask):
         return remote(item, group(item, mask), group(item, mask), chips + mask, place.twin)
 
-    started = []
-
-    def start(copy):
-        copy.start()
-        started.append(copy)
-
-    def start_along(item):
-        for step in range(1, narrow):
-            start(along(item, step))
+    waited = set()
 
     def stage(item, number):
         bits = bits_of(item)
+        if number > len(bits):
+            for mask in range(chips):
+                to_twin(item, mask).wait_recv()
+            return
+        held = [0]
         if number == 0:
-            if item % 2 == 0:
+            if items[item][0] not in waited:
+                waited.add(items[item][0])
                 own[items[item][0]].wait()
             for step in range(1, narrow):
                 along(item, step).wait_recv()
-            held = [0]
             fresh = [0]
         else:
-            held = [0]
             for bit in bits[: number - 1]:
                 held = held + [mask ^ bit for mask in held]
             fresh = [mask ^ bits[number - 1] for mask in held]
@@ -263,48 +294,266 @@
         for mask in fresh:
             start(to_twin(item, mask))
 
-    total = len(items)
-    ahead = 4
-    for item in range(min(ahead, total)):
-        start_along(item)
-    depth = len(place.bits) + 1
-    for tick in range(0, total + 2 * (depth - 1), 2):
-        for number in reversed(range(depth)):
-            for item in (tick - 2 * number, tick - 2 * number + 1):
-                if 0 <= item < total:
-                    stage(item, number)
-        for item in (tick + ahead, tick + ahead + 1):
-            if item < total:
-                start_along(item)
-    for item in range(total):
-        for mask in range(chips):
-            to_twin(item, mask).wait_recv()
+    arrived = [False] * total
+
+    def gather():
+        ahead = 4
+        for item in range(min(ahead, total)):
+            for step in range(1, narrow):
+                start(along(item, step))
+        depth = len(place.bits) + 2
+        for tick in range(0, total + 2 * (depth - 1), 2):
+            for number in reversed(range(depth)):
+                for item in (tick - 2 * number, tick - 2 * number + 1):
+                    if 0 <= item < total:
+                        stage(item, number)
+                        if number == depth - 1:
+                            arrived[item] = True
+            for item in (tick + ahead, tick + ahead + 1):
+                if item < total:
+                    for step in range(1, narrow):
+                        start(along(item, step))
+            yield
+
+    engine = gather()
+
+    def advance(steps=1):
+        for _ in range(steps):
+            next(engine, None)
+
+    def need(which, columns=None):
+        wanted = [
+            index
+            for index, (owner, begin, width, _) in enumerate(items)
+            if owner == which and (columns is None or (begin < columns[1] and begin + width > columns[0]))
+        ]
+        while not all(arrived[index] for index in wanted):
+            next(engine)
+
+    flushed = []
+
+    def flush(name):
+        copy = pltpu.make_async_copy(buf[name], at[name], out_sem.at[outs.index(name)])
+        copy.start()
+        flushed.append(copy)
+
+    def swap(src, dst, kind, step):
+        return pltpu.make_async_remote_copy(
+            src_ref=src,
+            dst_ref=dst,
+            send_sem=swap_send.at[kind, step],
+            recv_sem=swap_recv.at[kind, step],
+            device_id=place.along(step),
+            device_id_type=MESH,
+        )
+
+    gains = buf["gains"]
+    embedded, mid, last = buf["embedded"], buf["mid"], buf["last"]
+    normed, hidden, wave = at["normed"], at["hidden"], at["wave"]
+    away, qkv, heads_out, returned = at["away"], buf["qkv"], buf["heads_out"], at["returned"]
+
+    need(0)
+    width = weights[0].shape[1]
+    kind = lax.broadcasted_iota(jnp.int32, (8, LANES), 0)
+    spot = lax.broadcasted_iota(jnp.int32, (8, LANES), 1)
+    pick = (spot == kind + lead).astype(F32).astype(BF16)
+    gains[...] = back_mul(pick, weights[0][:, width - LANES :])
+    for block in range(0, D, 256):
+        cols = pl.ds(block, 256)
+        embedded[:, cols] = back_mul(at["patches"][...], weights[0][pl.ds(block, 256), : at["patches"].shape[1]])
+    flush("embedded")
+    flush("gains")
+
+    def norm_rows(source, row, dest):
+        step_rows = 64
+
+        def one(step, carry):
+            rows = pl.ds(pl.multiple_of(step * step_rows, step_rows), step_rows)
+            dest[rows, :] = normalize(
+                source[rows, :], gains[row : row + 1, :], gains[row + 3 : row + 4, :]
+            ).astype(BF16)
+            return carry
+
+        lax.fori_loop(0, tokens // step_rows, one, 0)
+
+    norm_rows(embedded, 0, normed)
+    need(1)
+    for step in list(range(1, narrow)) + [0]:
+        owner = lax.rem(me + step, narrow)
+
+        def project(part, carry):
+            offset = pl.multiple_of(part * D + owner * head_width, LANES)
+            value = matmul(normed[...], weights[1][:, pl.ds(offset, head_width)]).astype(BF16)
+            if step:
+                away[step - 1, part] = value
+            else:
+                qkv[me, part] = value
+            return carry
+
+        lax.fori_loop(0, 3, project, 0)
+        if step:
+            start(swap(away.at[step - 1], qkv.at[me], 0, step))
+    flush("w1")
+    buf["t1"][...] = normed[...].T
+    flush("t1")
+    advance(2)
+    for step in range(1, narrow):
+        swap(away.at[step - 1], qkv.at[me], 0, step).wait_recv()
+    flush("qkv")
+
+    lane = lax.broadcasted_iota(jnp.int32, (1, LANES), 1)
+    scale = HD ** (-0.5)
+    length = narrow * tokens
+    for step in list(range(1, narrow)) + [0]:
+        who = lax.rem(me + step, narrow)
+        log_sums = jnp.zeros((tokens, LANES), F32)
+        for pair in range(head_width // LANES):
+            lanes = pl.ds(pair * LANES, LANES)
+            query = qkv[who, 0, :, lanes].astype(F32)
+            key = qkv[:, 1, :, lanes].reshape(length, LANES)
+            value = qkv[:, 2, :, lanes].reshape(length, LANES)
+            out = jnp.zeros((tokens, LANES), F32)
+            for side in range(LANES // HD):
+                inside = lane // HD == side
+                own_query = (query * jnp.where(inside, scale, 0.0)).astype(BF16)
+                scores = back_mul(own_query, key)
+                highest = jnp.max(scores, -1, keepdims=True)
+                exponentials = jnp.exp(scores - highest)
+                summed = jnp.sum(exponentials, -1, keepdims=True)
+                part = matmul(exponentials.astype(BF16), value) / summed
+                out = jnp.where(inside, part, out)
+                log_sums = jnp.where(
+                    lane == pair * (LANES // HD) + side, highest + jnp.log(summed), log_sums
+                )
+            heads_out[who, :, lanes] = out.astype(BF16)
+        buf["log_sums"][who] = log_sums
+        if step:
+            start(swap(heads_out.at[who], returned.at[me], 1, step))
+            if step % 2 == 0:
+                advance()
+        else:
+            returned[me] = heads_out[who]
+    flush("heads_out")
+    flush("log_sums")
+    need(2)
+    for step in range(1, narrow):
+        swap(heads_out.at[me], returned.at[me], 1, step).wait_recv()
+    for block in range(0, D, 256):
+        cols = pl.ds(block, 256)
+        value = embedded[:, cols]
+        for source in range(narrow):
+            value = value + matmul(returned[source], weights[2][pl.ds(source * head_width, head_width), cols])
+        mid[:, cols] = value
+    flush("w2")
+    flush("mid")
+    norm_rows(mid, 1, normed)
+    for source in range(narrow):
+        buf["t2"][pl.ds(source * head_width, head_width), :] = returned[source].T
+    buf["t3"][...] = normed[...].T
+    flush("t2")
+    flush("t3")
+
+    ff = weights[3].shape[1]
+    tile = wave.shape[1]
+    slopes = buf["slopes"]
+    for block in range(0, ff, tile):
+        need(3, (block, block + tile))
+        wave[...] = matmul(normed[...], weights[3][:, pl.ds(block, tile)])
+
+        def bend(step, carry):
+            rows = pl.ds(pl.multiple_of(step * 16, 16), 16)
+            x = wave[rows, :]
+            half = 0.5 * (1.0 + lax.erf(x * (0.5**0.5)))
+            hidden[rows, pl.ds(block, tile)] = (x * half).astype(BF16)
+            bell = jnp.exp(-0.5 * x * x) * 0.3989422804014327
+            slopes[rows, pl.ds(block, tile)] = (half + x * bell).astype(BF16)
+            return carry
+
+        lax.fori_loop(0, tokens // 16, bend, 0)
+        buf["t4"][pl.ds(block, tile), :] = hidden[:, pl.ds(block, tile)].T
+    flush("w3")
+    flush("slopes")
+    flush("t4")
+    for block in range(0, D, 256):
+        need(4, (block, block + 256))
+        cols = pl.ds(block, 256)
+        last[:, cols] = mid[:, cols] + matmul(hidden[...], weights[4][:, cols])
+    flush("w4")
+    flush("last")
+    norm_rows(last, 2, normed)
+    need(5)
+    for block in range(0, weights[5].shape[1], 256):
+        cols = pl.ds(block, 256)
+        buf["gaussians"][:, cols] = matmul(normed[...], weights[5][:, cols])
+    flush("w5")
+    flush("gaussians")
+    buf["t5"][...] = normed[...].T
+    flush("t5")
+    advance(total)
     for copy in started:
         copy.wait_send()
-
-
-def gather_all(shards, wide, narrow):
-    count = len(shards)
+    for copy in flushed:
+        copy.wait()
+
+
+SEMS = ("own_sem", "send_sem", "recv_sem", "swap_send", "swap_recv", "out_sem")
+
+
+def forward_all(shards, patches, lead, wide, narrow):
+    tokens = patches.shape[0]
     widths = [shard.shape[1] for shard in shards]
-    items = work_items(widths, range(count))
+    heights = [shard.shape[0] * wide * narrow for shard in shards]
+    ff = widths[3]
+    head_width = D // narrow
+    items = forward_plan(widths)
     slots = wide + narrow - 1
-    shapes = [
-        jax.ShapeDtypeStruct((wide // 2, 2, narrow) + shard.shape, shard.dtype) for shard in shards
-    ]
-    whole = pl.pallas_call(
-        functools.partial(gather_kernel, items, wide, narrow, count),
-        out_shape=shapes,
-        in_specs=[pl.BlockSpec(memory_space=pl.ANY)] * count,
-        out_specs=[pl.BlockSpec(memory_space=pl.ANY)] * count,
-        scratch_shapes=[
-            pltpu.SemaphoreType.DMA((count,)),
-            pltpu.SemaphoreType.DMA((len(items), slots)),
-            pltpu.SemaphoreType.DMA((len(items), slots)),
-        ],
-        compiler_params=pltpu.CompilerParams(collective_id=0, has_side_effects=True),
-        name="gather_weights",
-    )(*shards)
-    return [full.reshape(-1, width) for full, width in zip(whole, widths)]
+    shapes = {"w%d" % which: ((heights[which], widths[which]), BF16) for which in range(1, 6)}
+    shapes.update(
+        gains=((8, D), F32),
+        embedded=((tokens, D), F32),
+        mid=((tokens, D), F32),
+        last=((tokens, D), F32),
+        slopes=((tokens, ff), BF16),
+        t1=((D, tokens), BF16),
+        t2=((D, tokens), BF16),
+        t3=((D, tokens), BF16),
+        t4=((ff, tokens), BF16),
+        t5=((D, tokens), BF16),
+        qkv=((narrow, 3, tokens, head_width), BF16),
+        heads_out=((narrow, tokens, head_width), BF16),
+        log_sums=((narrow, tokens, LANES), F32),
+        gaussians=((tokens, widths[5]), F32),
+    )
+    ins = tuple("s%d" % which for which in range(6)) + ("patches",)
+    outs = tuple(shapes)
+    extras = dict(
+        first_weight=pltpu.VMEM((heights[0], widths[0]), BF16),
+        normed=pltpu.VMEM((tokens, D), BF16),
+        hidden=pltpu.VMEM((tokens, ff), BF16),
+        wave=pltpu.VMEM((tokens, 512), F32),
+        away=pltpu.VMEM((narrow - 1, 3, tokens, head_width), BF16),
+        returned=pltpu.VMEM((narrow, tokens, head_width), BF16),
+        own_sem=pltpu.SemaphoreType.DMA((6,)),
+        send_sem=pltpu.SemaphoreType.DMA((len(items), slots)),
+        recv_sem=pltpu.SemaphoreType.DMA((len(items), slots)),
+        swap_send=pltpu.SemaphoreType.DMA((2, narrow)),
+        swap_recv=pltpu.SemaphoreType.DMA((2, narrow)),
+        out_sem=pltpu.SemaphoreType.DMA((len(outs),)),
+    )
+    scratch = tuple("v_" + name for name in outs) + tuple(extras)
+    anywhere = pl.BlockSpec(memory_space=pl.ANY)
+    results = pl.pallas_call(
+        functools.partial(forward_kernel, items, wide, narrow, lead, ins, outs, scratch),
+        out_shape=[jax.ShapeDtypeStruct(*shapes[name]) for name in outs],
+        in_specs=[anywhere] * 6 + [pl.BlockSpec(memory_space=pltpu.VMEM)],
+        out_specs=[anywhere] * len(outs),
+        scratch_shapes=[pltpu.VMEM(*shapes[name]) for name in outs] + list(extras.values()),
+        compiler_params=pltpu.CompilerParams(
+            collective_id=0, has_side_effects=True, vmem_limit_bytes=60 * MIB
+        ),
+        name="forward",
+    )(*shards, patches)
+    return dict(zip(outs, results))
 
 
 def tile_of(width):
@@ -679,6 +928,55 @@
     )(gaussians, spread, wanted, valid, pairs, view_count, pair_total)
 
 
+def forward_plain(shards, patches, features, kinds):
+    weights = [lax.all_gather(shard, ("wide", "narrow"), axis=0, tiled=True) for shard in shards]
+    groups = lax.axis_size("narrow")
+    rows = patches.shape[0]
+    gains = weights[0][:, features : features + kinds].T.astype(F32)
+    embedded = back_mul(patches[:, :features], weights[0][:, :features])
+    normed_one = layer_norm(embedded, gains[0], gains[3]).astype(BF16)
+    mixed = matmul(normed_one, weights[1]).astype(BF16).reshape(rows, 3, groups, -1)
+    mixed = mixed.transpose(2, 1, 0, 3)
+    qkv = lax.all_to_all(mixed, "narrow", split_axis=0, concat_axis=0, tiled=True)
+    width = qkv.shape[-1]
+    length = groups * rows
+    heads = width // HD
+    parts = [qkv[:, part].reshape(length, heads, HD) for part in range(3)]
+    attended, logsum = attention_forward(*parts)
+    log_sums = logsum.transpose(0, 2, 1).reshape(groups, rows, heads)
+    returned = lax.all_to_all(
+        attended.reshape(groups, rows, width), "narrow", split_axis=0, concat_axis=0, tiled=True
+    )
+    returned = returned.transpose(1, 0, 2).reshape(rows, D)
+    mid = embedded + matmul(returned, weights[2])
+    normed_two = layer_norm(mid, gains[1], gains[4]).astype(BF16)
+    expanded = matmul(normed_two, weights[3])
+    half = 0.5 * (1.0 + lax.erf(expanded * (0.5**0.5)))
+    activated = (expanded * half).astype(BF16)
+    bell = jnp.exp(-0.5 * expanded * expanded) * 0.3989422804014327
+    slopes = (half + expanded * bell).astype(BF16)
+    last = mid + matmul(activated, weights[4])
+    normed_three = layer_norm(last, gains[2], gains[5]).astype(BF16)
+    kept = {"w%d" % which: weights[which] for which in range(1, 6)}
+    kept.update(
+        gains=gains,
+        embedded=embedded,
+        mid=mid,
+        last=last,
+        slopes=slopes,
+        t1=normed_one.T,
+        t2=returned.T,
+        t3=normed_two.T,
+        t4=activated.T,
+        t5=normed_three.T,
+        qkv=qkv,
+        heads_out=attended,
+        log_sums=log_sums,
+        gaussians=matmul(normed_three, weights[5]),
+    )
+    return kept
+
+
 def body(
     views,
     render_w,
@@ -723,39 +1021,29 @@
     first_shard = jnp.concatenate([embed_weight.T, norm_params.T], 1)
     first_shard = jnp.pad(first_shard.astype(BF16), ((0, 0), (0, fill)))
     shards = [first_shard] + [weight.astype(BF16) for weight in masters[1:6]]
-    if by_kernel:
-        weights = gather_all(shards, wide_count, groups)
-    else:
-        weights = [lax.all_gather(shard, ("wide", "narrow"), axis=0, tiled=True) for shard in shards]
-    gains = weights[0][:, features : features + kinds].T.astype(F32)
-
     patches = views.reshape(-1, features)
     rows = patches.shape[0]
     patches = jnp.pad(patches, ((0, 0), (0, padded - features)))
-    embedded = back_mul(patches[:, :features], weights[0][:, :features])
-    normed_one, norm_back_one = jax.vjp(layer_norm, embedded, gains[0], gains[3])
-    normed_one = normed_one.astype(BF16)
-    mixed = matmul(normed_one, weights[1]).astype(BF16).reshape(rows, 3, groups, -1)
-    spread = lax.all_to_all(mixed, "narrow", split_axis=2, concat_axis=0, tiled=True)
-    length, width = (spread.shape[0], spread.shape[-1])
+    if by_kernel:
+        kept = forward_all(shards, patches, features % LANES, wide_count, groups)
+    else:
+        kept = forward_plain(shards, patches, features, kinds)
+    gains = kept["gains"]
+    weights = [None] + [kept["w%d" % which] for which in range(1, 6)]
+    norm_back_one = jax.vjp(layer_norm, kept["embedded"], gains[0], gains[3])[1]
+    norm_back_two = jax.vjp(layer_norm, kept["mid"], gains[1], gains[4])[1]
+    norm_back_three = jax.vjp(layer_norm, kept["last"], gains[2], gains[5])[1]
+    qkv = kept["qkv"]
+    width = qkv.shape[-1]
+    length = groups * rows
     local_heads = width // HD
-    queries = spread[:, 0, 0].reshape(length, local_heads, HD)
-    keys_all = spread[:, 1, 0].reshape(length, local_heads, HD)
-    values_all = spread[:, 2, 0].reshape(length, local_heads, HD)
-    attended, logsum = attention_forward(queries, keys_all, values_all)
-    returned = lax.all_to_all(
-        attended.reshape(length, 1, width), "narrow", split_axis=0, concat_axis=1, tiled=True
-    ).reshape(rows, D)
-    residual_one = embedded + matmul(returned, weights[2])
-    normed_two, norm_back_two = jax.vjp(layer_norm, residual_one, gains[1], gains[4])
-    normed_two = normed_two.astype(BF16)
-    expanded = matmul(normed_two, weights[3])
-    activated, gelu_back = jax.vjp(exact_gelu, expanded)
-    activated = activated.astype(BF16)
-    residual_two = residual_one + matmul(activated, weights[4])
-    normed_three, norm_back_three = jax.vjp(layer_norm, residual_two, gains[2], gains[5])
-    normed_three = normed_three.astype(BF16)
-    gaussians = matmul(normed_three, weights[5])
+    queries, keys_all, values_all = (
+        qkv[:, part].reshape(length, local_heads, HD) for part in range(3)
+    )
+    blocked = min(512, length)
+    logsum = kept["log_sums"][:, :, :local_heads].reshape(length // blocked, blocked, local_heads)
+    logsum = logsum.transpose(0, 2, 1)
+    gaussians = kept["gaussians"]
     divisor = pair_total[0].astype(F32)
 
     gauss_low, term = render(
@@ -763,8 +1051,7 @@
     )
     residual_grad, gain_three, shift_three = norm_back_three(back_mul(gauss_low, weights[5]))
     shrink_low = residual_grad.astype(BF16)
-    (expand_grad,) = gelu_back(back_mul(shrink_low, weights[4]))
-    expand_low = expand_grad.astype(BF16)
+    expand_low = (back_mul(shrink_low, weights[4]) * kept["slopes"].astype(F32)).astype(BF16)
     through_two, gain_two, shift_two = norm_back_two(back_mul(expand_low, weights[3]))
     residual_grad = residual_grad + through_two
     merge_low = residual_grad.astype(BF16)
@@ -781,7 +1068,7 @@
     embed_grad = (residual_grad + through_one).astype(BF16)
     grad_norms = jnp.stack([gain_one, gain_two, gain_three, shift_one, shift_two, shift_three])
 
-    lefts = [embed_grad.T, normed_one.T, returned.T, normed_two.T, activated.T, normed_three.T]
+    lefts = [embed_grad.T] + [kept["t%d" % which] for which in range(1, 6)]
     rights = [patches, mixed_grad, merge_low, expand_low, shrink_low, gauss_low]
     at = features % LANES
     extra = jnp.pad(grad_norms.T, ((0, 0), (at, LANES - at - kinds)))

time: 680 us -> 581 us (0.85)
  local copies, waits for them, and re-layouts: 94.9 us -> 49.3 us
  Pallas kernels: 323 us -> 362 us
  matrix products: 87.3 us -> 48.7 us
  waiting for transfers between devices: 75 us -> 50.9 us
  other arithmetic: 59.4 us -> 36.7 us
  starting transfers between devices: 24.8 us -> 14.8 us
    pallas_call x1, Pallas kernels: 144 us -> 184 us  [forward_all(): pl.pallas_call(functools.partial(forward_kernel, items, wide, narrow, lea...]
    all_to_all x2 -> x0, waiting for transfers between devices: 37.8 us -> none  [the longest x1 37.8 us: body(): lax.all_to_all(mixed, 'narrow', split_axis=2, concat_axis=0, tiled=True)]
    dot_general x7 -> x0, matrix products: 31.7 us -> none  [the longest x5 27.3 us: matmul(): return jnp.dot(left, right, preferred_element_type=F32)]
    convert_element_type x4 -> x0, other arithmetic: 17.3 us -> none  [the longest x1 10.2 us: body(): activated = activated.astype(BF16)]
    all_to_all x2 -> x0, starting transfers between devices: 15.1 us -> none  [the longest x1 10.6 us: body(): lax.all_to_all(mixed, 'narrow', split_axis=2, concat_axis=0, tiled=True)]
    all_to_all x1, waiting for transfers between devices: 35.1 us -> 46.9 us  [body(): lax.all_to_all(stacked, 'narrow', split_axis=0, concat_axis=2, tiled=True)]
    reshape x3 -> x1, local copies, waits for them, and re-layouts: 9.59 us -> 1.22 us  [body(): kept['log_sums'][:, :, :local_heads]]
    convert_element_type x4 -> x0, local copies, waits for them, and re-layouts: 8.13 us -> none  [the longest x1 2.04 us: body(): normed_three = normed_three.astype(BF16)]
  transfers between devices with their start and end apart: 4 -> 2, of which waited for: 3 -> 2; matrix products, arithmetic and copies ran while one was open for 6% -> 2% of each run, Pallas kernels for 0% -> 0%
where the time goes in v2:
time: 581 us; the launch traced here: 570 us
  Pallas kernels  362 us (62%)
  waiting for transfers between devices  50.9 us (9%)
  local copies, waits for them, and re-layouts  49.3 us (8%)
  matrix products  48.7 us (8%)
  other arithmetic  36.7 us (6%)
  starting transfers between devices  14.8 us (3%)
  between operations  6.99 us (1%)
    pallas_call x1, Pallas kernels, forward_all(): pl.pallas_call(functools.partial(forward_kernel, items, wide, narrow, lea...  184 us
    pallas_call x1, Pallas kernels, reduce_all(): pl.pallas_call(functools.partial(reduce_kernel, items, wide, narrow, coun...  173 us
    all_to_all x1, waiting for transfers between devices, body(): lax.all_to_all(stacked, 'narrow', split_axis=0, concat_axis=2, tiled=True)  46.9 us
    dot_general x5, matrix products, back_mul(): lax.dot_general(grad, weight, (((1,), (1,)), ((), ())), preferred_element...  19.7 us
  transfers between devices with their start and end apart: 2, of which 2 were waited for; matrix products, arithmetic and copies ran while one was open for 2% of the time, Pallas kernels for 0%

profile of v2, /device:TPU:0, one launch (start us, length us, event | category | flops | bytes accessed | tf_op | source)
XLA Modules:
  0.0 569.9 jit_solution(17016086475506681709)
XLA Ops:
  13.1 184.3 %forward.1 = (bf16[1024,3072]{1,0:T(8,128)(2,1)}, bf16[1024,1024]{1,0:T(8,128)(2,1)}, bf16[1024,4096]{1,0:T(8,128)(2,1)}, bf16[4096,1024]{1,0:T(8,128)(2,1)}, bf...) custom-call(bf16[32,640]{1,0:T(8,128)(2,1)} %fusion.40.refs_0_, ...), custom_call_target="tpu_custom_call" | custom-call | tf_op jit(solution)/shard_map/forward/pallas_call | solution.py:545
  201.0 2.3 copy.174
  208.7 4.9 render.1
  214.2 3.3 multiply_reduce_fusion.1
  220.6 6.6 %fusion.30.refs_9_ = bf16[256,4096]{1,0:T(8,128)(2,1)S(1)} fusion(bf16[256,1024]{1,0:T(8,128)(2,1)S(1)} %add_convert_fusion.1.refs_10_, bf16[4096,1024]{1,0:T(8,128)(2,1)} %get-tuple-element.104, bf16[256,4096]{1,0:T(8,128)(2,1)} %get-tuple-element.105), kind=kOutput, calls=%fused_computation.32 | convolution fusion | flops 2150629376 | bytes 13107200 | tf_op jit(solution)/shard_map/dot_general | solution.py:42
  227.3 3.2 multiply_reduce_fusion.2
  234.4 10.5 %all-to-all-start = ((bf16[256,4,256]{0,2,1:T(8,128)(2,1)}), bf16[256,4,256]{0,2,1:T(8,128)(2,1)}, u32[]{:S(2)}, u32[]{:S(2)}) async-start(bf16[256,4,256]{0,2,1:T(8,128)(2,1)} %bitcast.12), calls=%async_computation | async-start | bytes 1048576 | tf_op jit(solution)/shard_map/all_to_all | solution.py:1059
  244.9 2.5 fusion.56
  247.5 2.0 reshape.267
  256.3 4.0 all-to-all-done
  264.0 38.1 %while.15 = (s32[]{:T(128)}, f32[1024,4,64]{0,2,1:T(8,128)S(1)}, f32[1024,4,64]{0,2,1:T(8,128)S(1)}, bf16[2,512,4,64]{1,3,2,0:T(8,128)(2,1)}, bf16[2,512,4,64]{1...) while((s32[]{:T(128)}, f32[1024,4,64]{0,2,1:T(8,128)S(1)}, ...), condition=%wide.region_10.11_spmd.clone, body=%wide.region_8.10_spmd.clone.sunk | while | flops 1368782848 | bytes 143713584 | solution.py:116
  264.0 2.3 fusion.96
  266.4 2.9 multiply_reduce_fusion.11
  269.6 3.3 multiply_convert_fusion.2
  272.9 3.4 fusion.97
  276.3 4.1 fusion.99
  281.2 1.9 fusion.98
  283.1 2.3 fusion.96
  285.4 2.9 multiply_reduce_fusion.11
  288.7 3.3 multiply_convert_fusion.2
  292.0 3.4 fusion.97
  295.3 4.1 fusion.99
  300.2 1.9 fusion.98
  304.5 2.6 copy.161
  307.0 4.3 all-to-all-start.1
  312.9 46.9 %all-to-all-done.1 = bf16[1024,3,1,256]{3,1,2,0:T(4,128)(2,1)S(1)} async-done(((bf16[1024,3,1,256]{3,1,2,0:T(4,128)(2,1)}), bf16[1024,3,1,256]{3,1,2,0:T(4,128)(2,1)S(1)}, u32[]{:S(2)}, u32[]{:S(2)}) %all-to-all-start.1) | async-done | bytes 1572896 | tf_op jit(solution)/shard_map/all_to_all | solution.py:1064
  360.0 2.4 copy.163
  362.4 3.1 reshape.252.refs_7_
  366.8 5.9 %multiply_reduce_fusion.3 = (f32[1024]{0:T(1024)S(1)}, f32[256]{0:T(256)S(1)}, f32[1024]{0:T(1024)S(1)}, f32[256,1024]{1,0:T(8,128)}) fusion(f32[256,1024]{1,0:T(8,128)S(1)} %copy-done.10, f32[256]{0:T(256)S(1)} %fusion.44, f32[256]{0:T(256)S(1)} %copy-done.47, f32[1024]{0:T(1024)S(1)} %bitcast.151, bf16[256,3072]{1,0:T(8,128)(2,1)S(1)} %reshape.252.refs_7_, ...), kind=kOutput, calls=%fused_computation.40 | convolution fusion | flops 1612707584 | bytes 9976832 | tf_op jit(solution)/shard_map/dot_general | solution.py:42
  373.8 2.0 pad.14.clone
  378.8 173.0 %reduce_grads.1 = (f32[32,640]{1,0:T(8,128)}, f32[32,3072]{1,0:T(8,128)}, f32[32,1024]{1,0:T(8,128)}, f32[32,4096]{1,0:T(8,128)}, f32[128,1024]{1,0:T(8,128)}, /*index=5*/f32[32,768]{1,0:T(8,128)}, f32[8,128]{1,0:T(8,128)}) custom-call(bf16[4,2,4,32,256]{4,3,2,1,0:T(8,128)(2,1)} %bitcast.134, bf16[4,2,4,32,256]{4,3,2,1,0:T(8,128)(2,1)} %bitcast.140, ...), custom_call_target="tpu_custom_call" | custom-call | tf_op jit(solution)/shard_map/reduce_grads/pallas_call | solution.py:794
  561.1 2.6 multiply_subtract_fusion
  (208 shorter events, 60.6 us)
Async XLA Ops:
  197.4 6.4 %copy-start.29 = (bf16[1,12,3,4096]{3,2,1,0:T(4,128)(2,1)S(1)}, bf16[1,12,3,4096]{3,2,1,0:T(4,128)(2,1)}, u32[]{:S(2)}) copy-start(bf16[1,12,3,4096]{3,2,1,0:T(4,128)(2,1)} %param.32) | copy-start | bytes 884740
  219.1 11.9 %copy-start.7 = (f32[256,1024]{1,0:T(8,128)}, f32[256,1024]{1,0:T(8,128)S(1)}, u32[]{:S(2)}) copy-start(f32[256,1024]{1,0:T(8,128)S(1)} %get-tuple-element.372) | copy-start | bytes 3145732
  219.1 11.9 %copy-start.44 = (f32[256]{0:T(256)}, f32[256]{0:T(256)S(1)}, u32[]{:S(2)}) copy-start(f32[256]{0:T(256)S(1)} %negate_multiply_fusion.2) | copy-start | bytes 3076
  219.5 7.8 %copy-start.46 = (f32[256]{0:T(256)}, f32[256]{0:T(256)S(1)}, u32[]{:S(2)}) copy-start(f32[256]{0:T(256)S(1)} %broadcast_multiply_fusion) | copy-start | bytes 3076
  220.5 6.8 %slice-start = ((s8[8388608]{0:T(1024)(128)(4,1)}), s8[4194304]{0:T(1024)(128)(4,1)S(1)}, s32[]{:S(2)}) async-start(s8[8388608]{0:T(1024)(128)(4,1)} %bitcast.163), calls=%async_computation.2 | async-start | bytes 8388608
  220.6 6.7 %copy-start.16 = (bf16[256,1024]{1,0:T(8,128)(2,1)}, bf16[256,1024]{1,0:T(8,128)(2,1)S(1)}, u32[]{:S(2)}) copy-start(bf16[256,1024]{1,0:T(8,128)(2,1)S(1)} %add_convert_fusion.1.refs_10_) | copy-start | bytes 1572868
  220.6 6.7 %slice-start.1 = ((s8[8388608]{0:T(1024)(128)(4,1)}), s8[4194304]{0:T(1024)(128)(4,1)S(1)}, s32[]{:S(2)}) async-start(s8[8388608]{0:T(1024)(128)(4,1)} %bitcast.163), calls=%async_computation.3 | async-start | bytes 8388608
  234.4 25.9 %all-to-all-start = ((bf16[256,4,256]{0,2,1:T(8,128)(2,1)}), bf16[256,4,256]{0,2,1:T(8,128)(2,1)}, u32[]{:S(2)}, u32[]{:S(2)}) async-start(bf16[256,4,256]{0,2,1:T(8,128)(2,1)} %bitcast.12), calls=%async_computation | async-start | bytes 1048576 | tf_op jit(solution)/shard_map/all_to_all | solution.py:1059
  272.9 8.3 %copy-start.5 = (f32[4,512,1024]{2,1,0:T(8,128)S(1)}, f32[4,512,1024]{2,1,0:T(8,128)}, u32[]{:S(2)}) copy-start(f32[4,512,1024]{2,1,0:T(8,128)} %copy-done.4) | copy-start | bytes 25165828 | tf_op jit(solution)/shard_map/while
  292.0 8.3 %copy-start.5 = (f32[4,512,1024]{2,1,0:T(8,128)S(1)}, f32[4,512,1024]{2,1,0:T(8,128)}, u32[]{:S(2)}) copy-start(f32[4,512,1024]{2,1,0:T(8,128)} %copy-done.4) | copy-start | bytes 25165828 | tf_op jit(solution)/shard_map/while
  304.4 7.0 %copy-start.43 = (f32[6,32]{1,0:T(8,128)S(1)}, f32[6,32]{1,0:T(8,128)}, u32[]{:S(2)}) copy-start(f32[6,32]{1,0:T(8,128)} %param.55) | copy-start | bytes 2308
  304.4 7.1 %copy-start.53 = (f32[6,32]{1,0:T(8,128)S(1)}, f32[6,32]{1,0:T(8,128)}, u32[]{:S(2)}) copy-start(f32[6,32]{1,0:T(8,128)} %param.56) | copy-start | bytes 2308
  304.4 7.7 %copy-start.54 = (f32[6,32]{1,0:T(8,128)S(1)}, f32[6,32]{1,0:T(8,128)}, u32[]{:S(2)}) copy-start(f32[6,32]{1,0:T(8,128)} %param.57) | copy-start | bytes 2308
  304.5 8.4 %copy-start.48 = (f32[256]{0:T(256)S(1)}, f32[256]{0:T(256)}, u32[]{:S(2)}) copy-start(f32[256]{0:T(256)} %get-tuple-element.386) | copy-start | bytes 3076
  307.0 52.8 %all-to-all-start.1 = ((bf16[1024,3,1,256]{3,1,2,0:T(4,128)(2,1)}), bf16[1024,3,1,256]{3,1,2,0:T(4,128)(2,1)S(1)}, u32[]{:S(2)}, u32[]{:S(2)}) async-start(bf16[1024,3,1,256]{3,1,2,0:T(4,128)(2,1)} %copy.161), calls=%async_computation.1 | async-start | bytes 4194304 | tf_op jit(solution)/shard_map/all_to_all | solution.py:1064
  312.9 53.8 %copy-start.10 = (f32[256,1024]{1,0:T(8,128)S(1)}, f32[256,1024]{1,0:T(8,128)}, u32[]{:S(2)}) copy-start(f32[256,1024]{1,0:T(8,128)} %get-tuple-element.115) | copy-start | bytes 3145732
  312.9 53.8 %copy-start.42 = (f32[1,1024]{1,0:T(1,128)S(1)}, f32[1,1024]{1,0:T(1,128)}, u32[]{:S(2)}) copy-start(f32[1,1024]{1,0:T(1,128)} %get-tuple-element.378) | copy-start | bytes 12292
  312.9 53.8 %copy-start.47 = (f32[256]{0:T(256)S(1)}, f32[256]{0:T(256)}, u32[]{:S(2)}) copy-start(f32[256]{0:T(256)} %copy-done.46) | copy-start | bytes 3076
  366.7 6.0 %copy-start.49 = (f32[1024]{0:T(1024)S(1)}, f32[1024]{0:T(1024)}, u32[]{:S(2)}) copy-start(f32[1024]{0:T(1024)} %get-tuple-element.319) | copy-start | bytes 12292
  378.8 175.2 %copy-start.40 = (f32[6,32]{0,1:T(8,128)S(1)}, f32[6,32]{0,1:T(8,128)}, u32[]{:S(2)}) copy-start(f32[6,32]{0,1:T(8,128)} %copy.166) | copy-start | bytes 2308
  378.8 175.2 %copy-start.41 = (f32[6,32]{0,1:T(8,128)S(1)}, f32[6,32]{0,1:T(8,128)}, u32[]{:S(2)}) copy-start(f32[6,32]{0,1:T(8,128)} %copy.168) | copy-start | bytes 2308
  378.8 178.0 %copy-start.34 = (f32[576,32]{0,1:T(8,128)S(1)}, f32[576,32]{0,1:T(8,128)}, u32[]{:S(2)}) copy-start(f32[576,32]{0,1:T(8,128)} %param.37) | copy-start | bytes 221188
  378.8 178.0 %copy-start.39 = (f32[576,32]{0,1:T(8,128)S(1)}, f32[576,32]{0,1:T(8,128)}, u32[]{:S(2)}) copy-start(f32[576,32]{0,1:T(8,128)} %param.38) | copy-start | bytes 221188
  378.8 180.5 %copy-start.30 = (f32[32,768]{1,0:T(8,128)S(1)}, f32[32,768]{1,0:T(8,128)}, u32[]{:S(2)}) copy-start(f32[32,768]{1,0:T(8,128)} %param.52) | copy-start | bytes 294916
  378.8 182.3 %copy-start.18 = (f32[128,1024]{1,0:T(8,128)S(1)}, f32[128,1024]{1,0:T(8,128)}, u32[]{:S(2)}) copy-start(f32[128,1024]{1,0:T(8,128)} %param.49) | copy-start | bytes 1572868
  378.8 182.3 %copy-start.24 = (f32[128,1024]{1,0:T(8,128)S(1)}, f32[128,1024]{1,0:T(8,128)}, u32[]{:S(2)}) copy-start(f32[128,1024]{1,0:T(8,128)} %param.50) | copy-start | bytes 1572868
  378.8 182.3 %copy-start.25 = (f32[128,1024]{1,0:T(8,128)S(1)}, f32[128,1024]{1,0:T(8,128)}, u32[]{:S(2)}) copy-start(f32[128,1024]{1,0:T(8,128)} %param.51) | copy-start | bytes 1572868
  551.9 11.8 %copy-start.19 = (f32[32,4096]{1,0:T(8,128)S(1)}, f32[32,4096]{1,0:T(8,128)}, u32[]{:S(2)}) copy-start(f32[32,4096]{1,0:T(8,128)} %param.46) | copy-start | bytes 1572868
  551.9 11.8 %copy-start.26 = (f32[32,4096]{1,0:T(8,128)S(1)}, f32[32,4096]{1,0:T(8,128)}, u32[]{:S(2)}) copy-start(f32[32,4096]{1,0:T(8,128)} %param.47) | copy-start | bytes 1572868
  551.9 11.7 %copy-start.27 = (f32[32,4096]{1,0:T(8,128)S(1)}, f32[32,4096]{1,0:T(8,128)}, u32[]{:S(2)}) copy-start(f32[32,4096]{1,0:T(8,128)} %param.48) | copy-start | bytes 1572868
  556.8 8.3 %copy-start.21 = (f32[32,1024]{1,0:T(8,128)S(1)}, f32[32,1024]{1,0:T(8,128)}, u32[]{:S(2)}) copy-start(f32[32,1024]{1,0:T(8,128)} %param.43) | copy-start | bytes 393220
  558.5 6.6 %copy-start.36 = (f32[32,1024]{1,0:T(8,128)S(1)}, f32[32,1024]{1,0:T(8,128)}, u32[]{:S(2)}) copy-start(f32[32,1024]{1,0:T(8,128)} %param.44) | copy-start | bytes 393220
  (33 other events, 126.4 us)

commit v3 on v2

--- a/solution.py
+++ b/solution.py
@@ -25,6 +25,7 @@
 DECAY = 0.05
 RATES = (0.05, 0.05, 0.5, 0.05, 0.05, 0.05, 0.8)
 MESH = pl.DeviceIdType.MESH
+WIDE, NARROW = BOTH = ("wide", "narrow")
 HIGHEST = lax.Precision.HIGHEST
 F32 = jnp.float32
 BF16 = jnp.bfloat16
@@ -150,13 +151,18 @@
     return [(which,) + half + (side,) for which in order for side, half in enumerate(column_halves(widths[which]))]
 
 
+class Bag:
+    def __init__(self, pairs):
+        vars(self).update(pairs)
+
+
 class Place:
     def __init__(self, wide, narrow):
         self.wide, self.narrow = wide, narrow
         self.chips = wide // 2
         self.bits = chip_bits(self.chips)
-        self.w = lax.axis_index("wide")
-        self.n = lax.axis_index("narrow")
+        self.w = lax.axis_index(WIDE)
+        self.n = lax.axis_index(NARROW)
         self.chip = self.w // 2
         self.core = self.w % 2
         self.twin = (2 * self.chip + 1 - self.core, self.n)
@@ -199,14 +205,15 @@
 
 
 def forward_kernel(items, wide, narrow, lead, ins, outs, scratch, *refs):
-    at = dict(zip(ins + outs + scratch, refs))
-    buf = {name: at["v_" + name] for name in outs}
-    weights = [at["first_weight"]] + [buf["w%d" % which] for which in range(1, 6)]
-    shards = [at["s%d" % which] for which in range(6)]
-    own_sem, send_sem, recv_sem, swap_send, swap_recv, out_sem = (at[name] for name in SEMS)
+    at = Bag(zip(ins + scratch, refs[: len(ins)] + refs[len(ins) + len(outs) :]))
+    results = refs[len(ins) : len(ins) + len(outs)]
+    weights = [at.first_weight, at.w1, at.w2, at.w3, at.w4, at.w5]
+    shards = [at.s0, at.s1, at.s2, at.s3, at.s4, at.s5]
+    own_sem, send_sem, recv_sem = at.own_sem, at.send_sem, at.recv_sem
+    swap_send, swap_recv, out_sem = at.swap_send, at.swap_recv, at.out_sem
     place = Place(wide, narrow)
     chips, me = place.chips, place.n
-    tokens = at["patches"].shape[0]
+    tokens = at.patches.shape[0]
     head_width = D // narrow
     total = len(items)
     started = []
@@ -332,8 +339,9 @@
 
     flushed = []
 
-    def flush(name):
-        copy = pltpu.make_async_copy(buf[name], at[name], out_sem.at[outs.index(name)])
+    def flush(ref):
+        index = [vars(at)[name] is ref for name in outs].index(True)
+        copy = pltpu.make_async_copy(ref, results[index], out_sem.at[index])
         copy.start()
         flushed.append(copy)
 
@@ -347,10 +355,10 @@
             device_id_type=MESH,
         )
 
-    gains = buf["gains"]
-    embedded, mid, last = buf["embedded"], buf["mid"], buf["last"]
-    normed, hidden, wave = at["normed"], at["hidden"], at["wave"]
-    away, qkv, heads_out, returned = at["away"], buf["qkv"], buf["heads_out"], at["returned"]
+    gains = at.gains
+    embedded, mid, last = at.embedded, at.mid, at.last
+    normed, hidden, wave = at.normed, at.hidden, at.wave
+    away, qkv, heads_out, returned = at.away, at.qkv, at.heads_out, at.returned
 
     need(0)
     width = weights[0].shape[1]
@@ -360,9 +368,9 @@
     gains[...] = back_mul(pick, weights[0][:, width - LANES :])
     for block in range(0, D, 256):
         cols = pl.ds(block, 256)
-        embedded[:, cols] = back_mul(at["patches"][...], weights[0][pl.ds(block, 256), : at["patches"].shape[1]])
-    flush("embedded")
-    flush("gains")
+        embedded[:, cols] = back_mul(at.patches[...], weights[0][pl.ds(block, 256), : at.patches.shape[1]])
+    flush(at.embedded)
+    flush(at.gains)
 
     def norm_rows(source, row, dest):
         step_rows = 64
@@ -393,13 +401,13 @@
         lax.fori_loop(0, 3, project, 0)
         if step:
             start(swap(away.at[step - 1], qkv.at[me], 0, step))
-    flush("w1")
-    buf["t1"][...] = normed[...].T
-    flush("t1")
+    flush(at.w1)
+    at.t1[...] = normed[...].T
+    flush(at.t1)
     advance(2)
     for step in range(1, narrow):
         swap(away.at[step - 1], qkv.at[me], 0, step).wait_recv()
-    flush("qkv")
+    flush(at.qkv)
 
     lane = lax.broadcasted_iota(jnp.int32, (1, LANES), 1)
     scale = HD ** (-0.5)
@@ -426,15 +434,15 @@
                     lane == pair * (LANES // HD) + side, highest + jnp.log(summed), log_sums
                 )
             heads_out[who, :, lanes] = out.astype(BF16)
-        buf["log_sums"][who] = log_sums
+        at.log_sums[who] = log_sums
         if step:
             start(swap(heads_out.at[who], returned.at[me], 1, step))
             if step % 2 == 0:
                 advance()
         else:
             returned[me] = heads_out[who]
-    flush("heads_out")
-    flush("log_sums")
+    flush(at.heads_out)
+    flush(at.log_sums)
     need(2)
     for step in range(1, narrow):
         swap(heads_out.at[me], returned.at[me], 1, step).wait_recv()
@@ -444,18 +452,18 @@
         for source in range(narrow):
             value = value + matmul(returned[source], weights[2][pl.ds(source * head_width, head_width), cols])
         mid[:, cols] = value
-    flush("w2")
-    flush("mid")
+    flush(at.w2)
+    flush(at.mid)
     norm_rows(mid, 1, normed)
     for source in range(narrow):
-        buf["t2"][pl.ds(source * head_width, head_width), :] = returned[source].T
-    buf["t3"][...] = normed[...].T
-    flush("t2")
-    flush("t3")
+        at.t2[pl.ds(source * head_width, head_width), :] = returned[source].T
+    at.t3[...] = normed[...].T
+    flush(at.t2)
+    flush(at.t3)
 
     ff = weights[3].shape[1]
     tile = wave.shape[1]
-    slopes = buf["slopes"]
+    slopes = at.slopes
     for block in range(0, ff, tile):
         need(3, (block, block + tile))
         wave[...] = matmul(normed[...], weights[3][:, pl.ds(block, tile)])
@@ -470,33 +478,30 @@
             return carry
 
         lax.fori_loop(0, tokens // 16, bend, 0)
-        buf["t4"][pl.ds(block, tile), :] = hidden[:, pl.ds(block, tile)].T
-    flush("w3")
-    flush("slopes")
-    flush("t4")
+        at.t4[pl.ds(block, tile), :] = hidden[:, pl.ds(block, tile)].T
+    flush(at.w3)
+    flush(at.slopes)
+    flush(at.t4)
     for block in range(0, D, 256):
         need(4, (block, block + 256))
         cols = pl.ds(block, 256)
         last[:, cols] = mid[:, cols] + matmul(hidden[...], weights[4][:, cols])
-    flush("w4")
-    flush("last")
+    flush(at.w4)
+    flush(at.last)
     norm_rows(last, 2, normed)
     need(5)
     for block in range(0, weights[5].shape[1], 256):
         cols = pl.ds(block, 256)
-        buf["gaussians"][:, cols] = matmul(normed[...], weights[5][:, cols])
-    flush("w5")
-    flush("gaussians")
-    buf["t5"][...] = normed[...].T
-    flush("t5")
+        at.gaussians[:, cols] = matmul(normed[...], weights[5][:, cols])
+    flush(at.w5)
+    flush(at.gaussians)
+    at.t5[...] = normed[...].T
+    flush(at.t5)
     advance(total)
     for copy in started:
         copy.wait_send()
     for copy in flushed:
         copy.wait()
-
-
-SEMS = ("own_sem", "send_sem", "recv_sem", "swap_send", "swap_recv", "out_sem")
 
 
 def forward_all(shards, patches, lead, wide, narrow):
@@ -507,8 +512,13 @@
     head_width = D // narrow
     items = forward_plan(widths)
     slots = wide + narrow - 1
-    shapes = {"w%d" % which: ((heights[which], widths[which]), BF16) for which in range(1, 6)}
-    shapes.update(
+    full = [((height, width), BF16) for height, width in zip(heights, widths)]
+    shapes = dict(
+        w1=full[1],
+        w2=full[2],
+        w3=full[3],
+        w4=full[4],
+        w5=full[5],
         gains=((8, D), F32),
         embedded=((tokens, D), F32),
         mid=((tokens, D), F32),
@@ -524,7 +534,7 @@
         log_sums=((narrow, tokens, LANES), F32),
         gaussians=((tokens, widths[5]), F32),
     )
-    ins = tuple("s%d" % which for which in range(6)) + ("patches",)
+    ins = tuple(dict(s0=0, s1=0, s2=0, s3=0, s4=0, s5=0, patches=0))
     outs = tuple(shapes)
     extras = dict(
         first_weight=pltpu.VMEM((heights[0], widths[0]), BF16),
@@ -540,7 +550,7 @@
         swap_recv=pltpu.SemaphoreType.DMA((2, narrow)),
         out_sem=pltpu.SemaphoreType.DMA((len(outs),)),
     )
-    scratch = tuple("v_" + name for name in outs) + tuple(extras)
+    scratch = outs + tuple(extras)
     anywhere = pl.BlockSpec(memory_space=pl.ANY)
     results = pl.pallas_call(
         functools.partial(forward_kernel, items, wide, narrow, lead, ins, outs, scratch),
@@ -553,7 +563,17 @@
         ),
         name="forward",
     )(*shards, patches)
-    return dict(zip(outs, results))
+    return Bag(zip(outs, results))
+
+
+def backward_plan(widths):
+    items = []
+    for which, cuts in ((5, 1), (4, 2), (3, 2), (2, 1), (1, 3), (0, 1)):
+        size = widths[which] // cuts
+        for cut in range(cuts):
+            for side, (start, width) in enumerate(column_halves(size)):
+                items.append((which, cut * size + start, width, side))
+    return items
 
 
 def tile_of(width):
@@ -563,32 +583,76 @@
     return width
 
 
-def reduce_kernel(items, wide, narrow, count, *refs):
-    lefts, rights = refs[:count], refs[count : 2 * count]
-    extra, term = refs[2 * count : 2 * count + 2]
-    outs = refs[2 * count + 2 : 3 * count + 2]
-    sums = refs[3 * count + 2]
-    scratch = list(refs[3 * count + 3 :])
+def backward_kernel(items, wide, narrow, lead, ins, scratch, *refs):
+    src = Bag(zip(ins, refs))
+    refs = refs[len(ins) :]
+    sums, totals, refs = refs[:6], refs[6], list(refs[7:])
+    at = Bag(zip(scratch, refs))
     place = Place(wide, narrow)
-    chips = place.chips
+    chips, me = place.chips, place.n
     total = len(items)
-    sent = [scratch.pop(0) for _ in items]
-    held = [scratch.pop(0) for _ in items]
-    passed = [[scratch.pop(0) for _ in place.bits] for _ in items]
-    last = [scratch.pop(0) for _ in items]
-    wide_tiles, narrow_tiles, send_sem, recv_sem, tile_send, tile_recv = scratch
-    peers = [place.twin]
-    for step in range(1, wide):
-        peers.append((lax.rem(place.w + step, wide), place.n))
-    for step in range(1, narrow):
-        peers.append(place.along(step))
-    greet(peers[1:])
+    refs = refs[len(scratch) :]
+    held = [refs.pop(0) for _ in items]
+    passed = [[refs.pop(0) for _ in place.bits] for _ in items]
+    final = [refs.pop(0) for _ in items]
+    spare = [refs.pop(0) for _ in range(6)]
+    tokens = src.patches.shape[0]
+    head_width = D // narrow
+    length = narrow * tokens
+    send_sem, recv_sem, tile_send, tile_recv = at.send_sem, at.recv_sem, at.tile_send, at.tile_recv
+    swap_send, swap_recv, in_sem, ring_sem = at.swap_send, at.swap_recv, at.in_sem, at.ring_sem
+    gains, norms, extra = src.gains, at.norms, at.extra
+    stash, d_res, d_norm = at.stash, at.d_res, at.d_norm
+    mixed, merge_low, expand_low, shrink_low = at.mixed, at.merge_low, at.expand_low, at.shrink_low
+
+    loaded = [name for name in ins if name in scratch]
+
+    def load(ref):
+        index = [vars(at)[name] is ref for name in loaded].index(True)
+        return pltpu.make_async_copy(vars(src)[loaded[index]], ref, in_sem.at[index])
+
+    def load_stash(ref):
+        return pltpu.make_async_copy(ref, stash, in_sem.at[len(loaded)])
+
+    def ring(ref, slots, rows, columns, index, row):
+        slot = lax.rem(index, 2)
+        return pltpu.make_async_copy(
+            ref.at[pl.ds(pl.multiple_of(row, rows), rows), :],
+            slots.at[slot, pl.ds(0, rows), pl.ds(0, columns)],
+            ring_sem.at[0 if slots is at.tall else 1, slot],
+        )
+
+    slope_rows = at.tall.shape[1]
+
+    def slope_load(index):
+        slot = lax.rem(index, 2)
+        return pltpu.make_async_copy(
+            src.slopes.at[:, pl.ds(pl.multiple_of(index * slope_rows, slope_rows), slope_rows)],
+            at.slope_slots.at[slot],
+            ring_sem.at[2, slot],
+        )
+
+    u_rows, u_cols = 256, src.w5.shape[1]
+    load_stash(src.last).start()
+    for index in range(2):
+        ring(src.w5, at.tall, u_rows, u_cols, index, index * u_rows).start()
+        slope_load(index).start()
+        ring(src.w3, at.long, 128, src.w3.shape[1], index, index * 128).start()
+    for name in loaded:
+        load(vars(at)[name]).start()
+
+    peers = [(lax.rem(place.w + step, wide), place.n) for step in range(1, wide)]
+    peers += [place.along(step) for step in range(1, narrow)]
+    greet(peers)
 
     started = []
 
     def start(copy):
         copy.start()
         started.append(copy)
+
+    lefts = [at.embed_t, at.t1, at.t2, at.t3, at.t4, at.t5]
+    rights = [src.patches, mixed, merge_low, expand_low, shrink_low, src.gauss]
 
     def remote(item, src, dst, slot, peer):
         return pltpu.make_async_remote_copy(
@@ -606,34 +670,57 @@
     def product(item, mask, core, into, plus):
         which, begin, width, _ = items[item]
         left, right = lefts[which], rights[which]
-        rows = into.shape[2]
+        rows = into.shape[-2]
         tile = tile_of(width)
         together = max(1, min(narrow, 128 // rows))
-        owner = flip(place.chip, mask)
+        first = ((flip(place.chip, mask) * 2 + core) * narrow) * rows
         with_extra = which == 0 and begin + width == right.shape[1]
+        assert not with_extra or tile == width
+        part, begin = (begin // D, begin % D) if which == 1 else (None, begin)
 
         def one(step, carry):
             across, down = step % (width // tile), step // (width // tile)
             offset = pl.multiple_of(begin + across * tile, LANES)
             local = pl.multiple_of(across * tile, LANES)
             ns = pl.ds(down * together, together)
-            lhs = left[owner, core, ns].reshape(together * rows, left.shape[-1])
-            value = jnp.dot(lhs, right[:, pl.ds(offset, tile)], preferred_element_type=F32)
+            span = together * rows
+            where = pl.ds(pl.multiple_of(first + down * span, span), span)
+            if part is None:
+                rhs = right[:, pl.ds(offset, tile)]
+            else:
+                rhs = right[part, :, pl.ds(offset, tile)]
+            value = jnp.dot(left[where, :], rhs, preferred_element_type=F32)
             if with_extra:
-                more = extra[owner, core, ns].reshape(together * rows, LANES)
-                more = jnp.concatenate([jnp.zeros((together * rows, tile - LANES), F32), more], 1)
+                more = jnp.concatenate([jnp.zeros((span, tile - LANES), F32), extra[where, :]], 1)
                 value = value + more
             value = value.reshape(together, rows, tile)
-            if plus is not None:
-                value = value + plus[mask, ns, :, pl.ds(local, tile)].astype(F32)
+            if plus:
+                value = value + into[mask, ns, :, pl.ds(local, tile)].astype(F32)
             into[mask, ns, :, pl.ds(local, tile)] = value.astype(BF16)
             return carry
 
-        assert not with_extra or tile == width
         lax.fori_loop(0, (width // tile) * (narrow // together), one, 0)
 
+    last_sent = {}
+    pushed = set()
+
     def to_twin(item, mask):
-        return remote(item, sent[item].at[mask], held[item].at[mask], mask, place.twin)
+        which, _, width, _ = items[item]
+        own = spare[which].at[mask, :, :, pl.ds(0, width)]
+        return remote(item, own, held[item].at[mask], mask, place.twin)
+
+    def push(which, part=None):
+        for item, (owner, begin, _, _) in enumerate(items):
+            if owner != which or (part is not None and begin // D != part):
+                continue
+            for mask in range(chips):
+                if (which, mask) in last_sent:
+                    last_sent[which, mask].wait_send()
+                product(item, mask, 1 - place.core, spare[which], False)
+                copy = to_twin(item, mask)
+                copy.start()
+                last_sent[which, mask] = copy
+            pushed.add(item)
 
     def across(item, mask, bit, number, slot):
         return remote(
@@ -645,7 +732,7 @@
         return remote(
             item,
             held[item].at[0, target[1]],
-            last[item].at[narrow - step - 1],
+            final[item].at[narrow - step - 1],
             2 * chips + narrow - step - 1,
             target,
         )
@@ -660,17 +747,31 @@
         return [], keep
 
     def add_into(dest, dest_at, src, src_at):
-        rows, width = dest.shape[-2:]
-
         def one(step, carry):
-            a = dest[dest_at, step].astype(F32) + src[src_at, step].astype(F32)
-            dest[dest_at, step] = a.astype(BF16)
+            value = dest[dest_at, step].astype(F32) + src[src_at, step].astype(F32)
+            dest[dest_at, step] = value.astype(BF16)
             return carry
 
         lax.fori_loop(0, narrow, one, 0)
 
-    def send_on(item, number, ready):
+    def stage(item, number):
+        assert item in pushed
         bits = bits_of(item)
+        if number == 0:
+
+            def ready(mask):
+                to_twin(item, mask).wait_recv()
+                product(item, mask, place.core, held[item], True)
+
+        else:
+            bit = bits[number - 1]
+            _, kept = split(item, number - 1)
+
+            def ready(mask):
+                slot = kept.index(mask)
+                across(item, mask ^ bit, bit, number - 1, slot).wait_recv()
+                add_into(held[item], mask, passed[item][number - 1], slot)
+
         away, keep = split(item, number)
         if number < len(bits):
             for mask in away:
@@ -683,58 +784,268 @@
             for step in range(1, narrow):
                 start(along(item, step))
 
-    def stage(item, number):
-        bits = bits_of(item)
-        if number == 0:
-
-            def ready(mask):
-                to_twin(item, mask).wait_recv()
-                product(item, mask, place.core, held[item], held[item])
-
-            send_on(item, 0, ready)
-        else:
-            bit = bits[number - 1]
-            _, kept = split(item, number - 1)
-
-            def ready(mask):
-                slot = kept.index(mask)
-                across(item, mask ^ bit, bit, number - 1, slot).wait_recv()
-                add_into(held[item], mask, passed[item][number - 1], slot)
-
-            send_on(item, number, ready)
+    squares = []
 
     def finish(item):
         which, begin, width, _ = items[item]
-        value = held[item][0, place.n].astype(F32)
+        value = held[item][0, me].astype(F32)
         for step in range(1, narrow):
             along(item, step).wait_recv()
         for slot in range(narrow - 1):
-            value = value + last[item][slot].astype(F32)
-        outs[which][:, pl.ds(begin, width)] = value
-        return jnp.sum(value * value)
-
-    for item in range(total):
-        for mask in range(chips):
-            product(item, mask, 1 - place.core, sent[item], None)
-            start(to_twin(item, mask))
-    squares = jnp.zeros((), F32)
+            value = value + final[item][slot].astype(F32)
+        sums[which][:, pl.ds(begin, width)] = value
+        squares.append(jnp.sum(value * value))
+
+    progress = [0] * (total // 2)
     depth = len(place.bits) + 1
-    for tick in range(0, total + 2 * depth, 2):
-        for number in reversed(range(depth + 1)):
-            for item in (tick - 2 * number, tick - 2 * number + 1):
-                if 0 <= item < total:
+
+    def advance(steps=1):
+        for _ in range(steps):
+            entered = False
+            for pair in range(total // 2):
+                number = progress[pair]
+                if number > depth or (number == 0 and (entered or 2 * pair not in pushed)):
+                    continue
+                entered = entered or number == 0
+                progress[pair] = number + 1
+                for item in (2 * pair, 2 * pair + 1):
                     if number < depth:
                         stage(item, number)
                     else:
-                        squares = squares + finish(item)
+                        finish(item)
+
+    norms[...] = jnp.zeros_like(norms)
+
+    def norm_back(row, low, add):
+        step_rows = 64
+
+        def one(step, carry):
+            rows = pl.ds(pl.multiple_of(step * step_rows, step_rows), step_rows)
+            values = stash[rows, :]
+            upper = d_norm[rows, :]
+            centred = values - jnp.mean(values, -1, keepdims=True)
+            rate = lax.rsqrt(jnp.mean(centred * centred, -1, keepdims=True) + 1e-05)
+            unit = centred * rate
+            norms[row : row + 1, :] += jnp.sum(upper * unit, 0, keepdims=True)
+            norms[row + 3 : row + 4, :] += jnp.sum(upper, 0, keepdims=True)
+            scaled = upper * gains[row : row + 1, :]
+            inner = scaled - jnp.mean(scaled, -1, keepdims=True)
+            inner = rate * (inner - unit * jnp.mean(scaled * unit, -1, keepdims=True))
+            if add:
+                inner = inner + d_res[rows, :]
+            d_res[rows, :] = inner
+            low[rows, :] = inner.astype(BF16)
+            return carry
+
+        lax.fori_loop(0, tokens // step_rows, one, 0)
+
+    load(at.t5).wait()
+    push(5)
+    load_stash(src.last).wait()
+    count = D // u_rows
+    tall_rows = slope_rows
+
+    def through_unpatch(index, carry):
+        ring(src.w5, at.tall, u_rows, u_cols, index, index * u_rows).wait()
+        slot = at.tall.at[lax.rem(index, 2)]
+        offset = pl.multiple_of(index * u_rows, u_rows)
+        d_norm[:, pl.ds(offset, u_rows)] = back_mul(src.gauss[...], slot[0:u_rows, 0:u_cols])
+
+        @pl.when(index + 2 < count)
+        def _():
+            ring(src.w5, at.tall, u_rows, u_cols, index + 2, (index + 2) * u_rows).start()
+
+        return carry
+
+    lax.fori_loop(0, count, through_unpatch, 0)
+    for index in range(2):
+        ring(src.w4, at.tall, tall_rows, D, index, index * tall_rows).start()
+    norm_back(2, shrink_low, False)
+    load_stash(src.mid).start()
+    load(at.t4).wait()
+    push(4)
+    advance()
+    ff = src.w3.shape[1]
+    slabs = ff // tall_rows
+
+    def through_shrink(index, carry):
+        ring(src.w4, at.tall, tall_rows, D, index, index * tall_rows).wait()
+        slope_load(index).wait()
+        slot = lax.rem(index, 2)
+        value = back_mul(shrink_low[...], at.tall[slot])
+        value = value * at.slope_slots[slot].astype(F32)
+        expand_low[:, pl.ds(pl.multiple_of(index * tall_rows, tall_rows), tall_rows)] = value.astype(BF16)
+
+        @pl.when(index + 2 < slabs)
+        def _():
+            ring(src.w4, at.tall, tall_rows, D, index + 2, (index + 2) * tall_rows).start()
+            slope_load(index + 2).start()
+
+        return carry
+
+    lax.fori_loop(0, slabs, through_shrink, 0)
+    owners = [lax.rem(me + step, narrow) for step in list(range(1, narrow)) + [0]]
+    for index in range(2):
+        ring(src.w2, at.tall, head_width, D, index, owners[index] * head_width).start()
+    load(at.t3).wait()
+    push(3)
+    advance()
+
+    def through_expand(index, carry):
+        ring(src.w3, at.long, 128, ff, index, index * 128).wait()
+        offset = pl.multiple_of(index * 128, 128)
+        d_norm[:, pl.ds(offset, 128)] = back_mul(expand_low[...], at.long[lax.rem(index, 2)])
+
+        @pl.when(index + 2 < D // 128)
+        def _():
+            ring(src.w3, at.long, 128, ff, index + 2, (index + 2) * 128).start()
+
+        return carry
+
+    lax.fori_loop(0, D // 128, through_expand, 0)
+    for index in range(2):
+        ring(src.w1, at.long, 128, 3 * D, index, index * 128).start()
+    load_stash(src.mid).wait()
+    norm_back(1, merge_low, True)
+    load_stash(src.embedded).start()
+
+    def swap(src, dst, kind, step):
+        return pltpu.make_async_remote_copy(
+            src_ref=src,
+            dst_ref=dst,
+            send_sem=swap_send.at[kind, step],
+            recv_sem=swap_recv.at[kind, step],
+            device_id=place.along(step),
+            device_id_type=MESH,
+        )
+
+    d_heads, away = at.d_heads, at.away
+    for index, owner in enumerate(owners):
+        ring(src.w2, at.tall, head_width, D, index, owner * head_width).wait()
+        value = back_mul(merge_low[...], at.tall[index % 2, 0:head_width, :]).astype(BF16)
+        if index < narrow - 1:
+            away[index] = value
+            start(swap(away.at[index], d_heads.at[me], 0, index + 1))
+        else:
+            d_heads[me] = value
+        if index + 2 < narrow:
+            ring(src.w2, at.tall, head_width, D, index + 2, owners[index + 2] * head_width).start()
+    load(at.t2).wait()
+    push(2)
+    advance()
+    load(at.qkv).wait()
+    load(at.heads_out).wait()
+    load(at.log_sums).wait()
+    for step in range(1, narrow):
+        swap(away.at[step - 1], d_heads.at[me], 0, step).wait_recv()
+
+    qkv, heads_out, log_sums, parts = at.qkv, at.heads_out, at.log_sums, at.parts
+    key_t, key_acc, value_acc, query_acc = at.key_t, at.key_acc, at.value_acc, at.query_acc
+    lane = lax.broadcasted_iota(jnp.int32, (1, LANES), 1)
+    line = lax.broadcasted_iota(jnp.int32, (LANES, 1), 0)
+    sides = LANES // HD
+    scale = HD ** (-0.5)
+    choose = lax.broadcasted_iota(jnp.int32, (8, LANES), 1) // HD
+    choose = (choose == lax.broadcasted_iota(jnp.int32, (8, LANES), 0)).astype(F32)
+
+    def part_swap(pair, step):
+        lanes = pl.ds(pair * LANES, LANES)
+        who = lax.rem(me + step, narrow)
+        return swap(
+            parts.at[who, :, :, lanes],
+            mixed.at[:, :, pl.ds(pl.multiple_of(me * head_width + pair * LANES, LANES), LANES)],
+            1 + pair,
+            step,
+        )
+
+    for pair in range(head_width // LANES):
+        lanes = pl.ds(pair * LANES, LANES)
+        key_t[...] = qkv[:, 1, :, lanes].reshape(length, LANES).T
+        key_acc[...] = jnp.zeros_like(key_acc)
+        value_acc[...] = jnp.zeros_like(value_acc)
+        for step in range(narrow):
+            who = lax.rem(me + step, narrow)
+            query = qkv[who, 0, :, lanes].astype(F32)
+            upper = d_heads[who, :, lanes].astype(F32)
+            kept = heads_out[who, :, lanes].astype(F32)
+            delta = lax.dot_general(
+                choose,
+                upper * kept,
+                (((1,), (1,)), ((), ())),
+                precision=HIGHEST,
+                preferred_element_type=F32,
+            )
+            log_rows = log_sums[who].T[pair * sides : (pair + 1) * sides, :]
+            own_query = [(query * jnp.where(lane // HD == side, scale, 0.0)).astype(BF16) for side in range(sides)]
+            own_upper = [(upper * jnp.where(lane // HD == side, 1.0, 0.0)).astype(BF16) for side in range(sides)]
+            query_acc[...] = jnp.zeros_like(query_acc)
+
+            def block(source, carry):
+                rows = pl.ds(pl.multiple_of(source * tokens, tokens), tokens)
+                key, value = qkv[source, 1, :, lanes], qkv[source, 2, :, lanes]
+                key_turned = key_t[:, rows].astype(F32)
+                for side in range(sides):
+                    scores = back_mul(key, own_query[side])
+                    probs = jnp.exp(scores - log_rows[side : side + 1, :])
+                    d_probs = back_mul(value, own_upper[side])
+                    d_scores = (probs * (d_probs - delta[side : side + 1, :])).astype(BF16)
+                    value_acc[rows, :] += matmul(probs.astype(BF16), own_upper[side])
+                    key_acc[rows, :] += matmul(d_scores, own_query[side])
+                    turned = (key_turned * jnp.where(line // HD == side, scale, 0.0)).astype(BF16)
+                    query_acc[...] += matmul(turned, d_scores)
+                return carry
+
+            lax.fori_loop(0, narrow, block, 0)
+            parts[who, 0, :, lanes] = query_acc[...].T.astype(BF16)
+            if step % 2 == 1:
+                advance()
+        for source in range(narrow):
+            rows = pl.ds(source * tokens, tokens)
+            parts[source, 1, :, lanes] = key_acc[rows, :].astype(BF16)
+            parts[source, 2, :, lanes] = value_acc[rows, :].astype(BF16)
+        for step in range(1, narrow):
+            start(part_swap(pair, step))
+        mixed[:, :, pl.ds(pl.multiple_of(me * head_width + pair * LANES, LANES), LANES)] = parts[me, :, :, lanes]
+    load(at.t1).wait()
+    for pair in range(head_width // LANES):
+        for step in range(1, narrow):
+            part_swap(pair, step).wait_recv()
+    for part in range(3):
+        push(1, part)
+        advance()
+
+    def through_mixer(index, carry):
+        ring(src.w1, at.long, 128, 3 * D, index, index * 128).wait()
+        slot = lax.rem(index, 2)
+        value = back_mul(mixed[0], at.long[slot, :, 0:D])
+        for part in range(1, 3):
+            value = value + back_mul(mixed[part], at.long[slot, :, part * D : (part + 1) * D])
+        d_norm[:, pl.ds(pl.multiple_of(index * 128, 128), 128)] = value
+
+        @pl.when(index + 2 < D // 128)
+        def _():
+            ring(src.w1, at.long, 128, 3 * D, index + 2, (index + 2) * 128).start()
+
+        return carry
+
+    lax.fori_loop(0, D // 128, through_mixer, 0)
+    load_stash(src.embedded).wait()
+    norm_back(0, at.embed_low, True)
+    at.embed_t[...] = at.embed_low[...].T
+    turned = jnp.concatenate([norms[...], jnp.zeros((LANES - 8, D), F32)], 0).T
+    at.extra[...] = pltpu.roll(turned, lead, 1)
+    push(0)
+    advance(total)
+    assert min(progress) > depth
 
     rows = lax.broadcasted_iota(jnp.int32, (8, LANES), 0)
-    wide_tiles[place.w] = jnp.where(rows == 0, term[...], squares)
-
-    def tile_copy(buffer, at, slot, peer):
+    wide_tiles, narrow_tiles = at.wide_tiles, at.narrow_tiles
+    wide_tiles[place.w] = jnp.where(rows == 0, src.term[...], sum(squares))
+
+    def tile_copy(buffer, index, slot, peer):
         return pltpu.make_async_remote_copy(
-            src_ref=buffer.at[at],
-            dst_ref=buffer.at[at],
+            src_ref=buffer.at[index],
+            dst_ref=buffer.at[index],
             send_sem=tile_send.at[slot],
             recv_sem=tile_recv.at[slot],
             device_id=peer,
@@ -756,53 +1067,85 @@
     whole = narrow_tiles[0]
     for index in range(1, narrow):
         whole = whole + narrow_tiles[index]
-    sums[...] = whole
-    for copy in started:
+    totals[...] = whole
+    for copy in list(last_sent.values()) + started:
         copy.wait_send()
 
 
-def reduce_all(lefts, rights, extra, term, wide, narrow, order):
-    count = len(lefts)
+def backward_all(kept, patches, gauss, term, lead, wide, narrow):
+    tokens = patches.shape[0]
     chips = wide // 2
-    shaped = [left.reshape(chips, 2, narrow, -1, left.shape[1]) for left in lefts]
-    extra = extra.reshape(chips, 2, narrow, -1, LANES)
-    widths = [right.shape[1] for right in rights]
-    rows = [left.shape[3] for left in shaped]
-    items = work_items(widths, order)
+    weights = [kept.w1, kept.w2, kept.w3, kept.w4, kept.w5]
+    heights = [D] + [weight.shape[0] for weight in weights]
+    widths = [patches.shape[1]] + [weight.shape[1] for weight in weights]
+    rows = [height // (wide * narrow) for height in heights]
+    head_width = D // narrow
+    length = narrow * tokens
+    items = backward_plan(widths)
     slots = 2 * chips + narrow - 1
-    scratch = []
+    streamed = dict(w1=kept.w1, w2=kept.w2, w3=kept.w3, w4=kept.w4, w5=kept.w5)
+    streamed.update(last=kept.last, mid=kept.mid, embedded=kept.embedded, slopes=kept.slopes)
+    loaded = dict(t5=kept.t5, t4=kept.t4, t3=kept.t3, t2=kept.t2, t1=kept.t1)
+    loaded.update(qkv=kept.qkv, heads_out=kept.heads_out, log_sums=kept.log_sums)
+    whole = dict(gains=kept.gains, patches=patches, gauss=gauss, term=term)
+    operands = {**streamed, **loaded, **whole}
+    shapes = [jax.ShapeDtypeStruct((rows[which], widths[which]), F32) for which in range(6)]
+    shapes.append(jax.ShapeDtypeStruct((8, LANES), F32))
+    scratch = {name: pltpu.VMEM(value.shape, value.dtype) for name, value in loaded.items()}
+    scratch.update(
+        embed_t=pltpu.VMEM((D, tokens), BF16),
+        embed_low=pltpu.VMEM((tokens, D), BF16),
+        stash=pltpu.VMEM((tokens, D), F32),
+        d_res=pltpu.VMEM((tokens, D), F32),
+        d_norm=pltpu.VMEM((tokens, D), F32),
+        norms=pltpu.VMEM((8, D), F32),
+        extra=pltpu.VMEM((D, LANES), F32),
+        shrink_low=pltpu.VMEM((tokens, D), BF16),
+        expand_low=pltpu.VMEM((tokens, widths[3]), BF16),
+        merge_low=pltpu.VMEM((tokens, D), BF16),
+        mixed=pltpu.VMEM((3, tokens, D), BF16),
+        tall=pltpu.VMEM((2, 512, D), BF16),
+        long=pltpu.VMEM((2, 128, widths[3]), BF16),
+        slope_slots=pltpu.VMEM((2, tokens, 512), BF16),
+        d_heads=pltpu.VMEM((narrow, tokens, head_width), BF16),
+        away=pltpu.VMEM((narrow - 1, tokens, head_width), BF16),
+        parts=pltpu.VMEM((narrow, 3, tokens, head_width), BF16),
+        key_t=pltpu.VMEM((LANES, length), BF16),
+        key_acc=pltpu.VMEM((length, LANES), F32),
+        value_acc=pltpu.VMEM((length, LANES), F32),
+        query_acc=pltpu.VMEM((LANES, tokens), F32),
+        wide_tiles=pltpu.VMEM((wide, 8, LANES), F32),
+        narrow_tiles=pltpu.VMEM((narrow, 8, LANES), F32),
+        send_sem=pltpu.SemaphoreType.DMA((len(items), slots)),
+        recv_sem=pltpu.SemaphoreType.DMA((len(items), slots)),
+        tile_send=pltpu.SemaphoreType.DMA((wide + narrow,)),
+        tile_recv=pltpu.SemaphoreType.DMA((wide + narrow,)),
+        swap_send=pltpu.SemaphoreType.DMA((1 + head_width // LANES, narrow)),
+        swap_recv=pltpu.SemaphoreType.DMA((1 + head_width // LANES, narrow)),
+        in_sem=pltpu.SemaphoreType.DMA((9,)),
+        ring_sem=pltpu.SemaphoreType.DMA((3, 2)),
+    )
+    lists = [pltpu.VMEM((chips, narrow, rows[which], width), BF16) for which, _, width, _ in items]
     for which, _, width, _ in items:
-        scratch.append(pltpu.VMEM((chips, narrow, rows[which], width), BF16))
-    for which, _, width, _ in items:
-        scratch.append(pltpu.VMEM((chips, narrow, rows[which], width), BF16))
-    for which, _, width, _ in items:
-        size = chips
-        while size > 1:
-            size //= 2
-            scratch.append(pltpu.VMEM((size, narrow, rows[which], width), BF16))
-    for which, _, width, _ in items:
-        scratch.append(pltpu.VMEM((narrow - 1, rows[which], width), BF16))
-    scratch += [
-        pltpu.VMEM((wide, 8, LANES), F32),
-        pltpu.VMEM((narrow, 8, LANES), F32),
-        pltpu.SemaphoreType.DMA((len(items), slots)),
-        pltpu.SemaphoreType.DMA((len(items), slots)),
-        pltpu.SemaphoreType.DMA((wide + narrow,)),
-        pltpu.SemaphoreType.DMA((wide + narrow,)),
-    ]
+        for bit in chip_bits(chips):
+            lists.append(pltpu.VMEM((chips // (2 * bit), narrow, rows[which], width), BF16))
+    lists += [pltpu.VMEM((narrow - 1, rows[which], width), BF16) for which, _, width, _ in items]
+    for which in range(6):
+        widest = max(width for owner, _, width, _ in items if owner == which)
+        lists.append(pltpu.VMEM((chips, narrow, rows[which], widest), BF16))
     vmem = pl.BlockSpec(memory_space=pltpu.VMEM)
+    hbm = pl.BlockSpec(memory_space=pl.ANY)
     return pl.pallas_call(
-        functools.partial(reduce_kernel, items, wide, narrow, count),
-        out_shape=[jax.ShapeDtypeStruct((rows[i], widths[i]), F32) for i in range(count)]
-        + [jax.ShapeDtypeStruct((8, LANES), F32)],
-        in_specs=[vmem] * (2 * count + 2),
-        out_specs=[vmem] * (count + 1),
-        scratch_shapes=scratch,
+        functools.partial(backward_kernel, items, wide, narrow, lead, tuple(operands), tuple(scratch)),
+        out_shape=shapes,
+        in_specs=[vmem if name in whole else hbm for name in operands],
+        out_specs=[vmem] * len(shapes),
+        scratch_shapes=list(scratch.values()) + lists,
         compiler_params=pltpu.CompilerParams(
-            collective_id=1, has_side_effects=True, vmem_limit_bytes=60 * MIB
+            collective_id=1, has_side_effects=True, vmem_limit_bytes=63 * MIB
         ),
-        name="reduce_grads",
-    )(*shaped, *rights, extra, term)
+        name="backward",
+    )(*operands.values())
 
 
 def render_kernel(
@@ -929,15 +1272,15 @@
 
 
 def forward_plain(shards, patches, features, kinds):
-    weights = [lax.all_gather(shard, ("wide", "narrow"), axis=0, tiled=True) for shard in shards]
-    groups = lax.axis_size("narrow")
+    weights = [lax.all_gather(shard, BOTH, axis=0, tiled=True) for shard in shards]
+    groups = lax.axis_size(NARROW)
     rows = patches.shape[0]
     gains = weights[0][:, features : features + kinds].T.astype(F32)
     embedded = back_mul(patches[:, :features], weights[0][:, :features])
     normed_one = layer_norm(embedded, gains[0], gains[3]).astype(BF16)
     mixed = matmul(normed_one, weights[1]).astype(BF16).reshape(rows, 3, groups, -1)
     mixed = mixed.transpose(2, 1, 0, 3)
-    qkv = lax.all_to_all(mixed, "narrow", split_axis=0, concat_axis=0, tiled=True)
+    qkv = lax.all_to_all(mixed, NARROW, split_axis=0, concat_axis=0, tiled=True)
     width = qkv.shape[-1]
     length = groups * rows
     heads = width // HD
@@ -945,7 +1288,7 @@
     attended, logsum = attention_forward(*parts)
     log_sums = logsum.transpose(0, 2, 1).reshape(groups, rows, heads)
     returned = lax.all_to_all(
-        attended.reshape(groups, rows, width), "narrow", split_axis=0, concat_axis=0, tiled=True
+        attended.reshape(groups, rows, width), NARROW, split_axis=0, concat_axis=0, tiled=True
     )
     returned = returned.transpose(1, 0, 2).reshape(rows, D)
     mid = embedded + matmul(returned, weights[2])
@@ -957,8 +1300,13 @@
     slopes = (half + expanded * bell).astype(BF16)
     last = mid + matmul(activated, weights[4])
     normed_three = layer_norm(last, gains[2], gains[5]).astype(BF16)
-    kept = {"w%d" % which: weights[which] for which in range(1, 6)}
-    kept.update(
+    return Bag(
+        dict(
+        w1=weights[1],
+        w2=weights[2],
+        w3=weights[3],
+        w4=weights[4],
+        w5=weights[5],
         gains=gains,
         embedded=embedded,
         mid=mid,
@@ -973,8 +1321,52 @@
         heads_out=attended,
         log_sums=log_sums,
         gaussians=matmul(normed_three, weights[5]),
-    )
-    return kept
+    ).items())
+
+
+def backward_plain(kept, patches, gauss_low, term, features, kinds):
+    gains = kept.gains
+    weights = [None, kept.w1, kept.w2, kept.w3, kept.w4, kept.w5]
+    norm_back_one = jax.vjp(layer_norm, kept.embedded, gains[0], gains[3])[1]
+    norm_back_two = jax.vjp(layer_norm, kept.mid, gains[1], gains[4])[1]
+    norm_back_three = jax.vjp(layer_norm, kept.last, gains[2], gains[5])[1]
+    qkv = kept.qkv
+    groups, _, rows, width = qkv.shape
+    length = groups * rows
+    heads = width // HD
+    queries, keys, values = (qkv[:, part].reshape(length, heads, HD) for part in range(3))
+    blocked = min(512, length)
+    logsum = kept.log_sums[:, :, :heads].reshape(length // blocked, blocked, heads)
+    residual_grad, gain_three, shift_three = norm_back_three(back_mul(gauss_low, weights[5]))
+    shrink_low = residual_grad.astype(BF16)
+    expand_low = (back_mul(shrink_low, weights[4]) * kept.slopes.astype(F32)).astype(BF16)
+    through_two, gain_two, shift_two = norm_back_two(back_mul(expand_low, weights[3]))
+    residual_grad = residual_grad + through_two
+    merge_low = residual_grad.astype(BF16)
+    out_grad = back_mul(merge_low, weights[2]).astype(BF16).reshape(rows, groups, width)
+    head_grad = lax.all_to_all(
+        out_grad.transpose(1, 0, 2), NARROW, split_axis=0, concat_axis=0, tiled=True
+    ).reshape(length, heads, HD)
+    grads = attention_backward(queries, keys, values, logsum.transpose(0, 2, 1), head_grad)
+    stacked = jnp.stack(grads, 1).astype(BF16).reshape(groups, rows, 3, width)
+    mixed_grad = lax.all_to_all(stacked, NARROW, split_axis=0, concat_axis=0, tiled=True)
+    mixed_grad = mixed_grad.transpose(1, 2, 0, 3).reshape(rows, 3 * D)
+    through_one, gain_one, shift_one = norm_back_one(back_mul(mixed_grad, weights[1]))
+    embed_grad = (residual_grad + through_one).astype(BF16)
+    grad_norms = jnp.stack([gain_one, gain_two, gain_three, shift_one, shift_two, shift_three])
+    lefts = [embed_grad.T] + [kept.t1, kept.t2, kept.t3, kept.t4, kept.t5]
+    rights = [patches, mixed_grad, merge_low, expand_low, shrink_low, gauss_low]
+    products = [matmul(left, right) for left, right in zip(lefts, rights)]
+    products[0] = products[0].at[:, features : features + kinds].add(grad_norms.T)
+    sums = [
+        lax.psum_scatter(
+            product.astype(BF16), BOTH, scatter_dimension=0, tiled=True
+        ).astype(F32)
+        for product in products
+    ]
+    squares = sum(jnp.sum(part * part) for part in sums)
+    loss_sum, square_sum = lax.psum((term[0, 0], squares), BOTH)
+    return sums, loss_sum, square_sum
 
 
 def body(
@@ -1010,8 +1402,8 @@
     masters = (embed_weight, mixer_weight, merge_weight, expand_weight, shrink_weight, unpatch_weight, norm_params)
     firsts = (embed_first, mixer_first, merge_first, expand_first, shrink_first, unpatch_first, norm_first)
     seconds = (embed_second, mixer_second, merge_second, expand_second, shrink_second, unpatch_second, norm_second)
-    groups = lax.axis_size("narrow")
-    wide_count = lax.axis_size("wide")
+    groups = lax.axis_size(NARROW)
+    wide_count = lax.axis_size(WIDE)
     features = embed_weight.shape[0]
     kinds = norm_params.shape[0]
     padded = -(-(features + kinds) // LANES) * LANES
@@ -1028,66 +1420,17 @@
         kept = forward_all(shards, patches, features % LANES, wide_count, groups)
     else:
         kept = forward_plain(shards, patches, features, kinds)
-    gains = kept["gains"]
-    weights = [None] + [kept["w%d" % which] for which in range(1, 6)]
-    norm_back_one = jax.vjp(layer_norm, kept["embedded"], gains[0], gains[3])[1]
-    norm_back_two = jax.vjp(layer_norm, kept["mid"], gains[1], gains[4])[1]
-    norm_back_three = jax.vjp(layer_norm, kept["last"], gains[2], gains[5])[1]
-    qkv = kept["qkv"]
-    width = qkv.shape[-1]
-    length = groups * rows
-    local_heads = width // HD
-    queries, keys_all, values_all = (
-        qkv[:, part].reshape(length, local_heads, HD) for part in range(3)
+    divisor = pair_total[0].astype(F32)
+    gauss_low, term = render(
+        kept.gaussians, render_w[0], targets[0], pix_mask[0], pairs[0], view_count, pair_total
     )
-    blocked = min(512, length)
-    logsum = kept["log_sums"][:, :, :local_heads].reshape(length // blocked, blocked, local_heads)
-    logsum = logsum.transpose(0, 2, 1)
-    gaussians = kept["gaussians"]
-    divisor = pair_total[0].astype(F32)
-
-    gauss_low, term = render(
-        gaussians, render_w[0], targets[0], pix_mask[0], pairs[0], view_count, pair_total
-    )
-    residual_grad, gain_three, shift_three = norm_back_three(back_mul(gauss_low, weights[5]))
-    shrink_low = residual_grad.astype(BF16)
-    expand_low = (back_mul(shrink_low, weights[4]) * kept["slopes"].astype(F32)).astype(BF16)
-    through_two, gain_two, shift_two = norm_back_two(back_mul(expand_low, weights[3]))
-    residual_grad = residual_grad + through_two
-    merge_low = residual_grad.astype(BF16)
-    out_grad = back_mul(merge_low, weights[2]).astype(BF16).reshape(rows, groups, width)
-    head_grad = lax.all_to_all(out_grad, "narrow", split_axis=1, concat_axis=0, tiled=True).reshape(
-        length, local_heads, HD
-    )
-    query_grad, key_grad, value_grad = attention_backward(queries, keys_all, values_all, logsum, head_grad)
-    stacked = jnp.stack([query_grad, key_grad, value_grad], 1).astype(BF16).reshape(length, 3, 1, width)
-    mixed_grad = lax.all_to_all(stacked, "narrow", split_axis=0, concat_axis=2, tiled=True).reshape(
-        rows, 3 * D
-    )
-    through_one, gain_one, shift_one = norm_back_one(back_mul(mixed_grad, weights[1]))
-    embed_grad = (residual_grad + through_one).astype(BF16)
-    grad_norms = jnp.stack([gain_one, gain_two, gain_three, shift_one, shift_two, shift_three])
-
-    lefts = [embed_grad.T] + [kept["t%d" % which] for which in range(1, 6)]
-    rights = [patches, mixed_grad, merge_low, expand_low, shrink_low, gauss_low]
-    at = features % LANES
-    extra = jnp.pad(grad_norms.T, ((0, 0), (at, LANES - at - kinds)))
     if by_kernel:
-        *sums, totals = reduce_all(
-            lefts, rights, extra, term, wide_count, groups, (5, 4, 3, 2, 1, 0)
+        *sums, totals = backward_all(
+            kept, patches, gauss_low, term, features % LANES, wide_count, groups
         )
         loss_sum, square_sum = totals[0, 0], totals[1, 0]
     else:
-        products = [matmul(left, right) for left, right in zip(lefts, rights)]
-        products[0] = products[0].at[:, -LANES:].add(extra)
-        sums = [
-            lax.psum_scatter(
-                product.astype(BF16), ("wide", "narrow"), scatter_dimension=0, tiled=True
-            ).astype(F32)
-            for product in products
-        ]
-        squares = sum(jnp.sum(part * part) for part in sums)
-        loss_sum, square_sum = lax.psum((term[0, 0], squares), ("wide", "narrow"))
+        sums, loss_sum, square_sum = backward_plain(kept, patches, gauss_low, term, features, kinds)
     first_sum = sums[0].T
     grads = [first_sum[:features]] + list(sums[1:]) + [first_sum[features : features + kinds]]
     loss = loss_sum / divisor
@@ -1100,19 +1443,19 @@
 
 
 def solution(mesh):
-    columns = P(None, ("wide", "narrow"))
-    rows = P(("wide", "narrow"), None)
+    columns = P(None, BOTH)
+    rows = P(BOTH, None)
     weights = (columns,) * 3 + (rows,) * 15 + (columns,) * 3
     return jax.shard_map(
         body,
         mesh=mesh,
         in_specs=(
-            P("wide", None, "narrow", None),
-            P("wide", None, None, None, None),
-            P("wide", None, None, "narrow"),
-            P("wide", None, "narrow"),
-            P("wide", None, "narrow"),
-            P("wide"),
+            P(WIDE, None, NARROW, None),
+            P(WIDE, None, None, None, None),
+            P(WIDE, None, None, NARROW),
+            P(WIDE, None, NARROW),
+            P(WIDE, None, NARROW),
+            P(WIDE),
             P(),
         )
         + weights,

time: 581 us -> 459 us (0.79)
  waiting for transfers between devices: 50.9 us -> 0 us
  Pallas kernels: 362 us -> 411 us
  matrix products: 48.7 us -> 0 us
  local copies, waits for them, and re-layouts: 49.3 us -> 15.9 us
  other arithmetic: 36.7 us -> 20.2 us
  starting transfers between devices: 14.8 us -> 0 us
    all_to_all x2 -> x0, waiting for transfers between devices: 50.9 us -> none  [the longest x1 46.9 us: body(): lax.all_to_all(stacked, 'narrow', split_axis=0, concat_axis=2, tiled=True)]
    dot_general x15 -> x0, matrix products: 48.7 us -> none  [the longest x5 19.7 us: back_mul(): lax.dot_general(grad, weight, (((1,), (1,)), ((), ())), preferred_element...]
    pallas_call x1, Pallas kernels: 173 us -> 222 us  [backward_all(): pl.pallas_call(functools.partial(backward_kernel, items, wide, narrow, le...]
    all_to_all x2 -> x0, starting transfers between devices: 14.8 us -> none  [the longest x1 10.5 us: body(): lax.all_to_all(out_grad, 'narrow', split_axis=1, concat_axis=0, tiled=True)]
    another operation x9 -> x1, local copies, waits for them, and re-layouts: 9.35 us -> 0.1 us  [the longest x2 2.93 us: body(): jnp.stack([query_grad, key_grad, value_grad], 1).astype(BF16)]
    reduce_sum x8 -> x0, other arithmetic: 7.8 us -> none  [the longest x6 5.48 us: layer_norm(): centred = values - jnp.mean(values, -1, keepdims=True)]
    convert_element_type x4 -> x0, other arithmetic: 6.91 us -> none  [the longest x2 6.6 us: one_block(): score_low = score_grad.astype(jnp.bfloat16)]
    slice x4 -> x0, local copies, waits for them, and re-layouts: 6.68 us -> none  [the longest x3 5.21 us: body(): qkv[:, part].reshape(length, local_heads, HD)]
  transfers between devices with their start and end apart: 2 -> 0, of which waited for: 2 -> 0; matrix products, arithmetic and copies ran while one was open for 2% -> 0% of each run, Pallas kernels for 0% -> 0%
where the time goes in v3:
time: 459 us; the launch traced here: 453 us
  Pallas kernels  411 us (90%)
  other arithmetic  20.2 us (4%)
  local copies, waits for them, and re-layouts  15.9 us (3%)
  between operations  6.14 us (1%)
    pallas_call x1, Pallas kernels, backward_all(): pl.pallas_call(functools.partial(backward_kernel, items, wide, narrow, le...  222 us
    pallas_call x1, Pallas kernels, forward_all(): pl.pallas_call(functools.partial(forward_kernel, items, wide, narrow, lea...  184 us
    sub x7, other arithmetic, adamw(): weight - rate * (first_hat / (jnp.sqrt(second_hat) + ADAM_EPS) + DECAY *...  10.2 us

profile of v3, /device:TPU:0, one launch (start us, length us, event | category | flops | bytes accessed | tf_op | source)
XLA Modules:
  0.0 453.1 jit_solution(2945462292613981116)
XLA Ops:
  2.0 0.7 convert.9
  2.8 0.8 copy.81
  3.6 1.4 copy.83
  5.0 1.4 copy.85
  6.3 0.9 convert_bitcast_fusion
  7.2 0.7 fusion.8.refs_0_
  7.9 1.5 convert_element_type.30.refs_5_
  9.4 1.5 convert_element_type.27.refs_2_
  11.0 1.8 convert_element_type.26.refs_1_
  12.7 1.4 reduce
  14.7 0.7 convert_element_type.28.refs_3_
  15.5 0.7 convert_element_type.29.refs_4_
  16.2 0.8 pad.9.refs_6_.refs_18_
  17.2 0.6 reshape_squeeze.6
  18.7 2.3 copy.89
  21.5 184.4 %forward.1 = (bf16[1024,3072]{1,0:T(8,128)(2,1)}, bf16[1024,1024]{1,0:T(8,128)(2,1)}, bf16[1024,4096]{1,0:T(8,128)(2,1)}, bf16[4096,1024]{1,0:T(8,128)(2,1)}, bf...) custom-call(bf16[32,640]{1,0:T(8,128)(2,1)} %fusion.8.refs_0_, ...), custom_call_target="tpu_custom_call" | custom-call | tf_op jit(solution)/shard_map/forward/pallas_call | solution.py:555
  206.0 1.1 copy-done
  207.1 4.9 %render.1 = (bf16[256,768]{1,0:T(8,128)(2,1)S(1)}, f32[8,128]{1,0:T(8,128)S(1)}) custom-call(f32[256,768]{1,0:T(8,128)S(1)} %copy-done, f32[256,768]{1,0:T(8,128)S(1)} %reshape.64.weight_ref, bf16[192,768]{1,0:T(8,128)(2,1)S(1)} %reshape.62.target_ref, s32[64,768]{1,0:T(8,128)S(1)} %reshape.63.mask_ref, s32[2,2048]{1,0:T(2,128)S(1)} %bitcast.18, ...), custom_call_target="tpu_custom_call" | custom-call | tf_op jit(solution)/shard_map/render/pallas_call | solution.py:1260
  212.0 0.7 copy-done.1
  212.7 0.6 copy-done.3
  213.4 221.6 %backward.1 = (f32[32,640]{1,0:T(8,128)}, f32[32,3072]{1,0:T(8,128)}, f32[32,1024]{1,0:T(8,128)}, f32[32,4096]{1,0:T(8,128)}, f32[128,1024]{1,0:T(8,128)}, /*index=5*/f32[32,768]{1,0:T(8,128)}, f32[8,128]{1,0:T(8,128)}) custom-call(bf16[1024,3072]{1,0:T(8,128)(2,1)} %get-tuple-element.51.refs_0_, bf16[1024,1024]{1,0:T(8,128)(2,1)} %get-tuple-element.52.refs_1_, ...), custom_call_target="tpu_custom_call" | custom-call | tf_op jit(solution)/shard_map/backward/pallas_call | solution.py:1138
  435.0 1.3 fusion.17
  437.7 0.8 multiply_subtract_fusion.6
  438.5 0.7 copy.86
  439.2 0.7 copy.87
  439.9 0.7 copy.88
  440.6 1.7 multiply_subtract_fusion.5
  442.3 1.9 multiply_subtract_fusion.4
  444.2 1.7 multiply_subtract_fusion.3
  445.9 1.2 multiply_subtract_fusion.2
  447.2 1.4 multiply_subtract_fusion
  449.2 1.4 multiply_subtract_fusion.1
  (55 shorter events, 2.9 us)
Async XLA Ops:
  0.7 14.1 %copy-start.6 = (f32[32,4096]{1,0:T(8,128)S(1)}, f32[32,4096]{1,0:T(8,128)}, u32[]{:S(2)}) copy-start(f32[32,4096]{1,0:T(8,128)} %param.44) | copy-start | bytes 1572868
  11.0 4.5 copy-start.4
  12.7 3.5 copy-start.21
  14.3 2.6 copy-start.16
  21.0 185.0 %copy-start.2 = (s32[1,2,2048]{2,1,0:T(2,128)S(1)}, s32[1,2,2048]{2,1,0:T(2,128)}, u32[]{:S(2)}) copy-start(s32[1,2,2048]{2,1,0:T(2,128)} %param.32) | copy-start | bytes 49156
  206.0 1.1 copy-start
  212.0 0.7 copy-start.1
  212.7 0.6 copy-start.3
  213.3 227.2 %copy-start.22 = (f32[576,32]{0,1:T(8,128)S(1)}, f32[576,32]{0,1:T(8,128)}, u32[]{:S(2)}) copy-start(f32[576,32]{0,1:T(8,128)} %param.35) | copy-start | bytes 221188
  213.3 229.0 %copy-start.17 = (f32[32,768]{1,0:T(8,128)S(1)}, f32[32,768]{1,0:T(8,128)}, u32[]{:S(2)}) copy-start(f32[32,768]{1,0:T(8,128)} %param.50) | copy-start | bytes 294916
  213.3 230.9 %copy-start.9 = (f32[32,1024]{1,0:T(8,128)S(1)}, f32[32,1024]{1,0:T(8,128)}, u32[]{:S(2)}) copy-start(f32[32,1024]{1,0:T(8,128)} %param.41) | copy-start | bytes 393220
  213.3 230.9 %copy-start.23 = (f32[32,1024]{1,0:T(8,128)S(1)}, f32[32,1024]{1,0:T(8,128)}, u32[]{:S(2)}) copy-start(f32[32,1024]{1,0:T(8,128)} %param.42) | copy-start | bytes 393220
  213.3 230.9 %copy-start.24 = (f32[32,1024]{1,0:T(8,128)S(1)}, f32[32,1024]{1,0:T(8,128)}, u32[]{:S(2)}) copy-start(f32[32,1024]{1,0:T(8,128)} %param.43) | copy-start | bytes 393220
  435.0 10.9 %copy-start.8 = (f32[32,3072]{1,0:T(8,128)S(1)}, f32[32,3072]{1,0:T(8,128)}, u32[]{:S(2)}) copy-start(f32[32,3072]{1,0:T(8,128)} %param.38) | copy-start | bytes 1179652
  435.0 10.9 %copy-start.18 = (f32[32,3072]{1,0:T(8,128)S(1)}, f32[32,3072]{1,0:T(8,128)}, u32[]{:S(2)}) copy-start(f32[32,3072]{1,0:T(8,128)} %param.39) | copy-start | bytes 1179652
  435.0 10.9 %copy-start.19 = (f32[32,3072]{1,0:T(8,128)S(1)}, f32[32,3072]{1,0:T(8,128)}, u32[]{:S(2)}) copy-start(f32[32,3072]{1,0:T(8,128)} %param.40) | copy-start | bytes 1179652
  440.6 5.4 %copy-start.20 = (f32[32,3072]{1,0:T(8,128)S(1)}, f32[32,3072]{1,0:T(8,128)}, u32[]{:S(2)}) copy-start(f32[32,3072]{1,0:T(8,128)} %get-tuple-element.74) | copy-start | bytes 1179652
  442.3 4.9 %copy-start.5 = (f32[128,1024]{1,0:T(8,128)S(1)}, f32[128,1024]{1,0:T(8,128)}, u32[]{:S(2)}) copy-start(f32[128,1024]{1,0:T(8,128)} %param.47) | copy-start | bytes 1572868
  442.3 4.9 %copy-start.10 = (f32[128,1024]{1,0:T(8,128)S(1)}, f32[128,1024]{1,0:T(8,128)}, u32[]{:S(2)}) copy-start(f32[128,1024]{1,0:T(8,128)} %param.48) | copy-start | bytes 1572868
  442.3 4.9 %copy-start.11 = (f32[128,1024]{1,0:T(8,128)S(1)}, f32[128,1024]{1,0:T(8,128)}, u32[]{:S(2)}) copy-start(f32[128,1024]{1,0:T(8,128)} %param.49) | copy-start | bytes 1572868
  442.3 4.9 %copy-start.15 = (f32[128,1024]{1,0:T(8,128)S(1)}, f32[128,1024]{1,0:T(8,128)}, u32[]{:S(2)}) copy-start(f32[128,1024]{1,0:T(8,128)} %get-tuple-element.77) | copy-start | bytes 1572868
  447.1 1.5 copy-start.7
  447.1 1.5 copy-start.12
  447.1 1.9 copy-start.13
  447.1 2.1 copy-start.14

commit v4 on v3

--- a/solution.py
+++ b/solution.py
@@ -1,4 +1,5 @@
 import functools
+import heapq
 
 import jax
 import jax.numpy as jnp
@@ -181,6 +182,62 @@
         )
 
 
+class Planner:
+    def __init__(self):
+        self.now, self.count = 0.0, 0
+        self.free, self.events, self.done, self.spare = {}, [], set(), []
+
+    def transfer(self, link, cost, key, event):
+        self.free[link] = max(self.now, self.free.get(link, 0.0)) + cost
+        self.count += 1
+        heapq.heappush(self.events, (self.free[link] + 2.0, self.count, key, event))
+
+    def step(self):
+        when, _, key, event = heapq.heappop(self.events)
+        self.now = max(self.now, when) + 0.2
+        event()
+        self.done.add(key)
+
+    def fill(self, until):
+        for index, (keys, cost, work) in enumerate(self.spare):
+            if self.now + cost <= until and self.done.issuperset(keys):
+                del self.spare[index]
+                work()
+                self.now += cost
+                return True
+        return False
+
+    def need(self, keys):
+        while not self.done.issuperset(keys):
+            if not self.fill(self.events[0][0]):
+                self.step()
+
+    def work(self, cost, work):
+        while self.events and self.events[0][0] <= self.now:
+            self.step()
+        work()
+        self.now += cost
+
+    def later(self, cost, work, keys=()):
+        entry = (tuple(keys), cost, work)
+        self.spare.append(entry)
+        return entry
+
+    def force(self, entry):
+        if entry in self.spare:
+            self.spare.remove(entry)
+            self.work(entry[1], entry[2])
+
+    def finish(self):
+        while self.events or self.spare:
+            if not self.fill(self.events[0][0] if self.events else 1e9):
+                self.step()
+
+
+LINK = 100e3
+TWIN_LINK = 600e3
+
+
 def greet(peers):
     barrier = pltpu.get_barrier_semaphore()
     for peer in peers:
@@ -196,7 +253,7 @@
 
 def forward_plan(widths):
     items = []
-    for which, cuts in ((0, 1), (1, 3), (2, 1), (3, 4), (5, 1), (4, 4)):
+    for which, cuts in ((0, 1), (1, 3), (2, 1), (3, 2), (5, 1), (4, 2)):
         size = widths[which] // cuts
         for cut in range(cuts):
             for side, (start, width) in enumerate(column_halves(size)):
@@ -272,70 +329,63 @@
     def to_twin(item, mask):
         return remote(item, group(item, mask), group(item, mask), chips + mask, place.twin)
 
+    plan = Planner()
     waited = set()
-
-    def stage(item, number):
+    halves = (narrow // 2) * (narrow - narrow // 2)
+
+    def block_bytes(item):
+        which, _, width, _ = items[item]
+        return 2 * narrow * rows_of[which] * width
+
+    def twin_event(item, mask):
+        return lambda: to_twin(item, mask).wait_recv()
+
+    def onward(item, mask, number):
         bits = bits_of(item)
-        if number > len(bits):
-            for mask in range(chips):
-                to_twin(item, mask).wait_recv()
+        size = block_bytes(item)
+        for later in range(number, len(bits)):
+            start(across(item, mask, bits[later]))
+            coming = mask ^ bits[later]
+            plan.transfer(
+                bits[later], 2 * size / LINK, (item, coming), functools.partial(arrive, item, coming, later)
+            )
+        start(to_twin(item, mask))
+        plan.transfer(-1, size / TWIN_LINK, (item, chips + mask), twin_event(item, mask))
+
+    def arrive(item, mask, number):
+        across(item, mask ^ bits_of(item)[number], bits_of(item)[number]).wait_recv()
+        onward(item, mask, number + 1)
+
+    def begin_item(item):
+        if item >= total:
             return
-        held = [0]
-        if number == 0:
-            if items[item][0] not in waited:
-                waited.add(items[item][0])
-                own[items[item][0]].wait()
-            for step in range(1, narrow):
-                along(item, step).wait_recv()
-            fresh = [0]
-        else:
-            for bit in bits[: number - 1]:
-                held = held + [mask ^ bit for mask in held]
-            fresh = [mask ^ bits[number - 1] for mask in held]
-            for mask in fresh:
-                across(item, mask ^ bits[number - 1], bits[number - 1]).wait_recv()
-            held = held + fresh
-        if number < len(bits):
-            for mask in held:
-                start(across(item, mask, bits[number]))
-        for mask in fresh:
-            start(to_twin(item, mask))
-
-    arrived = [False] * total
-
-    def gather():
-        ahead = 4
-        for item in range(min(ahead, total)):
-            for step in range(1, narrow):
-                start(along(item, step))
-        depth = len(place.bits) + 2
-        for tick in range(0, total + 2 * (depth - 1), 2):
-            for number in reversed(range(depth)):
-                for item in (tick - 2 * number, tick - 2 * number + 1):
-                    if 0 <= item < total:
-                        stage(item, number)
-                        if number == depth - 1:
-                            arrived[item] = True
-            for item in (tick + ahead, tick + ahead + 1):
-                if item < total:
-                    for step in range(1, narrow):
-                        start(along(item, step))
-            yield
-
-    engine = gather()
-
-    def advance(steps=1):
-        for _ in range(steps):
-            next(engine, None)
+        for step in range(1, narrow):
+            start(along(item, step))
+        cost = halves * 2 * block_bytes(item) / narrow / LINK
+        plan.transfer(0, cost, (item, 0), functools.partial(line_event, item))
+
+    def line_event(item):
+        if items[item][0] not in waited:
+            waited.add(items[item][0])
+            own[items[item][0]].wait()
+        for step in range(1, narrow):
+            along(item, step).wait_recv()
+        begin_item(item + ahead)
+        onward(item, 0, 0)
+
+    ahead = 6
+    for item in range(min(ahead, total)):
+        begin_item(item)
 
     def need(which, columns=None):
-        wanted = [
-            index
-            for index, (owner, begin, width, _) in enumerate(items)
-            if owner == which and (columns is None or (begin < columns[1] and begin + width > columns[0]))
-        ]
-        while not all(arrived[index] for index in wanted):
-            next(engine)
+        plan.need(
+            [
+                (index, key)
+                for index, (owner, begin, width, _) in enumerate(items)
+                if owner == which and (columns is None or (begin < columns[1] and begin + width > columns[0]))
+                for key in range(2 * chips)
+            ]
+        )
 
     flushed = []
 
@@ -360,17 +410,25 @@
     normed, hidden, wave = at.normed, at.hidden, at.wave
     away, qkv, heads_out, returned = at.away, at.qkv, at.heads_out, at.returned
 
+    def turn(dest, source):
+        dest[...] = source[...].T
+        flush(dest)
+
     need(0)
     width = weights[0].shape[1]
     kind = lax.broadcasted_iota(jnp.int32, (8, LANES), 0)
     spot = lax.broadcasted_iota(jnp.int32, (8, LANES), 1)
     pick = (spot == kind + lead).astype(F32).astype(BF16)
     gains[...] = back_mul(pick, weights[0][:, width - LANES :])
-    for block in range(0, D, 256):
+    flush(gains)
+
+    def embed(block):
         cols = pl.ds(block, 256)
         embedded[:, cols] = back_mul(at.patches[...], weights[0][pl.ds(block, 256), : at.patches.shape[1]])
-    flush(at.embedded)
-    flush(at.gains)
+
+    for block in range(0, D, 256):
+        plan.work(0.5, functools.partial(embed, block))
+    flush(embedded)
 
     def norm_rows(source, row, dest):
         step_rows = 64
@@ -384,35 +442,39 @@
 
         lax.fori_loop(0, tokens // step_rows, one, 0)
 
-    norm_rows(embedded, 0, normed)
-    need(1)
-    for step in list(range(1, narrow)) + [0]:
+    plan.work(2.0, lambda: norm_rows(embedded, 0, normed))
+    turn_first = plan.later(2.0, lambda: turn(at.t1, normed))
+    piece = 2 * halves * 2 * tokens * head_width / LINK
+
+    def project(part, step):
         owner = lax.rem(me + step, narrow)
-
-        def project(part, carry):
-            offset = pl.multiple_of(part * D + owner * head_width, LANES)
-            value = matmul(normed[...], weights[1][:, pl.ds(offset, head_width)]).astype(BF16)
-            if step:
-                away[step - 1, part] = value
-            else:
-                qkv[me, part] = value
-            return carry
-
-        lax.fori_loop(0, 3, project, 0)
+        offset = pl.multiple_of(part * D + owner * head_width, LANES)
+        value = matmul(normed[...], weights[1][:, pl.ds(offset, head_width)]).astype(BF16)
         if step:
-            start(swap(away.at[step - 1], qkv.at[me], 0, step))
+            away[step - 1, part] = value
+            start(swap(away.at[step - 1, part], qkv.at[me, part], part, step))
+        else:
+            qkv[me, part] = value
+
+    def swap_event(part):
+        for step in range(1, narrow):
+            swap(away.at[step - 1, part], qkv.at[me, part], part, step).wait_recv()
+
+    for part in range(3):
+        need(1, (part * D, part * D + D))
+        for step in list(range(1, narrow)) + [0]:
+            plan.work(0.7, functools.partial(project, part, step))
+        plan.transfer(0, piece, (-1, part), functools.partial(swap_event, part))
     flush(at.w1)
-    at.t1[...] = normed[...].T
-    flush(at.t1)
-    advance(2)
-    for step in range(1, narrow):
-        swap(away.at[step - 1], qkv.at[me], 0, step).wait_recv()
-    flush(at.qkv)
+    plan.need([(-1, part) for part in range(3)])
+    flush(qkv)
+    plan.need([(-1, 2)])
 
     lane = lax.broadcasted_iota(jnp.int32, (1, LANES), 1)
     scale = HD ** (-0.5)
     length = narrow * tokens
-    for step in list(range(1, narrow)) + [0]:
+
+    def attend(step):
         who = lax.rem(me + step, narrow)
         log_sums = jnp.zeros((tokens, LANES), F32)
         for pair in range(head_width // LANES):
@@ -436,40 +498,53 @@
             heads_out[who, :, lanes] = out.astype(BF16)
         at.log_sums[who] = log_sums
         if step:
-            start(swap(heads_out.at[who], returned.at[me], 1, step))
-            if step % 2 == 0:
-                advance()
+            start(swap(heads_out.at[who], returned.at[me], 3, step))
         else:
             returned[me] = heads_out[who]
-    flush(at.heads_out)
+
+    def return_event(step):
+        return lambda: swap(heads_out.at[me], returned.at[me], 3, step).wait_recv()
+
+    for step in list(range(1, narrow)) + [0]:
+        plan.work(3.5, functools.partial(attend, step))
+        if step:
+            plan.transfer(0, piece / (narrow - 1), (-2, step), return_event(step))
+    flush(heads_out)
     flush(at.log_sums)
     need(2)
-    for step in range(1, narrow):
-        swap(heads_out.at[me], returned.at[me], 1, step).wait_recv()
-    for block in range(0, D, 256):
+    plan.need([(-2, step) for step in range(1, narrow)])
+
+    def merge(block):
         cols = pl.ds(block, 256)
         value = embedded[:, cols]
         for source in range(narrow):
             value = value + matmul(returned[source], weights[2][pl.ds(source * head_width, head_width), cols])
         mid[:, cols] = value
+
+    for block in range(0, D, 256):
+        plan.work(0.7, functools.partial(merge, block))
     flush(at.w2)
-    flush(at.mid)
-    norm_rows(mid, 1, normed)
-    for source in range(narrow):
-        at.t2[pl.ds(source * head_width, head_width), :] = returned[source].T
-    at.t3[...] = normed[...].T
-    flush(at.t2)
-    flush(at.t3)
+    flush(mid)
+    plan.force(turn_first)
+    plan.work(2.0, lambda: norm_rows(mid, 1, normed))
+
+    def turn_returned():
+        for source in range(narrow):
+            at.t2[pl.ds(source * head_width, head_width), :] = returned[source].T
+        flush(at.t2)
+
+    plan.later(2.0, turn_returned)
+    turn_second = plan.later(2.0, lambda: turn(at.t3, normed))
 
     ff = weights[3].shape[1]
     tile = wave.shape[1]
     slopes = at.slopes
-    for block in range(0, ff, tile):
-        need(3, (block, block + tile))
+
+    def expand(block):
         wave[...] = matmul(normed[...], weights[3][:, pl.ds(block, tile)])
 
         def bend(step, carry):
-            rows = pl.ds(pl.multiple_of(step * 16, 16), 16)
+            rows = pl.ds(pl.multiple_of(step * 32, 32), 32)
             x = wave[rows, :]
             half = 0.5 * (1.0 + lax.erf(x * (0.5**0.5)))
             hidden[rows, pl.ds(block, tile)] = (x * half).astype(BF16)
@@ -477,27 +552,42 @@
             slopes[rows, pl.ds(block, tile)] = (half + x * bell).astype(BF16)
             return carry
 
-        lax.fori_loop(0, tokens // 16, bend, 0)
+        lax.fori_loop(0, tokens // 32, bend, 0)
+
+    def turn_hidden(block):
         at.t4[pl.ds(block, tile), :] = hidden[:, pl.ds(block, tile)].T
+
+    for block in range(0, ff, tile):
+        need(3, (block, block + tile))
+        plan.work(2.5, functools.partial(expand, block))
+        plan.later(1.0, functools.partial(turn_hidden, block))
     flush(at.w3)
-    flush(at.slopes)
-    flush(at.t4)
+    flush(slopes)
+
+    def shrink(block):
+        cols = pl.ds(block, 256)
+        last[:, cols] = mid[:, cols] + matmul(hidden[...], weights[4][:, cols])
+
     for block in range(0, D, 256):
         need(4, (block, block + 256))
-        cols = pl.ds(block, 256)
-        last[:, cols] = mid[:, cols] + matmul(hidden[...], weights[4][:, cols])
+        plan.work(1.0, functools.partial(shrink, block))
     flush(at.w4)
-    flush(at.last)
-    norm_rows(last, 2, normed)
+    flush(last)
+    plan.force(turn_second)
+    plan.work(2.0, lambda: norm_rows(last, 2, normed))
     need(5)
-    for block in range(0, weights[5].shape[1], 256):
+
+    def unpatch(block):
         cols = pl.ds(block, 256)
         at.gaussians[:, cols] = matmul(normed[...], weights[5][:, cols])
+
+    for block in range(0, weights[5].shape[1], 256):
+        plan.work(0.7, functools.partial(unpatch, block))
     flush(at.w5)
     flush(at.gaussians)
-    at.t5[...] = normed[...].T
-    flush(at.t5)
-    advance(total)
+    plan.later(2.0, lambda: turn(at.t5, normed))
+    plan.finish()
+    flush(at.t4)
     for copy in started:
         copy.wait_send()
     for copy in flushed:
@@ -546,8 +636,8 @@
         own_sem=pltpu.SemaphoreType.DMA((6,)),
         send_sem=pltpu.SemaphoreType.DMA((len(items), slots)),
         recv_sem=pltpu.SemaphoreType.DMA((len(items), slots)),
-        swap_send=pltpu.SemaphoreType.DMA((2, narrow)),
-        swap_recv=pltpu.SemaphoreType.DMA((2, narrow)),
+        swap_send=pltpu.SemaphoreType.DMA((4, narrow)),
+        swap_recv=pltpu.SemaphoreType.DMA((4, narrow)),
         out_sem=pltpu.SemaphoreType.DMA((len(outs),)),
     )
     scratch = outs + tuple(extras)
@@ -702,25 +792,13 @@
         lax.fori_loop(0, (width // tile) * (narrow // together), one, 0)
 
     last_sent = {}
-    pushed = set()
+    plan = Planner()
+    halves = (narrow // 2) * (narrow - narrow // 2)
 
     def to_twin(item, mask):
         which, _, width, _ = items[item]
         own = spare[which].at[mask, :, :, pl.ds(0, width)]
         return remote(item, own, held[item].at[mask], mask, place.twin)
-
-    def push(which, part=None):
-        for item, (owner, begin, _, _) in enumerate(items):
-            if owner != which or (part is not None and begin // D != part):
-                continue
-            for mask in range(chips):
-                if (which, mask) in last_sent:
-                    last_sent[which, mask].wait_send()
-                product(item, mask, 1 - place.core, spare[which], False)
-                copy = to_twin(item, mask)
-                copy.start()
-                last_sent[which, mask] = copy
-            pushed.add(item)
 
     def across(item, mask, bit, number, slot):
         return remote(
@@ -737,14 +815,14 @@
             target,
         )
 
-    def split(item, number):
+    def leaves(item, mask):
         bits = bits_of(item)
-        keep = list(range(chips))
-        for bit in bits[:number]:
-            keep = [mask for mask in keep if not mask & bit]
-        if number < len(bits):
-            return [m for m in keep if m & bits[number]], [m for m in keep if not m & bits[number]]
-        return [], keep
+        return min([number for number, bit in enumerate(bits) if mask & bit], default=len(bits))
+
+    def slot_of(item, mask, number):
+        bits = bits_of(item)
+        kept = [m for m in range(chips) if not any(m & bit for bit in bits[: number + 1])]
+        return kept.index(mask)
 
     def add_into(dest, dest_at, src, src_at):
         def one(step, carry):
@@ -754,35 +832,58 @@
 
         lax.fori_loop(0, narrow, one, 0)
 
-    def stage(item, number):
-        assert item in pushed
+    def block_bytes(item):
+        which, _, width, _ = items[item]
+        return 2 * spare[which].shape[1] * spare[which].shape[2] * width
+
+    def push(which, part=None):
+        for item, (owner, begin, _, _) in enumerate(items):
+            if owner != which or (part is not None and begin // D != part):
+                continue
+            for mask in sorted(range(chips), key=lambda mask: leaves(item, mask)):
+                plan.work(block_bytes(item) / 4e5, functools.partial(push_one, item, mask))
+
+    def push_one(item, mask):
+        which = items[item][0]
+        if (which, mask) in last_sent:
+            last_sent[which, mask].wait_send()
+        product(item, mask, 1 - place.core, spare[which], False)
+        copy = to_twin(item, mask)
+        copy.start()
+        last_sent[which, mask] = copy
+        plan.transfer(-1, block_bytes(item) / TWIN_LINK, (item, 0, mask), functools.partial(own_event, item, mask))
+
+    def own_event(item, mask):
+        to_twin(item, mask).wait_recv()
+        product(item, mask, place.core, held[item], True)
+        plan.now += block_bytes(item) / 4e5
+        onward(item, mask, 0)
+
+    def onward(item, mask, number):
         bits = bits_of(item)
-        if number == 0:
-
-            def ready(mask):
-                to_twin(item, mask).wait_recv()
-                product(item, mask, place.core, held[item], True)
-
-        else:
-            bit = bits[number - 1]
-            _, kept = split(item, number - 1)
-
-            def ready(mask):
-                slot = kept.index(mask)
-                across(item, mask ^ bit, bit, number - 1, slot).wait_recv()
-                add_into(held[item], mask, passed[item][number - 1], slot)
-
-        away, keep = split(item, number)
-        if number < len(bits):
-            for mask in away:
-                ready(mask)
-                start(across(item, mask, bits[number], number, keep.index(mask ^ bits[number])))
-            for mask in keep:
-                ready(mask)
-        else:
-            ready(0)
+        if number == len(bits):
             for step in range(1, narrow):
                 start(along(item, step))
+            cost = halves * 2 * block_bytes(item) / narrow / LINK
+            plan.transfer(0, cost, (item, -1, 0), functools.partial(finish, item))
+        elif leaves(item, mask) == number:
+            kept = mask ^ bits[number]
+            start(across(item, mask, bits[number], number, slot_of(item, kept, number)))
+            plan.transfer(
+                bits[number],
+                2 * block_bytes(item) / LINK,
+                (item, 1 + number, kept),
+                functools.partial(sum_event, item, kept, number),
+            )
+
+    def sum_event(item, mask, number):
+        plan.need([(item, before, mask) for before in range(number + 1)])
+        bit = bits_of(item)[number]
+        slot = slot_of(item, mask, number)
+        across(item, mask ^ bit, bit, number, slot).wait_recv()
+        add_into(held[item], mask, passed[item][number], slot)
+        plan.now += block_bytes(item) / 8e5
+        onward(item, mask, number + 1)
 
     squares = []
 
@@ -795,24 +896,6 @@
             value = value + final[item][slot].astype(F32)
         sums[which][:, pl.ds(begin, width)] = value
         squares.append(jnp.sum(value * value))
-
-    progress = [0] * (total // 2)
-    depth = len(place.bits) + 1
-
-    def advance(steps=1):
-        for _ in range(steps):
-            entered = False
-            for pair in range(total // 2):
-                number = progress[pair]
-                if number > depth or (number == 0 and (entered or 2 * pair not in pushed)):
-                    continue
-                entered = entered or number == 0
-                progress[pair] = number + 1
-                for item in (2 * pair, 2 * pair + 1):
-                    if number < depth:
-                        stage(item, number)
-                    else:
-                        finish(item)
 
     norms[...] = jnp.zeros_like(norms)
 
@@ -841,6 +924,7 @@
 
     load(at.t5).wait()
     push(5)
+    plan.now += 3.0
     load_stash(src.last).wait()
     count = D // u_rows
     tall_rows = slope_rows
@@ -863,8 +947,8 @@
     norm_back(2, shrink_low, False)
     load_stash(src.mid).start()
     load(at.t4).wait()
+    plan.now += 3.0
     push(4)
-    advance()
     ff = src.w3.shape[1]
     slabs = ff // tall_rows
 
@@ -888,8 +972,8 @@
     for index in range(2):
         ring(src.w2, at.tall, head_width, D, index, owners[index] * head_width).start()
     load(at.t3).wait()
+    plan.now += 6.0
     push(3)
-    advance()
 
     def through_expand(index, carry):
         ring(src.w3, at.long, 128, ff, index, index * 128).wait()
@@ -920,6 +1004,13 @@
         )
 
     d_heads, away = at.d_heads, at.away
+    plan.now += 7.0
+    piece = 2 * halves * 2 * tokens * head_width / LINK
+
+    def head_event():
+        for step in range(1, narrow):
+            swap(away.at[step - 1], d_heads.at[me], 0, step).wait_recv()
+
     for index, owner in enumerate(owners):
         ring(src.w2, at.tall, head_width, D, index, owner * head_width).wait()
         value = back_mul(merge_low[...], at.tall[index % 2, 0:head_width, :]).astype(BF16)
@@ -930,14 +1021,14 @@
             d_heads[me] = value
         if index + 2 < narrow:
             ring(src.w2, at.tall, head_width, D, index + 2, owners[index + 2] * head_width).start()
+    plan.now += 3.0
+    plan.transfer(0, piece, (-1, 0, 0), head_event)
     load(at.t2).wait()
     push(2)
-    advance()
     load(at.qkv).wait()
     load(at.heads_out).wait()
     load(at.log_sums).wait()
-    for step in range(1, narrow):
-        swap(away.at[step - 1], d_heads.at[me], 0, step).wait_recv()
+    plan.need([(-1, 0, 0)])
 
     qkv, heads_out, log_sums, parts = at.qkv, at.heads_out, at.log_sums, at.parts
     key_t, key_acc, value_acc, query_acc = at.key_t, at.key_acc, at.value_acc, at.query_acc
@@ -958,12 +1049,16 @@
             step,
         )
 
+    def part_event(pair):
+        for step in range(1, narrow):
+            part_swap(pair, step).wait_recv()
+
     for pair in range(head_width // LANES):
         lanes = pl.ds(pair * LANES, LANES)
         key_t[...] = qkv[:, 1, :, lanes].reshape(length, LANES).T
         key_acc[...] = jnp.zeros_like(key_acc)
         value_acc[...] = jnp.zeros_like(value_acc)
-        for step in range(narrow):
+        def one_block(step, lanes=lanes, pair=pair):
             who = lax.rem(me + step, narrow)
             query = qkv[who, 0, :, lanes].astype(F32)
             upper = d_heads[who, :, lanes].astype(F32)
@@ -997,22 +1092,21 @@
 
             lax.fori_loop(0, narrow, block, 0)
             parts[who, 0, :, lanes] = query_acc[...].T.astype(BF16)
-            if step % 2 == 1:
-                advance()
+        for step in range(narrow):
+            plan.work(3.0, functools.partial(one_block, step))
         for source in range(narrow):
             rows = pl.ds(source * tokens, tokens)
             parts[source, 1, :, lanes] = key_acc[rows, :].astype(BF16)
             parts[source, 2, :, lanes] = value_acc[rows, :].astype(BF16)
         for step in range(1, narrow):
             start(part_swap(pair, step))
+        plan.now += 1.0
+        plan.transfer(0, 1.5 * piece, (-2, 0, pair), functools.partial(part_event, pair))
         mixed[:, :, pl.ds(pl.multiple_of(me * head_width + pair * LANES, LANES), LANES)] = parts[me, :, :, lanes]
     load(at.t1).wait()
-    for pair in range(head_width // LANES):
-        for step in range(1, narrow):
-            part_swap(pair, step).wait_recv()
+    plan.need([(-2, 0, pair) for pair in range(head_width // LANES)])
     for part in range(3):
         push(1, part)
-        advance()
 
     def through_mixer(index, carry):
         ring(src.w1, at.long, 128, 3 * D, index, index * 128).wait()
@@ -1028,15 +1122,14 @@
 
         return carry
 
-    lax.fori_loop(0, D // 128, through_mixer, 0)
+    plan.work(4.0, lambda: lax.fori_loop(0, D // 128, through_mixer, 0))
     load_stash(src.embedded).wait()
-    norm_back(0, at.embed_low, True)
+    plan.work(3.0, lambda: norm_back(0, at.embed_low, True))
     at.embed_t[...] = at.embed_low[...].T
     turned = jnp.concatenate([norms[...], jnp.zeros((LANES - 8, D), F32)], 0).T
     at.extra[...] = pltpu.roll(turned, lead, 1)
     push(0)
-    advance(total)
-    assert min(progress) > depth
+    plan.finish()
 
     rows = lax.broadcasted_iota(jnp.int32, (8, LANES), 0)
     wide_tiles, narrow_tiles = at.wide_tiles, at.narrow_tiles

time: 459 us -> 440 us (0.959)
  Pallas kernels: 411 us -> 392 us
    pallas_call x1, Pallas kernels: 184 us -> 165 us  [forward_all(): pl.pallas_call(functools.partial(forward_kernel, items, wide, narrow, lea...]
where the time goes in v4:
time: 440 us; the launch traced here: 434 us
  Pallas kernels  392 us (89%)
  other arithmetic  20.2 us (5%)
  local copies, waits for them, and re-layouts  15.9 us (4%)
  between operations  6.14 us (1%)
    pallas_call x1, Pallas kernels, backward_all(): pl.pallas_call(functools.partial(backward_kernel, items, wide, narrow, le...  222 us
    pallas_call x1, Pallas kernels, forward_all(): pl.pallas_call(functools.partial(forward_kernel, items, wide, narrow, lea...  165 us
    sub x7, other arithmetic, adamw(): weight - rate * (first_hat / (jnp.sqrt(second_hat) + ADAM_EPS) + DECAY *...  10.2 us
    unnamed x57, local copies, waits for them, and re-layouts  8.89 us

profile of v4, /device:TPU:0, one launch (start us, length us, event | category | flops | bytes accessed | tf_op | source)
XLA Modules:
  0.0 433.9 jit_solution(2010973543951450937)
XLA Ops:
  2.0 0.7 convert.9
  2.8 0.8 copy.81
  3.6 1.4 copy.83
  5.0 1.4 copy.85
  6.3 0.9 convert_bitcast_fusion
  7.2 0.7 fusion.8.refs_0_
  7.9 1.5 convert_element_type.30.refs_5_
  9.4 1.5 convert_element_type.27.refs_2_
  11.0 1.8 convert_element_type.26.refs_1_
  12.7 1.4 reduce
  14.7 0.7 convert_element_type.28.refs_3_
  15.5 0.7 convert_element_type.29.refs_4_
  16.2 0.8 pad.9.refs_6_.refs_18_
  17.2 0.6 reshape_squeeze.6
  18.7 2.3 copy.89
  21.5 165.0 %forward.1 = (bf16[1024,3072]{1,0:T(8,128)(2,1)}, bf16[1024,1024]{1,0:T(8,128)(2,1)}, bf16[1024,4096]{1,0:T(8,128)(2,1)}, bf16[4096,1024]{1,0:T(8,128)(2,1)}, bf...) custom-call(bf16[32,640]{1,0:T(8,128)(2,1)} %fusion.8.refs_0_, ...), custom_call_target="tpu_custom_call" | custom-call | tf_op jit(solution)/shard_map/forward/pallas_call | solution.py:645
  186.5 1.1 copy-done
  187.7 4.9 %render.1 = (bf16[256,768]{1,0:T(8,128)(2,1)S(1)}, f32[8,128]{1,0:T(8,128)S(1)}) custom-call(f32[256,768]{1,0:T(8,128)S(1)} %copy-done, f32[256,768]{1,0:T(8,128)S(1)} %reshape.64.weight_ref, bf16[192,768]{1,0:T(8,128)(2,1)S(1)} %reshape.62.target_ref, s32[64,768]{1,0:T(8,128)S(1)} %reshape.63.mask_ref, s32[2,2048]{1,0:T(2,128)S(1)} %bitcast.18, ...), custom_call_target="tpu_custom_call" | custom-call | tf_op jit(solution)/shard_map/render/pallas_call | solution.py:1353
  192.5 0.7 copy-done.1
  193.3 0.6 copy-done.3
  193.9 221.9 %backward.1 = (f32[32,640]{1,0:T(8,128)}, f32[32,3072]{1,0:T(8,128)}, f32[32,1024]{1,0:T(8,128)}, f32[32,4096]{1,0:T(8,128)}, f32[128,1024]{1,0:T(8,128)}, /*index=5*/f32[32,768]{1,0:T(8,128)}, f32[8,128]{1,0:T(8,128)}) custom-call(bf16[1024,3072]{1,0:T(8,128)(2,1)} %get-tuple-element.51.refs_0_, bf16[1024,1024]{1,0:T(8,128)(2,1)} %get-tuple-element.52.refs_1_, ...), custom_call_target="tpu_custom_call" | custom-call | tf_op jit(solution)/shard_map/backward/pallas_call | solution.py:1231
  415.8 1.3 fusion.17
  418.5 0.8 multiply_subtract_fusion.6
  419.4 0.7 copy.86
  420.0 0.7 copy.87
  420.7 0.7 copy.88
  421.4 1.7 multiply_subtract_fusion.5
  423.1 1.9 multiply_subtract_fusion.4
  425.0 1.7 multiply_subtract_fusion.3
  426.8 1.2 multiply_subtract_fusion.2
  428.0 1.4 multiply_subtract_fusion
  430.0 1.4 multiply_subtract_fusion.1
  (55 shorter events, 2.9 us)
Async XLA Ops:
  0.7 14.1 %copy-start.6 = (f32[32,4096]{1,0:T(8,128)S(1)}, f32[32,4096]{1,0:T(8,128)}, u32[]{:S(2)}) copy-start(f32[32,4096]{1,0:T(8,128)} %param.44) | copy-start | bytes 1572868
  11.0 4.5 %copy-start.4 = (f32[128,1024]{1,0:T(8,128)S(1)}, f32[128,1024]{1,0:T(8,128)}, u32[]{:S(2)}) copy-start(f32[128,1024]{1,0:T(8,128)} %param.47) | copy-start | bytes 1572868
  12.7 3.5 copy-start.21
  14.3 2.6 copy-start.16
  21.0 165.5 %copy-start.2 = (s32[1,2,2048]{2,1,0:T(2,128)S(1)}, s32[1,2,2048]{2,1,0:T(2,128)}, u32[]{:S(2)}) copy-start(s32[1,2,2048]{2,1,0:T(2,128)} %param.32) | copy-start | bytes 49156
  186.5 1.1 copy-start
  192.5 0.7 copy-start.1
  193.3 0.6 copy-start.3
  193.9 227.5 %copy-start.22 = (f32[576,32]{0,1:T(8,128)S(1)}, f32[576,32]{0,1:T(8,128)}, u32[]{:S(2)}) copy-start(f32[576,32]{0,1:T(8,128)} %param.35) | copy-start | bytes 221188
  193.9 229.2 %copy-start.17 = (f32[32,768]{1,0:T(8,128)S(1)}, f32[32,768]{1,0:T(8,128)}, u32[]{:S(2)}) copy-start(f32[32,768]{1,0:T(8,128)} %param.50) | copy-start | bytes 294916
  193.9 231.1 %copy-start.9 = (f32[32,1024]{1,0:T(8,128)S(1)}, f32[32,1024]{1,0:T(8,128)}, u32[]{:S(2)}) copy-start(f32[32,1024]{1,0:T(8,128)} %param.41) | copy-start | bytes 393220
  193.9 231.1 %copy-start.23 = (f32[32,1024]{1,0:T(8,128)S(1)}, f32[32,1024]{1,0:T(8,128)}, u32[]{:S(2)}) copy-start(f32[32,1024]{1,0:T(8,128)} %param.42) | copy-start | bytes 393220
  193.9 231.1 %copy-start.24 = (f32[32,1024]{1,0:T(8,128)S(1)}, f32[32,1024]{1,0:T(8,128)}, u32[]{:S(2)}) copy-start(f32[32,1024]{1,0:T(8,128)} %param.43) | copy-start | bytes 393220
  415.8 10.9 %copy-start.8 = (f32[32,3072]{1,0:T(8,128)S(1)}, f32[32,3072]{1,0:T(8,128)}, u32[]{:S(2)}) copy-start(f32[32,3072]{1,0:T(8,128)} %param.38) | copy-start | bytes 1179652
  415.8 10.9 %copy-start.18 = (f32[32,3072]{1,0:T(8,128)S(1)}, f32[32,3072]{1,0:T(8,128)}, u32[]{:S(2)}) copy-start(f32[32,3072]{1,0:T(8,128)} %param.39) | copy-start | bytes 1179652
  415.8 10.9 %copy-start.19 = (f32[32,3072]{1,0:T(8,128)S(1)}, f32[32,3072]{1,0:T(8,128)}, u32[]{:S(2)}) copy-start(f32[32,3072]{1,0:T(8,128)} %param.40) | copy-start | bytes 1179652
  421.4 5.4 %copy-start.20 = (f32[32,3072]{1,0:T(8,128)S(1)}, f32[32,3072]{1,0:T(8,128)}, u32[]{:S(2)}) copy-start(f32[32,3072]{1,0:T(8,128)} %get-tuple-element.74) | copy-start | bytes 1179652
  423.1 4.9 %copy-start.5 = (f32[128,1024]{1,0:T(8,128)S(1)}, f32[128,1024]{1,0:T(8,128)}, u32[]{:S(2)}) copy-start(f32[128,1024]{1,0:T(8,128)} %param.47) | copy-start | bytes 1572868
  423.1 4.9 %copy-start.10 = (f32[128,1024]{1,0:T(8,128)S(1)}, f32[128,1024]{1,0:T(8,128)}, u32[]{:S(2)}) copy-start(f32[128,1024]{1,0:T(8,128)} %param.48) | copy-start | bytes 1572868
  423.1 4.9 %copy-start.11 = (f32[128,1024]{1,0:T(8,128)S(1)}, f32[128,1024]{1,0:T(8,128)}, u32[]{:S(2)}) copy-start(f32[128,1024]{1,0:T(8,128)} %param.49) | copy-start | bytes 1572868
  423.1 4.9 %copy-start.15 = (f32[128,1024]{1,0:T(8,128)S(1)}, f32[128,1024]{1,0:T(8,128)}, u32[]{:S(2)}) copy-start(f32[128,1024]{1,0:T(8,128)} %get-tuple-element.77) | copy-start | bytes 1572868
  428.0 1.5 copy-start.7
  428.0 1.5 copy-start.12
  428.0 1.9 copy-start.13
  428.0 2.1 copy-start.14

commit v5 on v4

--- a/solution.py
+++ b/solution.py
@@ -186,6 +186,7 @@
     def __init__(self):
         self.now, self.count = 0.0, 0
         self.free, self.events, self.done, self.spare = {}, [], set(), []
+        self.refill = lambda: None
 
     def transfer(self, link, cost, key, event):
         self.free[link] = max(self.now, self.free.get(link, 0.0)) + cost
@@ -197,6 +198,7 @@
         self.now = max(self.now, when) + 0.2
         event()
         self.done.add(key)
+        self.refill()
 
     def fill(self, until):
         for index, (keys, cost, work) in enumerate(self.spare):
@@ -215,6 +217,7 @@
     def work(self, cost, work):
         while self.events and self.events[0][0] <= self.now:
             self.step()
+        self.refill()
         work()
         self.now += cost
 
@@ -265,7 +268,8 @@
     at = Bag(zip(ins + scratch, refs[: len(ins)] + refs[len(ins) + len(outs) :]))
     results = refs[len(ins) : len(ins) + len(outs)]
     weights = [at.first_weight, at.w1, at.w2, at.w3, at.w4, at.w5]
-    shards = [at.s0, at.s1, at.s2, at.s3, at.s4, at.s5]
+    shards = [at.c0, at.c1, at.c2, at.c3, at.c4, at.c5]
+    raw = [at.s0, at.s1, at.s2, at.s3, at.s4, at.s5]
     own_sem, send_sem, recv_sem = at.own_sem, at.send_sem, at.recv_sem
     swap_send, swap_recv, out_sem = at.swap_send, at.swap_recv, at.out_sem
     place = Place(wide, narrow)
@@ -279,6 +283,16 @@
         copy.start()
         started.append(copy)
 
+    features = at.s0.shape[1]
+    tail = shards[0].shape[1] - LANES
+    kinds = at.norm_raw.shape[0]
+    kind = lax.broadcasted_iota(jnp.int32, (kinds, LANES), 0)
+    spot = lax.broadcasted_iota(jnp.int32, (kinds, LANES), 1)
+    put = (spot == kind + lead).astype(F32).astype(BF16)
+    shards[0][:, tail:] = outer_sum(at.norm_raw[...].astype(BF16), put).astype(BF16)
+    shards[0][:, 0:features] = at.s0[...].astype(BF16)
+    for source, dest in zip(raw[1:], shards[1:]):
+        dest[...] = source[...].astype(BF16)
     greet(place.neighbours())
     rows_of = [shard.shape[0] for shard in shards]
 
@@ -357,8 +371,6 @@
         onward(item, mask, number + 1)
 
     def begin_item(item):
-        if item >= total:
-            return
         for step in range(1, narrow):
             start(along(item, step))
         cost = halves * 2 * block_bytes(item) / narrow / LINK
@@ -370,12 +382,17 @@
             own[items[item][0]].wait()
         for step in range(1, narrow):
             along(item, step).wait_recv()
-        begin_item(item + ahead)
         onward(item, 0, 0)
 
-    ahead = 6
-    for item in range(min(ahead, total)):
-        begin_item(item)
+    begun = []
+
+    def refill():
+        while len(begun) < total and plan.free.get(0, 0.0) < plan.now + 7.0:
+            begin_item(len(begun))
+            begun.append(True)
+
+    plan.refill = refill
+    refill()
 
     def need(which, columns=None):
         plan.need(
@@ -594,9 +611,9 @@
         copy.wait()
 
 
-def forward_all(shards, patches, lead, wide, narrow):
+def forward_all(shards, norms, patches, lead, wide, narrow):
     tokens = patches.shape[0]
-    widths = [shard.shape[1] for shard in shards]
+    widths = [patches.shape[1]] + [shard.shape[1] for shard in shards[1:]]
     heights = [shard.shape[0] * wide * narrow for shard in shards]
     ff = widths[3]
     head_width = D // narrow
@@ -624,10 +641,16 @@
         log_sums=((narrow, tokens, LANES), F32),
         gaussians=((tokens, widths[5]), F32),
     )
-    ins = tuple(dict(s0=0, s1=0, s2=0, s3=0, s4=0, s5=0, patches=0))
+    ins = tuple(dict(s0=0, s1=0, s2=0, s3=0, s4=0, s5=0, norm_raw=0, patches=0))
     outs = tuple(shapes)
     extras = dict(
         first_weight=pltpu.VMEM((heights[0], widths[0]), BF16),
+        c0=pltpu.VMEM((shards[0].shape[0], widths[0]), BF16),
+        c1=pltpu.VMEM(shards[1].shape, BF16),
+        c2=pltpu.VMEM(shards[2].shape, BF16),
+        c3=pltpu.VMEM(shards[3].shape, BF16),
+        c4=pltpu.VMEM(shards[4].shape, BF16),
+        c5=pltpu.VMEM(shards[5].shape, BF16),
         normed=pltpu.VMEM((tokens, D), BF16),
         hidden=pltpu.VMEM((tokens, ff), BF16),
         wave=pltpu.VMEM((tokens, 512), F32),
@@ -645,14 +668,14 @@
     results = pl.pallas_call(
         functools.partial(forward_kernel, items, wide, narrow, lead, ins, outs, scratch),
         out_shape=[jax.ShapeDtypeStruct(*shapes[name]) for name in outs],
-        in_specs=[anywhere] * 6 + [pl.BlockSpec(memory_space=pltpu.VMEM)],
+        in_specs=[pl.BlockSpec(memory_space=pltpu.VMEM)] * len(ins),
         out_specs=[anywhere] * len(outs),
         scratch_shapes=[pltpu.VMEM(*shapes[name]) for name in outs] + list(extras.values()),
         compiler_params=pltpu.CompilerParams(
             collective_id=0, has_side_effects=True, vmem_limit_bytes=60 * MIB
         ),
         name="forward",
-    )(*shards, patches)
+    )(*shards, norms, patches)
     return Bag(zip(outs, results))
 
 
@@ -757,48 +780,56 @@
     def bits_of(item):
         return place.bits[::-1] if items[item][3] == 0 else place.bits
 
-    def product(item, mask, core, into, plus):
+    def groups_of(item):
+        size = max(1, 512 // (narrow * spare[items[item][0]].shape[2]))
+        masks = list(range(chips))
+        if bits_of(item) and bits_of(item)[0] > 1:
+            masks = masks[chips // 2 :] + masks[: chips // 2]
+        return [sorted(masks[at_mask : at_mask + size]) for at_mask in range(0, chips, size)]
+
+    def product(item, masks, core, into, plus):
         which, begin, width, _ = items[item]
         left, right = lefts[which], rights[which]
         rows = into.shape[-2]
+        span = narrow * rows
         tile = tile_of(width)
-        together = max(1, min(narrow, 128 // rows))
-        first = ((flip(place.chip, mask) * 2 + core) * narrow) * rows
+        firsts = [((flip(place.chip, mask) * 2 + core) * narrow) * rows for mask in masks]
         with_extra = which == 0 and begin + width == right.shape[1]
         assert not with_extra or tile == width
         part, begin = (begin // D, begin % D) if which == 1 else (None, begin)
 
         def one(step, carry):
-            across, down = step % (width // tile), step // (width // tile)
-            offset = pl.multiple_of(begin + across * tile, LANES)
-            local = pl.multiple_of(across * tile, LANES)
-            ns = pl.ds(down * together, together)
-            span = together * rows
-            where = pl.ds(pl.multiple_of(first + down * span, span), span)
+            offset = pl.multiple_of(begin + step * tile, LANES)
+            local = pl.multiple_of(step * tile, LANES)
             if part is None:
                 rhs = right[:, pl.ds(offset, tile)]
             else:
                 rhs = right[part, :, pl.ds(offset, tile)]
-            value = jnp.dot(left[where, :], rhs, preferred_element_type=F32)
-            if with_extra:
-                more = jnp.concatenate([jnp.zeros((span, tile - LANES), F32), extra[where, :]], 1)
-                value = value + more
-            value = value.reshape(together, rows, tile)
-            if plus:
-                value = value + into[mask, ns, :, pl.ds(local, tile)].astype(F32)
-            into[mask, ns, :, pl.ds(local, tile)] = value.astype(BF16)
+            spots = [pl.ds(pl.multiple_of(first, span), span) for first in firsts]
+            lhs = jnp.concatenate([left[spot, :] for spot in spots], 0)
+            value = jnp.dot(lhs, rhs, preferred_element_type=F32)
+            for index, mask in enumerate(masks):
+                piece = value[index * span : (index + 1) * span]
+                if with_extra:
+                    blank = jnp.zeros((span, tile - LANES), F32)
+                    piece = piece + jnp.concatenate([blank, extra[spots[index], :]], 1)
+                piece = piece.reshape(narrow, rows, tile)
+                if plus:
+                    piece = piece + into[mask, :, :, pl.ds(local, tile)].astype(F32)
+                into[mask, :, :, pl.ds(local, tile)] = piece.astype(BF16)
             return carry
 
-        lax.fori_loop(0, (width // tile) * (narrow // together), one, 0)
+        lax.fori_loop(0, width // tile, one, 0)
 
     last_sent = {}
     plan = Planner()
     halves = (narrow // 2) * (narrow - narrow // 2)
 
-    def to_twin(item, mask):
+    def to_twin(item, masks):
         which, _, width, _ = items[item]
-        own = spare[which].at[mask, :, :, pl.ds(0, width)]
-        return remote(item, own, held[item].at[mask], mask, place.twin)
+        some = pl.ds(masks[0], len(masks))
+        own = spare[which].at[some, :, :, pl.ds(0, width)]
+        return remote(item, own, held[item].at[some], masks[0], place.twin)
 
     def across(item, mask, bit, number, slot):
         return remote(
@@ -840,24 +871,28 @@
         for item, (owner, begin, _, _) in enumerate(items):
             if owner != which or (part is not None and begin // D != part):
                 continue
-            for mask in sorted(range(chips), key=lambda mask: leaves(item, mask)):
-                plan.work(block_bytes(item) / 4e5, functools.partial(push_one, item, mask))
-
-    def push_one(item, mask):
+            for masks in groups_of(item):
+                cost = len(masks) * block_bytes(item) / 1e6
+                plan.work(cost, functools.partial(push_some, item, masks))
+
+    def push_some(item, masks):
         which = items[item][0]
-        if (which, mask) in last_sent:
-            last_sent[which, mask].wait_send()
-        product(item, mask, 1 - place.core, spare[which], False)
-        copy = to_twin(item, mask)
+        for key in [key for key in last_sent if key[0] == which and set(key[1]) & set(masks)]:
+            last_sent.pop(key).wait_send()
+        product(item, masks, 1 - place.core, spare[which], False)
+        copy = to_twin(item, masks)
         copy.start()
-        last_sent[which, mask] = copy
-        plan.transfer(-1, block_bytes(item) / TWIN_LINK, (item, 0, mask), functools.partial(own_event, item, mask))
-
-    def own_event(item, mask):
-        to_twin(item, mask).wait_recv()
-        product(item, mask, place.core, held[item], True)
-        plan.now += block_bytes(item) / 4e5
-        onward(item, mask, 0)
+        last_sent[which, tuple(masks)] = copy
+        cost = len(masks) * block_bytes(item) / TWIN_LINK
+        plan.transfer(-1, cost, (item, 0, masks[0]), functools.partial(own_event, item, masks))
+
+    def own_event(item, masks):
+        to_twin(item, masks).wait_recv()
+        product(item, masks, place.core, held[item], True)
+        plan.now += len(masks) * block_bytes(item) / 1e6
+        plan.done.update((item, 0, mask) for mask in masks)
+        for mask in masks:
+            onward(item, mask, 0)
 
     def onward(item, mask, number):
         bits = bits_of(item)
@@ -1462,6 +1497,53 @@
     return sums, loss_sum, square_sum
 
 
+def update_kernel(features, total_ref, sums_ref, *refs):
+    grads, refs = refs[:6], refs[6:]
+    olds, news = refs[:21], refs[21:42]
+    loss_ref, norm_ref, turned = refs[42:]
+    square_sum = sums_ref[1:2, 0:1]
+    grad_norm = jnp.sqrt(square_sum)
+    factor = jnp.minimum(1.0, CLIP_NORM / (grad_norm + 1e-06))
+    norm_ref[...] = grad_norm
+    loss_ref[...] = sums_ref[0:1, 0:1] / total_ref[0].astype(F32)
+    width = grads[0].shape[1]
+    turned[...] = grads[0][:, width - LANES :].T
+    for which in range(7):
+        weight, first, second = olds[3 * which : 3 * which + 3]
+        rows, columns = weight.shape
+        chunk = min(8, rows)
+
+        def one(step, carry):
+            spot = pl.ds(pl.multiple_of(step * chunk, chunk), chunk)
+            if which == 0:
+                grad = grads[0][spot, 0:columns]
+            elif which == 6:
+                grad = turned[features % LANES : features % LANES + rows, 0:columns]
+            else:
+                grad = grads[which][spot, :]
+            values = adamw(weight[spot, :], first[spot, :], second[spot, :], grad * factor, RATES[which])
+            for dest, value in zip(news[3 * which : 3 * which + 3], values):
+                dest[spot, :] = value
+            return carry
+
+        lax.fori_loop(0, rows // chunk, one, 0)
+
+
+def update_all(olds, sums, totals, pair_total, features):
+    vmem = pl.BlockSpec(memory_space=pltpu.VMEM)
+    smem = pl.BlockSpec(memory_space=pltpu.SMEM)
+    shapes = [jax.ShapeDtypeStruct(old.shape, F32) for old in olds]
+    return pl.pallas_call(
+        functools.partial(update_kernel, features),
+        out_shape=shapes + [jax.ShapeDtypeStruct((1, 1), F32)] * 2,
+        in_specs=[smem] + [vmem] * 28,
+        out_specs=[vmem] * 23,
+        scratch_shapes=[pltpu.VMEM((LANES, sums[0].shape[0]), F32)],
+        compiler_params=pltpu.CompilerParams(vmem_limit_bytes=40 * MIB),
+        name="update",
+    )(pair_total, totals, *sums, *olds)
+
+
 def body(
     views,
     render_w,
@@ -1503,15 +1585,16 @@
     fill = padded - features - kinds
     by_kernel = mixer_weight.shape[0] % 16 == 0
 
-    first_shard = jnp.concatenate([embed_weight.T, norm_params.T], 1)
-    first_shard = jnp.pad(first_shard.astype(BF16), ((0, 0), (0, fill)))
-    shards = [first_shard] + [weight.astype(BF16) for weight in masters[1:6]]
     patches = views.reshape(-1, features)
     rows = patches.shape[0]
     patches = jnp.pad(patches, ((0, 0), (0, padded - features)))
     if by_kernel:
-        kept = forward_all(shards, patches, features % LANES, wide_count, groups)
+        raw = (embed_weight.T,) + masters[1:6]
+        kept = forward_all(raw, norm_params, patches, features % LANES, wide_count, groups)
     else:
+        first_shard = jnp.concatenate([embed_weight.T, norm_params.T], 1)
+        first_shard = jnp.pad(first_shard.astype(BF16), ((0, 0), (0, fill)))
+        shards = [first_shard] + [weight.astype(BF16) for weight in masters[1:6]]
         kept = forward_plain(shards, patches, features, kinds)
     divisor = pair_total[0].astype(F32)
     gauss_low, term = render(
@@ -1521,9 +1604,14 @@
         *sums, totals = backward_all(
             kept, patches, gauss_low, term, features % LANES, wide_count, groups
         )
-        loss_sum, square_sum = totals[0, 0], totals[1, 0]
-    else:
-        sums, loss_sum, square_sum = backward_plain(kept, patches, gauss_low, term, features, kinds)
+        olds = []
+        for triple in zip(masters, firsts, seconds):
+            olds += triple
+        olds[:3] = [old.T for old in olds[:3]]
+        *news, loss, grad_norm = update_all(olds, sums, totals, pair_total, features)
+        news[:3] = [new.T for new in news[:3]]
+        return tuple(news) + (loss[0, 0], grad_norm[0, 0])
+    sums, loss_sum, square_sum = backward_plain(kept, patches, gauss_low, term, features, kinds)
     first_sum = sums[0].T
     grads = [first_sum[:features]] + list(sums[1:]) + [first_sum[features : features + kinds]]
     loss = loss_sum / divisor

time: 440 us -> 427 us (0.970)
  other arithmetic: 20.2 us -> 1.4 us
  local copies, waits for them, and re-layouts: 15.9 us -> 30 us
  Pallas kernels: 392 us -> 387 us
    unnamed x57 -> x69, local copies, waits for them, and re-layouts: 8.89 us -> 24.4 us
    sub x7 -> x0, other arithmetic: 10.2 us -> none  [adamw(): weight - rate * (first_hat / (jnp.sqrt(second_hat) + ADAM_EPS) + DECAY *...]
    convert_element_type x5 -> x0, other arithmetic: 6.28 us -> none  [body(): shards = [first_shard] + [weight.astype(BF16) for weight in masters[1:6]]]
    pallas_call x1, Pallas kernels: 222 us -> 216 us  [backward_all(): pl.pallas_call(functools.partial(backward_kernel, items, wide, narrow, le...]
    pallas_call x0 -> x1, Pallas kernels: none -> 4.48 us  [update_all(): pl.pallas_call(functools.partial(update_kernel, features), out_shape=shap...]
where the time goes in v5:
time: 427 us; the launch traced here: 421 us
  Pallas kernels  387 us (91%)
  local copies, waits for them, and re-layouts  30 us (7%)
    pallas_call x1, Pallas kernels, backward_all(): pl.pallas_call(functools.partial(backward_kernel, items, wide, narrow, le...  216 us
    pallas_call x1, Pallas kernels, forward_all(): pl.pallas_call(functools.partial(forward_kernel, items, wide, narrow, lea...  162 us
    unnamed x69, local copies, waits for them, and re-layouts  24.4 us

profile of v5, /device:TPU:0, one launch (start us, length us, event | category | flops | bytes accessed | tf_op | source)
XLA Modules:
  0.0 420.6 jit_solution(7958762525206122157)
XLA Ops:
  2.0 1.4 reduce
  4.0 0.8 pad.4.refs_7_.refs_18_
  6.5 2.3 copy.59
  9.3 161.6 %forward.1 = (bf16[1024,3072]{1,0:T(8,128)(2,1)}, bf16[1024,1024]{1,0:T(8,128)(2,1)}, bf16[1024,4096]{1,0:T(8,128)(2,1)}, bf16[4096,1024]{1,0:T(8,128)(2,1)}, bf...) custom-call(f32[32,576]{1,0:T(8,128)} %bitcast.19, ...), custom_call_target="tpu_custom_call" | custom-call | tf_op jit(solution)/shard_map/forward/pallas_call | solution.py:668
  170.9 1.1 copy-done.3
  172.0 4.9 %render.1 = (bf16[256,768]{1,0:T(8,128)(2,1)S(1)}, f32[8,128]{1,0:T(8,128)S(1)}) custom-call(f32[256,768]{1,0:T(8,128)S(1)} %copy-done.3, f32[256,768]{1,0:T(8,128)S(1)} %reshape.62.weight_ref, bf16[192,768]{1,0:T(8,128)(2,1)S(1)} %reshape.60.target_ref, s32[64,768]{1,0:T(8,128)S(1)} %reshape.61.mask_ref, s32[2,2048]{1,0:T(2,128)S(1)} %bitcast.23, ...), custom_call_target="tpu_custom_call" | custom-call | tf_op jit(solution)/shard_map/render/pallas_call | solution.py:1388
  176.9 0.7 copy-done.11
  178.3 215.8 %backward.1 = (f32[32,640]{1,0:T(8,128)}, f32[32,3072]{1,0:T(8,128)}, f32[32,1024]{1,0:T(8,128)}, f32[32,4096]{1,0:T(8,128)}, f32[128,1024]{1,0:T(8,128)}, /*index=5*/f32[32,768]{1,0:T(8,128)}, f32[8,128]{1,0:T(8,128)}) custom-call(bf16[1024,3072]{1,0:T(8,128)(2,1)} %get-tuple-element.74.refs_0_, bf16[1024,1024]{1,0:T(8,128)(2,1)} %get-tuple-element.75.refs_1_, ...), custom_call_target="tpu_custom_call" | custom-call | tf_op jit(solution)/shard_map/backward/pallas_call | solution.py:1266
  394.1 1.0 copy-done.1
  395.2 0.9 copy-done.4
  396.1 1.0 copy-done.5
  397.1 1.0 copy-done.6
  398.2 1.0 copy-done.7
  399.2 1.0 copy-done.8
  400.2 1.0 copy-done.9
  401.3 1.0 copy-done.10
  402.3 1.0 copy-done.12
  403.3 1.0 copy-done.13
  404.3 1.0 copy-done.14
  405.3 0.9 copy-done.15
  406.2 0.9 copy-done.16
  407.1 0.9 copy-done.17
  408.0 0.9 copy-done.18
  408.9 0.9 copy-done.19
  409.8 0.9 copy-done.20
  410.7 0.9 copy-done.21
  411.6 0.9 copy-done.22
  412.5 0.9 copy-done.23
  413.4 0.9 copy-done.24
  414.3 0.9 copy-done.25
  415.2 0.7 copy-done.31
  415.8 4.5 %update.1 = (f32[32,576]{1,0:T(8,128)}, f32[32,576]{1,0:T(8,128)}, f32[32,576]{1,0:T(8,128)}, f32[32,3072]{1,0:T(8,128)}, f32[32,3072]{1,0:T(8,128)}, /*index=5*...) custom-call(s32[1]{0:T(128)S(6)} %copy.64.total_ref, ...), custom_call_target="tpu_custom_call" | custom-call | tf_op jit(solution)/shard_map/update/pallas_call | solution.py:1536
  (51 shorter events, 3.4 us)
Async XLA Ops:
  0.7 4.1 copy-start.32
  0.7 3.3 copy-start.33
  8.8 162.1 %copy-start.26 = (s32[1,2,2048]{2,1,0:T(2,128)S(1)}, s32[1,2,2048]{2,1,0:T(2,128)}, u32[]{:S(2)}) copy-start(s32[1,2,2048]{2,1,0:T(2,128)} %param.32) | copy-start | bytes 49156
  170.9 1.1 copy-start.3
  176.9 0.7 copy-start.11
  178.3 215.8 %copy-start = (f32[32,4096]{1,0:T(8,128)S(1)}, f32[32,4096]{1,0:T(8,128)}, u32[]{:S(2)}) copy-start(f32[32,4096]{1,0:T(8,128)} %refs_15_.1) | copy-start | bytes 1572868
  178.3 215.8 %copy-start.2 = (f32[32,3072]{1,0:T(8,128)S(1)}, f32[32,3072]{1,0:T(8,128)}, u32[]{:S(2)}) copy-start(f32[32,3072]{1,0:T(8,128)} %refs_9_.1) | copy-start | bytes 1179652
  178.3 215.8 %copy-start.27 = (f32[6,32]{1,0:T(8,128)S(1)}, f32[6,32]{1,0:T(8,128)}, u32[]{:S(2)}) copy-start(f32[6,32]{1,0:T(8,128)} %refs_24_.1) | copy-start | bytes 2308
  178.3 215.8 %copy-start.29 = (f32[6,32]{1,0:T(8,128)S(1)}, f32[6,32]{1,0:T(8,128)}, u32[]{:S(2)}) copy-start(f32[6,32]{1,0:T(8,128)} %refs_25_.1) | copy-start | bytes 2308
  178.3 215.8 %copy-start.30 = (f32[6,32]{1,0:T(8,128)S(1)}, f32[6,32]{1,0:T(8,128)}, u32[]{:S(2)}) copy-start(f32[6,32]{1,0:T(8,128)} %refs_26_.1) | copy-start | bytes 2308
  394.1 1.0 copy-start.1
  395.2 0.9 copy-start.4
  396.1 1.0 copy-start.5
  397.1 1.0 copy-start.6
  398.2 1.0 copy-start.7
  399.2 1.0 copy-start.8
  400.2 1.0 copy-start.9
  401.3 1.0 copy-start.10
  402.3 1.0 copy-start.12
  403.3 1.0 copy-start.13
  404.3 1.0 copy-start.14
  405.3 0.9 copy-start.15
  406.2 0.9 copy-start.16
  407.1 0.9 copy-start.17
  408.0 0.9 copy-start.18
  408.9 0.9 copy-start.19
  409.8 0.9 copy-start.20
  410.7 0.9 copy-start.21
  411.6 0.9 copy-start.22
  412.5 0.9 copy-start.23
  413.4 0.9 copy-start.24
  414.3 0.9 copy-start.25
  (2 other events, 1.3 us)

commit v6 on v5

--- a/solution.py
+++ b/solution.py
@@ -232,12 +232,14 @@
             self.work(entry[1], entry[2])
 
     def finish(self):
+        self.refill()
         while self.events or self.spare:
             if not self.fill(self.events[0][0] if self.events else 1e9):
                 self.step()
 
 
 LINK = 100e3
+Z_AHEAD = 4.0
 TWIN_LINK = 600e3
 
 
@@ -277,7 +279,7 @@
     tokens = at.patches.shape[0]
     head_width = D // narrow
     total = len(items)
-    started = []
+    started, guarded = [], []
 
     def start(copy):
         copy.start()
@@ -324,15 +326,30 @@
         which, begin, width, _ = items[item]
         return weights[which].at[rows_at(which, flip(place.chip, mask), place.core), pl.ds(begin, width)]
 
-    def along(item, step):
+    def along(item, sign, hop):
         which, begin, width, _ = items[item]
+        columns = pl.ds(begin, width)
+        rows = rows_at(which, place.chip, place.core, me - sign * (hop - 1))
         return remote(
             item,
-            shards[which].at[:, pl.ds(begin, width)],
-            weights[which].at[rows_at(which, place.chip, place.core, me), pl.ds(begin, width)],
-            2 * chips + step - 1,
-            place.along(step),
-        )
+            shards[which].at[:, columns] if hop == 1 else weights[which].at[rows, columns],
+            weights[which].at[rows, columns],
+            2 * chips + hop - 1 + (narrow - 1 if sign < 0 else 0),
+            (place.w, me + sign),
+        )
+
+    def has_next(sign):
+        return me < narrow - 1 if sign > 0 else me >= 1
+
+    def has_come(sign, hop):
+        return me >= hop if sign > 0 else me < narrow - hop
+
+    def start_if(condition, copy):
+        @pl.when(condition)
+        def _():
+            copy.start()
+
+        guarded.append((condition, copy))
 
     def bits_of(item):
         return place.bits if items[item][3] == 0 else place.bits[::-1]
@@ -345,7 +362,6 @@
 
     plan = Planner()
     waited = set()
-    halves = (narrow // 2) * (narrow - narrow // 2)
 
     def block_bytes(item):
         which, _, width, _ = items[item]
@@ -371,23 +387,36 @@
         onward(item, mask, number + 1)
 
     def begin_item(item):
-        for step in range(1, narrow):
-            start(along(item, step))
-        cost = halves * 2 * block_bytes(item) / narrow / LINK
-        plan.transfer(0, cost, (item, 0), functools.partial(line_event, item))
-
-    def line_event(item):
+        for sign in (1, -1):
+            start_if(has_next(sign), along(item, sign, 1))
+        line_transfer(item, 1)
+
+    def line_transfer(item, hop):
+        cost = 2 * block_bytes(item) / narrow / LINK
+        key = (item, 0) if hop == narrow - 1 else (item, -hop)
+        plan.transfer(0, cost, key, functools.partial(line_event, item, hop))
+
+    def line_event(item, hop):
         if items[item][0] not in waited:
             waited.add(items[item][0])
             own[items[item][0]].wait()
-        for step in range(1, narrow):
-            along(item, step).wait_recv()
-        onward(item, 0, 0)
+        for sign in (1, -1):
+
+            @pl.when(has_come(sign, hop))
+            def _():
+                along(item, sign, hop).wait_recv()
+
+            if hop < narrow - 1:
+                start_if(jnp.logical_and(has_come(sign, hop), has_next(sign)), along(item, sign, hop + 1))
+        if hop < narrow - 1:
+            line_transfer(item, hop + 1)
+        else:
+            onward(item, 0, 0)
 
     begun = []
 
     def refill():
-        while len(begun) < total and plan.free.get(0, 0.0) < plan.now + 7.0:
+        while len(begun) < total and plan.free.get(0, 0.0) < plan.now + 0.5:
             begin_item(len(begun))
             begun.append(True)
 
@@ -461,7 +490,7 @@
 
     plan.work(2.0, lambda: norm_rows(embedded, 0, normed))
     turn_first = plan.later(2.0, lambda: turn(at.t1, normed))
-    piece = 2 * halves * 2 * tokens * head_width / LINK
+    piece = 2 * (narrow - 1) * 2 * tokens * head_width / LINK
 
     def project(part, step):
         owner = lax.rem(me + step, narrow)
@@ -607,6 +636,12 @@
     flush(at.t4)
     for copy in started:
         copy.wait_send()
+    for condition, copy in guarded:
+
+        @pl.when(condition)
+        def _():
+            copy.wait_send()
+
     for copy in flushed:
         copy.wait()
 
@@ -618,7 +653,7 @@
     ff = widths[3]
     head_width = D // narrow
     items = forward_plan(widths)
-    slots = wide + narrow - 1
+    slots = wide + 2 * (narrow - 1)
     full = [((height, width), BF16) for height, width in zip(heights, widths)]
     shapes = dict(
         w1=full[1],
@@ -679,10 +714,18 @@
     return Bag(zip(outs, results))
 
 
-def backward_plan(widths):
+def backward_plan(widths, pairs):
     items = []
-    for which, cuts in ((5, 1), (4, 2), (3, 2), (2, 1), (1, 3), (0, 1)):
+    for which, cuts in ((5, 1), (4, 2), (3, 2), (2, 1), (1, pairs), (0, 1)):
         size = widths[which] // cuts
+        if which == 1:
+            piece = size // 3
+            for cut in range(cuts):
+                start = cut * size
+                items += [(1, start, piece, 0), (1, start + piece, piece, 1)]
+                for side, (shift, width) in enumerate(column_halves(piece)):
+                    items.append((1, start + 2 * piece + shift, width, side))
+            continue
         for cut in range(cuts):
             for side, (start, width) in enumerate(column_halves(size)):
                 items.append((which, cut * size + start, width, side))
@@ -712,6 +755,7 @@
     tokens = src.patches.shape[0]
     head_width = D // narrow
     length = narrow * tokens
+    reach = narrow * LANES
     send_sem, recv_sem, tile_send, tile_recv = at.send_sem, at.recv_sem, at.tile_send, at.tile_recv
     swap_send, swap_recv, in_sem, ring_sem = at.swap_send, at.swap_recv, at.in_sem, at.ring_sem
     gains, norms, extra = src.gains, at.norms, at.extra
@@ -758,7 +802,7 @@
     peers += [place.along(step) for step in range(1, narrow)]
     greet(peers)
 
-    started = []
+    started, guarded = [], []
 
     def start(copy):
         copy.start()
@@ -796,7 +840,7 @@
         firsts = [((flip(place.chip, mask) * 2 + core) * narrow) * rows for mask in masks]
         with_extra = which == 0 and begin + width == right.shape[1]
         assert not with_extra or tile == width
-        part, begin = (begin // D, begin % D) if which == 1 else (None, begin)
+        part, begin = (begin // reach, begin % reach) if which == 1 else (None, begin)
 
         def one(step, carry):
             offset = pl.multiple_of(begin + step * tile, LANES)
@@ -804,7 +848,7 @@
             if part is None:
                 rhs = right[:, pl.ds(offset, tile)]
             else:
-                rhs = right[part, :, pl.ds(offset, tile)]
+                rhs = right[part // 3, part % 3, :, pl.ds(offset, tile)]
             spots = [pl.ds(pl.multiple_of(first, span), span) for first in firsts]
             lhs = jnp.concatenate([left[spot, :] for spot in spots], 0)
             value = jnp.dot(lhs, rhs, preferred_element_type=F32)
@@ -823,7 +867,6 @@
 
     last_sent = {}
     plan = Planner()
-    halves = (narrow // 2) * (narrow - narrow // 2)
 
     def to_twin(item, masks):
         which, _, width, _ = items[item]
@@ -836,15 +879,56 @@
             item, held[item].at[mask], passed[item][number].at[slot], chips + mask, place.across(bit)
         )
 
-    def along(item, step):
-        target = place.along(step)
+    def along(item, sign, hop):
+        count = narrow - hop
+        first = hop if sign > 0 else 0
+        node = hop if sign > 0 else narrow - 1 - hop
         return remote(
             item,
-            held[item].at[0, target[1]],
-            final[item].at[narrow - step - 1],
-            2 * chips + narrow - step - 1,
-            target,
-        )
+            held[item].at[0, pl.ds(first, count)],
+            final[item].at[pl.ds(first + (1 if sign > 0 else 0), count)],
+            2 * chips + (0 if sign > 0 else 1),
+            (place.w, node),
+        )
+
+    def send_along(item, sign, hop):
+        sender = me == (hop - 1 if sign > 0 else narrow - hop)
+
+        @pl.when(sender)
+        def _():
+            along(item, sign, hop).start()
+
+        guarded.append((sender, along(item, sign, hop)))
+
+    def line_event(item, hop):
+        for sign in (1, -1):
+            count = narrow - hop - 1
+            first = hop + 1 if sign > 0 else 0
+
+            @pl.when(me == (hop if sign > 0 else narrow - 1 - hop))
+            def _():
+                along(item, sign, hop).wait_recv()
+
+                def one(step, carry):
+                    spot = first + step
+                    value = held[item][0, spot].astype(F32)
+                    value = value + final[item][spot + (1 if sign > 0 else 0)].astype(F32)
+                    held[item][0, spot] = value.astype(BF16)
+                    return carry
+
+                if count:
+                    lax.fori_loop(0, count, one, 0)
+
+            if count:
+                send_along(item, sign, hop + 1)
+        line_transfer(item, hop + 1)
+
+    def line_transfer(item, hop):
+        cost = (narrow - hop) * 2 * block_bytes(item) / narrow / LINK
+        event = line_event if hop < narrow else finish
+        if hop == narrow:
+            return finish(item)
+        plan.transfer(0 if hop == 1 else 100 + hop, cost, (item, -hop, 0), functools.partial(event, item, hop))
 
     def leaves(item, mask):
         bits = bits_of(item)
@@ -867,9 +951,9 @@
         which, _, width, _ = items[item]
         return 2 * spare[which].shape[1] * spare[which].shape[2] * width
 
-    def push(which, part=None):
+    def push(which, pair=None):
         for item, (owner, begin, _, _) in enumerate(items):
-            if owner != which or (part is not None and begin // D != part):
+            if owner != which or (pair is not None and begin // (3 * reach) != pair):
                 continue
             for masks in groups_of(item):
                 cost = len(masks) * block_bytes(item) / 1e6
@@ -897,10 +981,8 @@
     def onward(item, mask, number):
         bits = bits_of(item)
         if number == len(bits):
-            for step in range(1, narrow):
-                start(along(item, step))
-            cost = halves * 2 * block_bytes(item) / narrow / LINK
-            plan.transfer(0, cost, (item, -1, 0), functools.partial(finish, item))
+            lined.append(item)
+            refill()
         elif leaves(item, mask) == number:
             kept = mask ^ bits[number]
             start(across(item, mask, bits[number], number, slot_of(item, kept, number)))
@@ -911,6 +993,17 @@
                 functools.partial(sum_event, item, kept, number),
             )
 
+    lined = []
+
+    def refill():
+        while lined and plan.free.get(0, 0.0) < plan.now + Z_AHEAD:
+            item = lined.pop(0)
+            for sign in (1, -1):
+                send_along(item, sign, 1)
+            line_transfer(item, 1)
+
+    plan.refill = refill
+
     def sum_event(item, mask, number):
         plan.need([(item, before, mask) for before in range(number + 1)])
         bit = bits_of(item)[number]
@@ -924,12 +1017,25 @@
 
     def finish(item):
         which, begin, width, _ = items[item]
-        value = held[item][0, me].astype(F32)
-        for step in range(1, narrow):
-            along(item, step).wait_recv()
-        for slot in range(narrow - 1):
-            value = value + final[item][slot].astype(F32)
-        sums[which][:, pl.ds(begin, width)] = value
+        acc = at.acc.at[pl.ds(0, held[item].shape[2]), pl.ds(0, width)]
+        acc[...] = held[item][0, me].astype(F32)
+
+        @pl.when(me >= 1)
+        def _():
+            acc[...] += final[item][me + 1].astype(F32)
+
+        @pl.when(me < narrow - 1)
+        def _():
+            acc[...] += final[item][me].astype(F32)
+
+        value = acc[...]
+        if which == 1:
+            for shift in range(0, width, LANES):
+                part, spot = (begin + shift) // reach, (begin + shift) % reach
+                column = part % 3 * D + spot // LANES * head_width + part // 3 * LANES
+                sums[which][:, pl.ds(column, LANES)] = value[:, shift : shift + LANES]
+        else:
+            sums[which][:, pl.ds(begin, width)] = value
         squares.append(jnp.sum(value * value))
 
     norms[...] = jnp.zeros_like(norms)
@@ -958,8 +1064,7 @@
         lax.fori_loop(0, tokens // step_rows, one, 0)
 
     load(at.t5).wait()
-    push(5)
-    plan.now += 3.0
+    plan.now += 5.0
     load_stash(src.last).wait()
     count = D // u_rows
     tall_rows = slope_rows
@@ -982,8 +1087,6 @@
     norm_back(2, shrink_low, False)
     load_stash(src.mid).start()
     load(at.t4).wait()
-    plan.now += 3.0
-    push(4)
     ff = src.w3.shape[1]
     slabs = ff // tall_rows
 
@@ -1008,7 +1111,6 @@
         ring(src.w2, at.tall, head_width, D, index, owners[index] * head_width).start()
     load(at.t3).wait()
     plan.now += 6.0
-    push(3)
 
     def through_expand(index, carry):
         ring(src.w3, at.long, 128, ff, index, index * 128).wait()
@@ -1040,7 +1142,7 @@
 
     d_heads, away = at.d_heads, at.away
     plan.now += 7.0
-    piece = 2 * halves * 2 * tokens * head_width / LINK
+    piece = 2 * (narrow - 1) * 2 * tokens * head_width / LINK
 
     def head_event():
         for step in range(1, narrow):
@@ -1059,7 +1161,8 @@
     plan.now += 3.0
     plan.transfer(0, piece, (-1, 0, 0), head_event)
     load(at.t2).wait()
-    push(2)
+    for which in (5, 4, 3, 2):
+        push(which)
     load(at.qkv).wait()
     load(at.heads_out).wait()
     load(at.log_sums).wait()
@@ -1079,10 +1182,13 @@
         who = lax.rem(me + step, narrow)
         return swap(
             parts.at[who, :, :, lanes],
-            mixed.at[:, :, pl.ds(pl.multiple_of(me * head_width + pair * LANES, LANES), LANES)],
+            mixed.at[pair, :, :, pl.ds(pl.multiple_of(me * LANES, LANES), LANES)],
             1 + pair,
             step,
         )
+
+    pushed_pairs = []
+    load(at.t1).wait()
 
     def part_event(pair):
         for step in range(1, narrow):
@@ -1129,6 +1235,10 @@
             parts[who, 0, :, lanes] = query_acc[...].T.astype(BF16)
         for step in range(narrow):
             plan.work(3.0, functools.partial(one_block, step))
+            for earlier in range(pair):
+                if earlier not in pushed_pairs and (-2, 0, earlier) in plan.done:
+                    pushed_pairs.append(earlier)
+                    push(1, earlier)
         for source in range(narrow):
             rows = pl.ds(source * tokens, tokens)
             parts[source, 1, :, lanes] = key_acc[rows, :].astype(BF16)
@@ -1137,18 +1247,21 @@
             start(part_swap(pair, step))
         plan.now += 1.0
         plan.transfer(0, 1.5 * piece, (-2, 0, pair), functools.partial(part_event, pair))
-        mixed[:, :, pl.ds(pl.multiple_of(me * head_width + pair * LANES, LANES), LANES)] = parts[me, :, :, lanes]
-    load(at.t1).wait()
-    plan.need([(-2, 0, pair) for pair in range(head_width // LANES)])
-    for part in range(3):
-        push(1, part)
+        mixed[pair, :, :, pl.ds(pl.multiple_of(me * LANES, LANES), LANES)] = parts[me, :, :, lanes]
+    for pair in range(head_width // LANES):
+        if pair not in pushed_pairs:
+            plan.need([(-2, 0, pair)])
+            push(1, pair)
 
     def through_mixer(index, carry):
         ring(src.w1, at.long, 128, 3 * D, index, index * 128).wait()
         slot = lax.rem(index, 2)
-        value = back_mul(mixed[0], at.long[slot, :, 0:D])
-        for part in range(1, 3):
-            value = value + back_mul(mixed[part], at.long[slot, :, part * D : (part + 1) * D])
+        value = jnp.zeros((tokens, 128), F32)
+        for pair in range(head_width // LANES):
+            for part in range(3):
+                columns = [part * D + owner * head_width + pair * LANES for owner in range(narrow)]
+                weight = [at.long[slot, :, column : column + LANES] for column in columns]
+                value = value + back_mul(mixed[pair, part], jnp.concatenate(weight, 1))
         d_norm[:, pl.ds(pl.multiple_of(index * 128, 128), 128)] = value
 
         @pl.when(index + 2 < D // 128)
@@ -1198,6 +1311,11 @@
     totals[...] = whole
     for copy in list(last_sent.values()) + started:
         copy.wait_send()
+    for condition, copy in guarded:
+
+        @pl.when(condition)
+        def _():
+            copy.wait_send()
 
 
 def backward_all(kept, patches, gauss, term, lead, wide, narrow):
@@ -1209,8 +1327,8 @@
     rows = [height // (wide * narrow) for height in heights]
     head_width = D // narrow
     length = narrow * tokens
-    items = backward_plan(widths)
-    slots = 2 * chips + narrow - 1
+    items = backward_plan(widths, head_width // LANES)
+    slots = 2 * chips + 2
     streamed = dict(w1=kept.w1, w2=kept.w2, w3=kept.w3, w4=kept.w4, w5=kept.w5)
     streamed.update(last=kept.last, mid=kept.mid, embedded=kept.embedded, slopes=kept.slopes)
     loaded = dict(t5=kept.t5, t4=kept.t4, t3=kept.t3, t2=kept.t2, t1=kept.t1)
@@ -1221,6 +1339,7 @@
     shapes.append(jax.ShapeDtypeStruct((8, LANES), F32))
     scratch = {name: pltpu.VMEM(value.shape, value.dtype) for name, value in loaded.items()}
     scratch.update(
+        acc=pltpu.VMEM((max(rows), max(width for _, _, width, _ in items)), F32),
         embed_t=pltpu.VMEM((D, tokens), BF16),
         embed_low=pltpu.VMEM((tokens, D), BF16),
         stash=pltpu.VMEM((tokens, D), F32),
@@ -1231,7 +1350,7 @@
         shrink_low=pltpu.VMEM((tokens, D), BF16),
         expand_low=pltpu.VMEM((tokens, widths[3]), BF16),
         merge_low=pltpu.VMEM((tokens, D), BF16),
-        mixed=pltpu.VMEM((3, tokens, D), BF16),
+        mixed=pltpu.VMEM((head_width // LANES, 3, tokens, narrow * LANES), BF16),
         tall=pltpu.VMEM((2, 512, D), BF16),
         long=pltpu.VMEM((2, 128, widths[3]), BF16),
         slope_slots=pltpu.VMEM((2, tokens, 512), BF16),
@@ -1257,7 +1376,7 @@
     for which, _, width, _ in items:
         for bit in chip_bits(chips):
             lists.append(pltpu.VMEM((chips // (2 * bit), narrow, rows[which], width), BF16))
-    lists += [pltpu.VMEM((narrow - 1, rows[which], width), BF16) for which, _, width, _ in items]
+    lists += [pltpu.VMEM((narrow + 1, rows[which], width), BF16) for which, _, width, _ in items]
     for which in range(6):
         widest = max(width for owner, _, width, _ in items if owner == which)
         lists.append(pltpu.VMEM((chips, narrow, rows[which], widest), BF16))
@@ -1498,17 +1617,28 @@
 
 
 def update_kernel(features, total_ref, sums_ref, *refs):
-    grads, refs = refs[:6], refs[6:]
-    olds, news = refs[:21], refs[21:42]
-    loss_ref, norm_ref, turned = refs[42:]
+    sources, targets, refs = refs[:27], refs[27:48], refs[48:]
+    loss_ref, norm_ref, refs = refs[0], refs[1], refs[2:]
+    inside, news, refs = refs[:27], refs[27:48], refs[48:]
+    turned, in_sem, out_sem = refs
+    loads = [pltpu.make_async_copy(source, dest, in_sem.at[i]) for i, (source, dest) in enumerate(zip(sources, inside))]
+    stores = [pltpu.make_async_copy(source, dest, out_sem.at[i]) for i, (source, dest) in enumerate(zip(news, targets))]
+    for copy in loads:
+        copy.start()
+    grads, olds = inside[:6], inside[6:]
     square_sum = sums_ref[1:2, 0:1]
     grad_norm = jnp.sqrt(square_sum)
     factor = jnp.minimum(1.0, CLIP_NORM / (grad_norm + 1e-06))
     norm_ref[...] = grad_norm
     loss_ref[...] = sums_ref[0:1, 0:1] / total_ref[0].astype(F32)
     width = grads[0].shape[1]
-    turned[...] = grads[0][:, width - LANES :].T
     for which in range(7):
+        if which < 6:
+            loads[which].wait()
+        if which == 0:
+            turned[...] = grads[0][:, width - LANES :].T
+        for copy in loads[6 + 3 * which : 9 + 3 * which]:
+            copy.wait()
         weight, first, second = olds[3 * which : 3 * which + 3]
         rows, columns = weight.shape
         chunk = min(8, rows)
@@ -1527,19 +1657,31 @@
             return carry
 
         lax.fori_loop(0, rows // chunk, one, 0)
+        for copy in stores[3 * which : 3 * which + 3]:
+            copy.start()
+    for copy in stores:
+        copy.wait()
 
 
 def update_all(olds, sums, totals, pair_total, features):
     vmem = pl.BlockSpec(memory_space=pltpu.VMEM)
     smem = pl.BlockSpec(memory_space=pltpu.SMEM)
+    hbm = pl.BlockSpec(memory_space=pltpu.HBM)
     shapes = [jax.ShapeDtypeStruct(old.shape, F32) for old in olds]
+    inside = [pltpu.VMEM(value.shape, F32) for value in list(sums) + list(olds)]
     return pl.pallas_call(
         functools.partial(update_kernel, features),
         out_shape=shapes + [jax.ShapeDtypeStruct((1, 1), F32)] * 2,
-        in_specs=[smem] + [vmem] * 28,
-        out_specs=[vmem] * 23,
-        scratch_shapes=[pltpu.VMEM((LANES, sums[0].shape[0]), F32)],
-        compiler_params=pltpu.CompilerParams(vmem_limit_bytes=40 * MIB),
+        in_specs=[smem, vmem] + [hbm] * 27,
+        out_specs=[hbm] * 21 + [vmem] * 2,
+        scratch_shapes=inside
+        + [pltpu.VMEM(old.shape, F32) for old in olds]
+        + [
+            pltpu.VMEM((LANES, sums[0].shape[0]), F32),
+            pltpu.SemaphoreType.DMA((27,)),
+            pltpu.SemaphoreType.DMA((21,)),
+        ],
+        compiler_params=pltpu.CompilerParams(vmem_limit_bytes=60 * MIB),
         name="update",
     )(pair_total, totals, *sums, *olds)
 

time: 427 us -> 363 us (0.85)
  Pallas kernels: 387 us -> 346 us
  local copies, waits for them, and re-layouts: 30 us -> 8.28 us
    pallas_call x1, Pallas kernels: 216 us -> 189 us  [backward_all(): pl.pallas_call(functools.partial(backward_kernel, items, wide, narrow, le...]
    unnamed x69 -> x13, local copies, waits for them, and re-layouts: 24.4 us -> 2.7 us
    pallas_call x1, Pallas kernels: 162 us -> 145 us  [forward_all(): pl.pallas_call(functools.partial(forward_kernel, items, wide, narrow, lea...]
where the time goes in v6:
time: 363 us; the launch traced here: 358 us
  Pallas kernels  346 us (95%)
  local copies, waits for them, and re-layouts  8.28 us (2%)
    pallas_call x1, Pallas kernels, backward_all(): pl.pallas_call(functools.partial(backward_kernel, items, wide, narrow, le...  189 us
    pallas_call x1, Pallas kernels, forward_all(): pl.pallas_call(functools.partial(forward_kernel, items, wide, narrow, lea...  145 us

profile of v6, /device:TPU:0, one launch (start us, length us, event | category | flops | bytes accessed | tf_op | source)
XLA Modules:
  0.0 358.0 jit_solution(5531471363832047673)
XLA Ops:
  0.7 0.0 copy-start.4
  0.7 0.0 copy-start.5
  2.0 1.4 reduce
  3.4 0.2 reshape_squeeze.7
  3.6 0.2 copy.62
  3.8 0.1 reshape.61.mask_ref
  4.0 0.0 copy-done.5
  4.0 0.8 pad.4.refs_7_.refs_18_
  4.8 0.0 copy-done.4
  4.8 0.2 copy.55
  5.0 0.6 reshape_squeeze.6
  5.6 0.4 copy.56
  6.0 0.4 reshape.60.target_ref
  6.5 2.3 copy.59
  8.8 0.0 copy-start.2
  8.8 0.5 reshape.62.weight_ref
  9.3 145.3 %forward.1 = (bf16[1024,3072]{1,0:T(8,128)(2,1)}, bf16[1024,1024]{1,0:T(8,128)(2,1)}, bf16[1024,4096]{1,0:T(8,128)(2,1)}, bf16[4096,1024]{1,0:T(8,128)(2,1)}, bf...) custom-call(f32[32,576]{1,0:T(8,128)} %bitcast.24, ...), custom_call_target="tpu_custom_call" | custom-call | tf_op jit(solution)/shard_map/forward/pallas_call | solution.py:703
  154.6 0.0 copy-done.2
  154.6 0.0 copy-start
  154.6 1.1 copy-done
  155.7 4.9 %render.1 = (bf16[256,768]{1,0:T(8,128)(2,1)S(1)}, f32[8,128]{1,0:T(8,128)S(1)}) custom-call(f32[256,768]{1,0:T(8,128)S(1)} %copy-done, f32[256,768]{1,0:T(8,128)S(1)} %reshape.62.weight_ref, bf16[192,768]{1,0:T(8,128)(2,1)S(1)} %reshape.60.target_ref, s32[64,768]{1,0:T(8,128)S(1)} %reshape.61.mask_ref, s32[2,2048]{1,0:T(2,128)S(1)} %bitcast.19, ...), custom_call_target="tpu_custom_call" | custom-call | tf_op jit(solution)/shard_map/render/pallas_call | solution.py:1507
  160.6 0.0 copy-start.1
  160.6 0.7 copy-done.1
  161.3 0.0 copy-start.3
  161.3 0.6 copy-done.3
  161.9 189.2 %backward.1 = (f32[32,640]{1,0:T(8,128)}, f32[32,3072]{1,0:T(8,128)}, f32[32,1024]{1,0:T(8,128)}, f32[32,4096]{1,0:T(8,128)}, f32[128,1024]{1,0:T(8,128)}, /*index=5*/f32[32,768]{1,0:T(8,128)}, f32[8,128]{1,0:T(8,128)}) custom-call(bf16[1024,3072]{1,0:T(8,128)(2,1)} %get-tuple-element.74.refs_0_, bf16[1024,1024]{1,0:T(8,128)(2,1)} %get-tuple-element.75.refs_1_, ...), custom_call_target="tpu_custom_call" | custom-call | tf_op jit(solution)/shard_map/backward/pallas_call | solution.py:1385
  351.1 6.6 %update.1 = (f32[32,576]{1,0:T(8,128)}, f32[32,576]{1,0:T(8,128)}, f32[32,576]{1,0:T(8,128)}, f32[32,3072]{1,0:T(8,128)}, f32[32,3072]{1,0:T(8,128)}, /*index=5*...) custom-call(s32[1]{0:T(128)S(6)} %copy.64.total_ref, ...), custom_call_target="tpu_custom_call" | custom-call | tf_op jit(solution)/shard_map/update/pallas_call | solution.py:1672
Async XLA Ops:
  0.7 4.1 %copy-start.4 = (bf16[1,12,3,4096]{3,2,1,0:T(4,128)(2,1)S(1)}, bf16[1,12,3,4096]{3,2,1,0:T(4,128)(2,1)}, u32[]{:S(2)}) copy-start(bf16[1,12,3,4096]{3,2,1,0:T(4,128)(2,1)} %param.30) | copy-start | bytes 884740
  0.7 3.3 copy-start.5
  8.8 145.8 %copy-start.2 = (s32[1,2,2048]{2,1,0:T(2,128)S(1)}, s32[1,2,2048]{2,1,0:T(2,128)}, u32[]{:S(2)}) copy-start(s32[1,2,2048]{2,1,0:T(2,128)} %param.32) | copy-start | bytes 49156
  154.6 1.1 copy-start
  160.6 0.7 copy-start.1
  161.3 0.6 copy-start.3

commit v7 on v6

--- a/solution.py
+++ b/solution.py
@@ -477,7 +477,7 @@
     flush(embedded)
 
     def norm_rows(source, row, dest):
-        step_rows = 64
+        step_rows = 32
 
         def one(step, carry):
             rows = pl.ds(pl.multiple_of(step * step_rows, step_rows), step_rows)
@@ -512,47 +512,60 @@
             plan.work(0.7, functools.partial(project, part, step))
         plan.transfer(0, piece, (-1, part), functools.partial(swap_event, part))
     flush(at.w1)
-    plan.need([(-1, part) for part in range(3)])
-    flush(qkv)
-    plan.need([(-1, 2)])
-
     lane = lax.broadcasted_iota(jnp.int32, (1, LANES), 1)
     scale = HD ** (-0.5)
     length = narrow * tokens
-
-    def attend(step):
+    sides = LANES // HD
+
+    def weigh(step):
         who = lax.rem(me + step, narrow)
         log_sums = jnp.zeros((tokens, LANES), F32)
+        sums = jnp.ones((tokens, LANES), F32)
         for pair in range(head_width // LANES):
             lanes = pl.ds(pair * LANES, LANES)
             query = qkv[who, 0, :, lanes].astype(F32)
             key = qkv[:, 1, :, lanes].reshape(length, LANES)
-            value = qkv[:, 2, :, lanes].reshape(length, LANES)
-            out = jnp.zeros((tokens, LANES), F32)
-            for side in range(LANES // HD):
-                inside = lane // HD == side
-                own_query = (query * jnp.where(inside, scale, 0.0)).astype(BF16)
+            for side in range(sides):
+                head = pair * sides + side
+                own_query = (query * jnp.where(lane // HD == side, scale, 0.0)).astype(BF16)
                 scores = back_mul(own_query, key)
                 highest = jnp.max(scores, -1, keepdims=True)
                 exponentials = jnp.exp(scores - highest)
                 summed = jnp.sum(exponentials, -1, keepdims=True)
-                part = matmul(exponentials.astype(BF16), value) / summed
-                out = jnp.where(inside, part, out)
-                log_sums = jnp.where(
-                    lane == pair * (LANES // HD) + side, highest + jnp.log(summed), log_sums
-                )
+                at.weighed[step, head] = exponentials.astype(BF16)
+                log_sums = jnp.where(lane == head, highest + jnp.log(summed), log_sums)
+                sums = jnp.where(lane == head, summed, sums)
+        at.log_sums[who] = log_sums
+        at.weigh_sums[step] = sums
+
+    def attend(step):
+        who = lax.rem(me + step, narrow)
+        for pair in range(head_width // LANES):
+            lanes = pl.ds(pair * LANES, LANES)
+            value = qkv[:, 2, :, lanes].reshape(length, LANES)
+            out = jnp.zeros((tokens, LANES), F32)
+            for side in range(sides):
+                head = pair * sides + side
+                part = matmul(at.weighed[step, head], value) / at.weigh_sums[step, :, head : head + 1]
+                out = jnp.where(lane // HD == side, part, out)
             heads_out[who, :, lanes] = out.astype(BF16)
-        at.log_sums[who] = log_sums
         if step:
             start(swap(heads_out.at[who], returned.at[me], 3, step))
         else:
             returned[me] = heads_out[who]
 
+    steps = list(range(1, narrow)) + [0]
+    plan.need([(-1, 0), (-1, 1)])
+    for step in steps:
+        plan.work(2.7, functools.partial(weigh, step))
+    plan.need([(-1, 2)])
+    flush(qkv)
+
     def return_event(step):
         return lambda: swap(heads_out.at[me], returned.at[me], 3, step).wait_recv()
 
-    for step in list(range(1, narrow)) + [0]:
-        plan.work(3.5, functools.partial(attend, step))
+    for step in steps:
+        plan.work(0.9, functools.partial(attend, step))
         if step:
             plan.transfer(0, piece / (narrow - 1), (-2, step), return_event(step))
     flush(heads_out)
@@ -600,15 +613,12 @@
 
         lax.fori_loop(0, tokens // 32, bend, 0)
 
-    def turn_hidden(block):
-        at.t4[pl.ds(block, tile), :] = hidden[:, pl.ds(block, tile)].T
-
     for block in range(0, ff, tile):
         need(3, (block, block + tile))
         plan.work(2.5, functools.partial(expand, block))
-        plan.later(1.0, functools.partial(turn_hidden, block))
     flush(at.w3)
     flush(slopes)
+    flush(hidden)
 
     def shrink(block):
         cols = pl.ds(block, 256)
@@ -633,7 +643,6 @@
     flush(at.gaussians)
     plan.later(2.0, lambda: turn(at.t5, normed))
     plan.finish()
-    flush(at.t4)
     for copy in started:
         copy.wait_send()
     for condition, copy in guarded:
@@ -669,7 +678,7 @@
         t1=((D, tokens), BF16),
         t2=((D, tokens), BF16),
         t3=((D, tokens), BF16),
-        t4=((ff, tokens), BF16),
+        hidden=((tokens, ff), BF16),
         t5=((D, tokens), BF16),
         qkv=((narrow, 3, tokens, head_width), BF16),
         heads_out=((narrow, tokens, head_width), BF16),
@@ -687,9 +696,10 @@
         c4=pltpu.VMEM(shards[4].shape, BF16),
         c5=pltpu.VMEM(shards[5].shape, BF16),
         normed=pltpu.VMEM((tokens, D), BF16),
-        hidden=pltpu.VMEM((tokens, ff), BF16),
         wave=pltpu.VMEM((tokens, 512), F32),
         away=pltpu.VMEM((narrow - 1, 3, tokens, head_width), BF16),
+        weighed=pltpu.VMEM((narrow, head_width // HD, tokens, narrow * tokens), BF16),
+        weigh_sums=pltpu.VMEM((narrow, tokens, LANES), F32),
         returned=pltpu.VMEM((narrow, tokens, head_width), BF16),
         own_sem=pltpu.SemaphoreType.DMA((6,)),
         send_sem=pltpu.SemaphoreType.DMA((len(items), slots)),
@@ -772,7 +782,7 @@
         return pltpu.make_async_copy(ref, stash, in_sem.at[len(loaded)])
 
     def ring(ref, slots, rows, columns, index, row):
-        slot = lax.rem(index, 2)
+        slot = lax.rem(index, slots.shape[0])
         return pltpu.make_async_copy(
             ref.at[pl.ds(pl.multiple_of(row, rows), rows), :],
             slots.at[slot, pl.ds(0, rows), pl.ds(0, columns)],
@@ -780,9 +790,10 @@
         )
 
     slope_rows = at.tall.shape[1]
+    tall, long = at.tall.shape[0], at.long.shape[0]
 
     def slope_load(index):
-        slot = lax.rem(index, 2)
+        slot = lax.rem(index, tall)
         return pltpu.make_async_copy(
             src.slopes.at[:, pl.ds(pl.multiple_of(index * slope_rows, slope_rows), slope_rows)],
             at.slope_slots.at[slot],
@@ -791,9 +802,10 @@
 
     u_rows, u_cols = 256, src.w5.shape[1]
     load_stash(src.last).start()
-    for index in range(2):
+    for index in range(tall):
         ring(src.w5, at.tall, u_rows, u_cols, index, index * u_rows).start()
         slope_load(index).start()
+    for index in range(long):
         ring(src.w3, at.long, 128, src.w3.shape[1], index, index * 128).start()
     for name in loaded:
         load(vars(at)[name]).start()
@@ -808,8 +820,8 @@
         copy.start()
         started.append(copy)
 
-    lefts = [at.embed_t, at.t1, at.t2, at.t3, at.t4, at.t5]
-    rights = [src.patches, mixed, merge_low, expand_low, shrink_low, src.gauss]
+    lefts = [at.embed_t, at.t1, at.t2, at.t3, at.shrink_t, at.t5]
+    rights = [src.patches, mixed, merge_low, expand_low, at.hidden, src.gauss]
 
     def remote(item, src, dst, slot, peer):
         return pltpu.make_async_remote_copy(
@@ -826,6 +838,8 @@
 
     def groups_of(item):
         size = max(1, 512 // (narrow * spare[items[item][0]].shape[2]))
+        if items[item][0] == 4:
+            size = chips
         masks = list(range(chips))
         if bits_of(item) and bits_of(item)[0] > 1:
             masks = masks[chips // 2 :] + masks[: chips // 2]
@@ -837,6 +851,18 @@
         rows = into.shape[-2]
         span = narrow * rows
         tile = tile_of(width)
+        if which == 4:
+            size = into.shape[-1]
+            for mask in masks:
+                column = ((flip(place.chip, mask) * 2 + core) * narrow) * size
+                rhs = right[:, pl.ds(pl.multiple_of(column, narrow * size), narrow * size)]
+                value = jnp.dot(left[begin : begin + width, :], rhs, preferred_element_type=F32)
+                for node in range(narrow):
+                    piece = value[:, node * size : (node + 1) * size]
+                    if plus:
+                        piece = piece + into[mask, node].astype(F32)
+                    into[mask, node] = piece.astype(BF16)
+            return
         firsts = [((flip(place.chip, mask) * 2 + core) * narrow) * rows for mask in masks]
         with_extra = which == 0 and begin + width == right.shape[1]
         assert not with_extra or tile == width
@@ -871,7 +897,7 @@
     def to_twin(item, masks):
         which, _, width, _ = items[item]
         some = pl.ds(masks[0], len(masks))
-        own = spare[which].at[some, :, :, pl.ds(0, width)]
+        own = spare[which].at[some] if which == 4 else spare[which].at[some, :, :, pl.ds(0, width)]
         return remote(item, own, held[item].at[some], masks[0], place.twin)
 
     def across(item, mask, bit, number, slot):
@@ -940,16 +966,11 @@
         return kept.index(mask)
 
     def add_into(dest, dest_at, src, src_at):
-        def one(step, carry):
-            value = dest[dest_at, step].astype(F32) + src[src_at, step].astype(F32)
-            dest[dest_at, step] = value.astype(BF16)
-            return carry
-
-        lax.fori_loop(0, narrow, one, 0)
+        dest[dest_at] = (dest[dest_at].astype(F32) + src[src_at].astype(F32)).astype(BF16)
 
     def block_bytes(item):
-        which, _, width, _ = items[item]
-        return 2 * spare[which].shape[1] * spare[which].shape[2] * width
+        _, nodes, rows, width = held[item].shape
+        return 2 * nodes * rows * width
 
     def push(which, pair=None):
         for item, (owner, begin, _, _) in enumerate(items):
@@ -1017,7 +1038,7 @@
 
     def finish(item):
         which, begin, width, _ = items[item]
-        acc = at.acc.at[pl.ds(0, held[item].shape[2]), pl.ds(0, width)]
+        acc = at.acc.at[pl.ds(0, held[item].shape[2]), pl.ds(0, held[item].shape[3])]
         acc[...] = held[item][0, me].astype(F32)
 
         @pl.when(me >= 1)
@@ -1034,6 +1055,8 @@
                 part, spot = (begin + shift) // reach, (begin + shift) % reach
                 column = part % 3 * D + spot // LANES * head_width + part // 3 * LANES
                 sums[which][:, pl.ds(column, LANES)] = value[:, shift : shift + LANES]
+        elif which == 4:
+            sums[which][pl.ds(begin, width), :] = value
         else:
             sums[which][:, pl.ds(begin, width)] = value
         squares.append(jnp.sum(value * value))
@@ -1041,7 +1064,7 @@
     norms[...] = jnp.zeros_like(norms)
 
     def norm_back(row, low, add):
-        step_rows = 64
+        step_rows = 32
 
         def one(step, carry):
             rows = pl.ds(pl.multiple_of(step * step_rows, step_rows), step_rows)
@@ -1071,43 +1094,43 @@
 
     def through_unpatch(index, carry):
         ring(src.w5, at.tall, u_rows, u_cols, index, index * u_rows).wait()
-        slot = at.tall.at[lax.rem(index, 2)]
+        slot = at.tall.at[lax.rem(index, tall)]
         offset = pl.multiple_of(index * u_rows, u_rows)
         d_norm[:, pl.ds(offset, u_rows)] = back_mul(src.gauss[...], slot[0:u_rows, 0:u_cols])
 
-        @pl.when(index + 2 < count)
+        @pl.when(index + tall < count)
         def _():
-            ring(src.w5, at.tall, u_rows, u_cols, index + 2, (index + 2) * u_rows).start()
+            ring(src.w5, at.tall, u_rows, u_cols, index + tall, (index + tall) * u_rows).start()
 
         return carry
 
     lax.fori_loop(0, count, through_unpatch, 0)
-    for index in range(2):
+    for index in range(tall):
         ring(src.w4, at.tall, tall_rows, D, index, index * tall_rows).start()
     norm_back(2, shrink_low, False)
     load_stash(src.mid).start()
-    load(at.t4).wait()
+    load(at.hidden).wait()
     ff = src.w3.shape[1]
     slabs = ff // tall_rows
 
     def through_shrink(index, carry):
         ring(src.w4, at.tall, tall_rows, D, index, index * tall_rows).wait()
         slope_load(index).wait()
-        slot = lax.rem(index, 2)
+        slot = lax.rem(index, tall)
         value = back_mul(shrink_low[...], at.tall[slot])
         value = value * at.slope_slots[slot].astype(F32)
         expand_low[:, pl.ds(pl.multiple_of(index * tall_rows, tall_rows), tall_rows)] = value.astype(BF16)
 
-        @pl.when(index + 2 < slabs)
+        @pl.when(index + tall < slabs)
         def _():
-            ring(src.w4, at.tall, tall_rows, D, index + 2, (index + 2) * tall_rows).start()
-            slope_load(index + 2).start()
+            ring(src.w4, at.tall, tall_rows, D, index + tall, (index + tall) * tall_rows).start()
+            slope_load(index + tall).start()
 
         return carry
 
     lax.fori_loop(0, slabs, through_shrink, 0)
     owners = [lax.rem(me + step, narrow) for step in list(range(1, narrow)) + [0]]
-    for index in range(2):
+    for index in range(min(tall, narrow)):
         ring(src.w2, at.tall, head_width, D, index, owners[index] * head_width).start()
     load(at.t3).wait()
     plan.now += 6.0
@@ -1115,16 +1138,16 @@
     def through_expand(index, carry):
         ring(src.w3, at.long, 128, ff, index, index * 128).wait()
         offset = pl.multiple_of(index * 128, 128)
-        d_norm[:, pl.ds(offset, 128)] = back_mul(expand_low[...], at.long[lax.rem(index, 2)])
-
-        @pl.when(index + 2 < D // 128)
+        d_norm[:, pl.ds(offset, 128)] = back_mul(expand_low[...], at.long[lax.rem(index, long)])
+
+        @pl.when(index + long < D // 128)
         def _():
-            ring(src.w3, at.long, 128, ff, index + 2, (index + 2) * 128).start()
+            ring(src.w3, at.long, 128, ff, index + long, (index + long) * 128).start()
 
         return carry
 
     lax.fori_loop(0, D // 128, through_expand, 0)
-    for index in range(2):
+    for index in range(long):
         ring(src.w1, at.long, 128, 3 * D, index, index * 128).start()
     load_stash(src.mid).wait()
     norm_back(1, merge_low, True)
@@ -1150,18 +1173,21 @@
 
     for index, owner in enumerate(owners):
         ring(src.w2, at.tall, head_width, D, index, owner * head_width).wait()
-        value = back_mul(merge_low[...], at.tall[index % 2, 0:head_width, :]).astype(BF16)
+        value = back_mul(merge_low[...], at.tall[index % tall, 0:head_width, :]).astype(BF16)
         if index < narrow - 1:
             away[index] = value
             start(swap(away.at[index], d_heads.at[me], 0, index + 1))
         else:
             d_heads[me] = value
-        if index + 2 < narrow:
-            ring(src.w2, at.tall, head_width, D, index + 2, owners[index + 2] * head_width).start()
+        if index + tall < narrow:
+            ring(src.w2, at.tall, head_width, D, index + tall, owners[index + tall] * head_width).start()
     plan.now += 3.0
     plan.transfer(0, piece, (-1, 0, 0), head_event)
     load(at.t2).wait()
-    for which in (5, 4, 3, 2):
+    push(5)
+    at.shrink_t[...] = shrink_low[...].T
+    plan.now += 2.0
+    for which in (4, 3, 2):
         push(which)
     load(at.qkv).wait()
     load(at.heads_out).wait()
@@ -1171,7 +1197,6 @@
     qkv, heads_out, log_sums, parts = at.qkv, at.heads_out, at.log_sums, at.parts
     key_t, key_acc, value_acc, query_acc = at.key_t, at.key_acc, at.value_acc, at.query_acc
     lane = lax.broadcasted_iota(jnp.int32, (1, LANES), 1)
-    line = lax.broadcasted_iota(jnp.int32, (LANES, 1), 0)
     sides = LANES // HD
     scale = HD ** (-0.5)
     choose = lax.broadcasted_iota(jnp.int32, (8, LANES), 1) // HD
@@ -1212,27 +1237,29 @@
                 preferred_element_type=F32,
             )
             log_rows = log_sums[who].T[pair * sides : (pair + 1) * sides, :]
-            own_query = [(query * jnp.where(lane // HD == side, scale, 0.0)).astype(BF16) for side in range(sides)]
-            own_upper = [(upper * jnp.where(lane // HD == side, 1.0, 0.0)).astype(BF16) for side in range(sides)]
+            masks = [jnp.where(lane // HD == side, 1.0, 0.0) for side in range(sides)]
+            own_query = jnp.concatenate([query * (scale * mask) for mask in masks], 0).astype(BF16)
+            own_upper = jnp.concatenate([upper * mask for mask in masks], 0).astype(BF16)
+            log_row = jnp.concatenate([log_rows[side : side + 1, :] for side in range(sides)], 1)
+            delta_row = jnp.concatenate([delta[side : side + 1, :] for side in range(sides)], 1)
             query_acc[...] = jnp.zeros_like(query_acc)
 
             def block(source, carry):
                 rows = pl.ds(pl.multiple_of(source * tokens, tokens), tokens)
                 key, value = qkv[source, 1, :, lanes], qkv[source, 2, :, lanes]
-                key_turned = key_t[:, rows].astype(F32)
+                probs = jnp.exp(back_mul(key, own_query) - log_row)
+                d_probs = back_mul(value, own_upper)
+                d_scores = (probs * (d_probs - delta_row)).astype(BF16)
+                value_acc[rows, :] += matmul(probs.astype(BF16), own_upper)
+                key_acc[rows, :] += matmul(d_scores, own_query)
+                turned = matmul(key_t[:, rows], d_scores)
                 for side in range(sides):
-                    scores = back_mul(key, own_query[side])
-                    probs = jnp.exp(scores - log_rows[side : side + 1, :])
-                    d_probs = back_mul(value, own_upper[side])
-                    d_scores = (probs * (d_probs - delta[side : side + 1, :])).astype(BF16)
-                    value_acc[rows, :] += matmul(probs.astype(BF16), own_upper[side])
-                    key_acc[rows, :] += matmul(d_scores, own_query[side])
-                    turned = (key_turned * jnp.where(line // HD == side, scale, 0.0)).astype(BF16)
-                    query_acc[...] += matmul(turned, d_scores)
+                    spot = slice(side * HD, (side + 1) * HD)
+                    query_acc[spot, :] += turned[spot, side * tokens : (side + 1) * tokens]
                 return carry
 
             lax.fori_loop(0, narrow, block, 0)
-            parts[who, 0, :, lanes] = query_acc[...].T.astype(BF16)
+            parts[who, 0, :, lanes] = (query_acc[...].T * scale).astype(BF16)
         for step in range(narrow):
             plan.work(3.0, functools.partial(one_block, step))
             for earlier in range(pair):
@@ -1255,7 +1282,7 @@
 
     def through_mixer(index, carry):
         ring(src.w1, at.long, 128, 3 * D, index, index * 128).wait()
-        slot = lax.rem(index, 2)
+        slot = lax.rem(index, long)
         value = jnp.zeros((tokens, 128), F32)
         for pair in range(head_width // LANES):
             for part in range(3):
@@ -1264,9 +1291,9 @@
                 value = value + back_mul(mixed[pair, part], jnp.concatenate(weight, 1))
         d_norm[:, pl.ds(pl.multiple_of(index * 128, 128), 128)] = value
 
-        @pl.when(index + 2 < D // 128)
+        @pl.when(index + long < D // 128)
         def _():
-            ring(src.w1, at.long, 128, 3 * D, index + 2, (index + 2) * 128).start()
+            ring(src.w1, at.long, 128, 3 * D, index + long, (index + long) * 128).start()
 
         return carry
 
@@ -1331,17 +1358,19 @@
     slots = 2 * chips + 2
     streamed = dict(w1=kept.w1, w2=kept.w2, w3=kept.w3, w4=kept.w4, w5=kept.w5)
     streamed.update(last=kept.last, mid=kept.mid, embedded=kept.embedded, slopes=kept.slopes)
-    loaded = dict(t5=kept.t5, t4=kept.t4, t3=kept.t3, t2=kept.t2, t1=kept.t1)
+    loaded = dict(t5=kept.t5, hidden=kept.hidden, t3=kept.t3, t2=kept.t2, t1=kept.t1)
     loaded.update(qkv=kept.qkv, heads_out=kept.heads_out, log_sums=kept.log_sums)
     whole = dict(gains=kept.gains, patches=patches, gauss=gauss, term=term)
     operands = {**streamed, **loaded, **whole}
     shapes = [jax.ShapeDtypeStruct((rows[which], widths[which]), F32) for which in range(6)]
+    shapes[4] = jax.ShapeDtypeStruct((D, rows[4]), F32)
     shapes.append(jax.ShapeDtypeStruct((8, LANES), F32))
     scratch = {name: pltpu.VMEM(value.shape, value.dtype) for name, value in loaded.items()}
     scratch.update(
-        acc=pltpu.VMEM((max(rows), max(width for _, _, width, _ in items)), F32),
+        acc=pltpu.VMEM((max(rows[3], D // 4), max(width for _, _, width, _ in items)), F32),
         embed_t=pltpu.VMEM((D, tokens), BF16),
         embed_low=pltpu.VMEM((tokens, D), BF16),
+        shrink_t=pltpu.VMEM((D, tokens), BF16),
         stash=pltpu.VMEM((tokens, D), F32),
         d_res=pltpu.VMEM((tokens, D), F32),
         d_norm=pltpu.VMEM((tokens, D), F32),
@@ -1351,9 +1380,9 @@
         expand_low=pltpu.VMEM((tokens, widths[3]), BF16),
         merge_low=pltpu.VMEM((tokens, D), BF16),
         mixed=pltpu.VMEM((head_width // LANES, 3, tokens, narrow * LANES), BF16),
-        tall=pltpu.VMEM((2, 512, D), BF16),
-        long=pltpu.VMEM((2, 128, widths[3]), BF16),
-        slope_slots=pltpu.VMEM((2, tokens, 512), BF16),
+        tall=pltpu.VMEM((4, 256, D), BF16),
+        long=pltpu.VMEM((3, 128, widths[3]), BF16),
+        slope_slots=pltpu.VMEM((4, tokens, 256), BF16),
         d_heads=pltpu.VMEM((narrow, tokens, head_width), BF16),
         away=pltpu.VMEM((narrow - 1, tokens, head_width), BF16),
         parts=pltpu.VMEM((narrow, 3, tokens, head_width), BF16),
@@ -1370,16 +1399,17 @@
         swap_send=pltpu.SemaphoreType.DMA((1 + head_width // LANES, narrow)),
         swap_recv=pltpu.SemaphoreType.DMA((1 + head_width // LANES, narrow)),
         in_sem=pltpu.SemaphoreType.DMA((9,)),
-        ring_sem=pltpu.SemaphoreType.DMA((3, 2)),
+        ring_sem=pltpu.SemaphoreType.DMA((3, 4)),
     )
-    lists = [pltpu.VMEM((chips, narrow, rows[which], width), BF16) for which, _, width, _ in items]
-    for which, _, width, _ in items:
+    blocks = [(width, rows[which]) if which == 4 else (rows[which], width) for which, _, width, _ in items]
+    lists = [pltpu.VMEM((chips, narrow) + block, BF16) for block in blocks]
+    for block in blocks:
         for bit in chip_bits(chips):
-            lists.append(pltpu.VMEM((chips // (2 * bit), narrow, rows[which], width), BF16))
-    lists += [pltpu.VMEM((narrow + 1, rows[which], width), BF16) for which, _, width, _ in items]
+            lists.append(pltpu.VMEM((chips // (2 * bit), narrow) + block, BF16))
+    lists += [pltpu.VMEM((narrow + 1,) + block, BF16) for block in blocks]
     for which in range(6):
-        widest = max(width for owner, _, width, _ in items if owner == which)
-        lists.append(pltpu.VMEM((chips, narrow, rows[which], widest), BF16))
+        widest = max(block for item, block in zip(items, blocks) if item[0] == which)
+        lists.append(pltpu.VMEM((chips, narrow) + widest, BF16))
     vmem = pl.BlockSpec(memory_space=pltpu.VMEM)
     hbm = pl.BlockSpec(memory_space=pl.ANY)
     return pl.pallas_call(
@@ -1562,7 +1592,7 @@
         t1=normed_one.T,
         t2=returned.T,
         t3=normed_two.T,
-        t4=activated.T,
+        hidden=activated,
         t5=normed_three.T,
         qkv=qkv,
         heads_out=attended,
@@ -1601,7 +1631,7 @@
     through_one, gain_one, shift_one = norm_back_one(back_mul(mixed_grad, weights[1]))
     embed_grad = (residual_grad + through_one).astype(BF16)
     grad_norms = jnp.stack([gain_one, gain_two, gain_three, shift_one, shift_two, shift_three])
-    lefts = [embed_grad.T] + [kept.t1, kept.t2, kept.t3, kept.t4, kept.t5]
+    lefts = [embed_grad.T, kept.t1, kept.t2, kept.t3, kept.hidden.T, kept.t5]
     rights = [patches, mixed_grad, merge_low, expand_low, shrink_low, gauss_low]
     products = [matmul(left, right) for left, right in zip(lefts, rights)]
     products[0] = products[0].at[:, features : features + kinds].add(grad_norms.T)
@@ -1620,7 +1650,7 @@
     sources, targets, refs = refs[:27], refs[27:48], refs[48:]
     loss_ref, norm_ref, refs = refs[0], refs[1], refs[2:]
     inside, news, refs = refs[:27], refs[27:48], refs[48:]
-    turned, in_sem, out_sem = refs
+    turned, turned_four, in_sem, out_sem = refs
     loads = [pltpu.make_async_copy(source, dest, in_sem.at[i]) for i, (source, dest) in enumerate(zip(sources, inside))]
     stores = [pltpu.make_async_copy(source, dest, out_sem.at[i]) for i, (source, dest) in enumerate(zip(news, targets))]
     for copy in loads:
@@ -1637,6 +1667,8 @@
             loads[which].wait()
         if which == 0:
             turned[...] = grads[0][:, width - LANES :].T
+        if which == 4:
+            turned_four[...] = grads[4][...].T
         for copy in loads[6 + 3 * which : 9 + 3 * which]:
             copy.wait()
         weight, first, second = olds[3 * which : 3 * which + 3]
@@ -1647,6 +1679,8 @@
             spot = pl.ds(pl.multiple_of(step * chunk, chunk), chunk)
             if which == 0:
                 grad = grads[0][spot, 0:columns]
+            elif which == 4:
+                grad = turned_four[spot, :]
             elif which == 6:
                 grad = turned[features % LANES : features % LANES + rows, 0:columns]
             else:
@@ -1678,6 +1712,7 @@
         + [pltpu.VMEM(old.shape, F32) for old in olds]
         + [
             pltpu.VMEM((LANES, sums[0].shape[0]), F32),
+            pltpu.VMEM(olds[12].shape, F32),
             pltpu.SemaphoreType.DMA((27,)),
             pltpu.SemaphoreType.DMA((21,)),
         ],
@@ -1725,7 +1760,7 @@
     kinds = norm_params.shape[0]
     padded = -(-(features + kinds) // LANES) * LANES
     fill = padded - features - kinds
-    by_kernel = mixer_weight.shape[0] % 16 == 0
+    by_kernel = mixer_weight.shape[0] % 16 == 0 and shrink_weight.shape[0] % LANES == 0
 
     patches = views.reshape(-1, features)
     rows = patches.shape[0]

time: 363 us -> 354 us (0.975)
  Pallas kernels: 346 us -> 337 us
    pallas_call x1, Pallas kernels: 189 us -> 179 us  [backward_all(): pl.pallas_call(functools.partial(backward_kernel, items, wide, narrow, le...]
where the time goes in v7:
time: 354 us; the launch traced here: 349 us
  Pallas kernels  337 us (95%)
  local copies, waits for them, and re-layouts  8.28 us (2%)
    pallas_call x1, Pallas kernels, backward_all(): pl.pallas_call(functools.partial(backward_kernel, items, wide, narrow, le...  179 us
    pallas_call x1, Pallas kernels, forward_all(): pl.pallas_call(functools.partial(forward_kernel, items, wide, narrow, lea...  147 us

profile of v7, /device:TPU:0, one launch (start us, length us, event | category | flops | bytes accessed | tf_op | source)
XLA Modules:
  0.0 349.2 jit_solution(13143233510786246675)
XLA Ops:
  0.7 0.0 copy-start.4
  0.7 0.0 copy-start.5
  2.0 1.4 reduce
  3.4 0.2 reshape_squeeze.7
  3.6 0.2 copy.62
  3.8 0.1 reshape.61.mask_ref
  4.0 0.0 copy-done.5
  4.0 0.8 pad.4.refs_7_.refs_18_
  4.8 0.0 copy-done.4
  4.8 0.2 copy.55
  5.0 0.6 reshape_squeeze.6
  5.6 0.4 copy.56
  6.0 0.4 reshape.60.target_ref
  6.5 2.3 copy.59
  8.8 0.0 copy-start.2
  8.8 0.5 reshape.62.weight_ref
  9.3 146.7 %forward.1 = (bf16[1024,3072]{1,0:T(8,128)(2,1)}, bf16[1024,1024]{1,0:T(8,128)(2,1)}, bf16[1024,4096]{1,0:T(8,128)(2,1)}, bf16[4096,1024]{1,0:T(8,128)(2,1)}, bf...) custom-call(f32[32,576]{1,0:T(8,128)} %bitcast.24, ...), custom_call_target="tpu_custom_call" | custom-call | tf_op jit(solution)/shard_map/forward/pallas_call | solution.py:713
  156.1 0.0 copy-done.2
  156.1 0.0 copy-start
  156.1 1.1 copy-done
  157.2 4.9 %render.1 = (bf16[256,768]{1,0:T(8,128)(2,1)S(1)}, f32[8,128]{1,0:T(8,128)S(1)}) custom-call(f32[256,768]{1,0:T(8,128)S(1)} %copy-done, f32[256,768]{1,0:T(8,128)S(1)} %reshape.62.weight_ref, bf16[192,768]{1,0:T(8,128)(2,1)S(1)} %reshape.60.target_ref, s32[64,768]{1,0:T(8,128)S(1)} %reshape.61.mask_ref, s32[2,2048]{1,0:T(2,128)S(1)} %bitcast.19, ...), custom_call_target="tpu_custom_call" | custom-call | tf_op jit(solution)/shard_map/render/pallas_call | solution.py:1537
  162.1 0.0 copy-start.1
  162.1 0.7 copy-done.1
  162.8 0.0 copy-start.3
  162.8 0.6 copy-done.3
  163.4 178.8 %backward.1 = (f32[32,640]{1,0:T(8,128)}, f32[32,3072]{1,0:T(8,128)}, f32[32,1024]{1,0:T(8,128)}, f32[32,4096]{1,0:T(8,128)}, f32[1024,128]{1,0:T(8,128)}, /*index=5*/f32[32,768]{1,0:T(8,128)}, f32[8,128]{1,0:T(8,128)}) custom-call(bf16[1024,3072]{1,0:T(8,128)(2,1)} %get-tuple-element.74.refs_0_, bf16[1024,1024]{1,0:T(8,128)(2,1)} %get-tuple-element.75.refs_1_, ...), custom_call_target="tpu_custom_call" | custom-call | tf_op jit(solution)/shard_map/backward/pallas_call | solution.py:1415
  342.3 6.8 %update.1 = (f32[32,576]{1,0:T(8,128)}, f32[32,576]{1,0:T(8,128)}, f32[32,576]{1,0:T(8,128)}, f32[32,3072]{1,0:T(8,128)}, f32[32,3072]{1,0:T(8,128)}, /*index=5*...) custom-call(s32[1]{0:T(128)S(6)} %copy.64.total_ref, ...), custom_call_target="tpu_custom_call" | custom-call | tf_op jit(solution)/shard_map/update/pallas_call | solution.py:1706
Async XLA Ops:
  0.7 4.1 %copy-start.4 = (bf16[1,12,3,4096]{3,2,1,0:T(4,128)(2,1)S(1)}, bf16[1,12,3,4096]{3,2,1,0:T(4,128)(2,1)}, u32[]{:S(2)}) copy-start(bf16[1,12,3,4096]{3,2,1,0:T(4,128)(2,1)} %param.30) | copy-start | bytes 884740
  0.7 3.3 copy-start.5
  8.8 147.3 %copy-start.2 = (s32[1,2,2048]{2,1,0:T(2,128)S(1)}, s32[1,2,2048]{2,1,0:T(2,128)}, u32[]{:S(2)}) copy-start(s32[1,2,2048]{2,1,0:T(2,128)} %param.32) | copy-start | bytes 49156
  156.1 1.1 copy-start
  162.1 0.7 copy-start.1
  162.8 0.6 copy-start.3

commit v8 on v7

--- a/solution.py
+++ b/solution.py
@@ -238,8 +238,10 @@
                 self.step()
 
 
-LINK = 100e3
+LINK = 90e3
 Z_AHEAD = 4.0
+Z_EARLY = 1.0
+Z_LATE = 2.0
 TWIN_LINK = 600e3
 
 
@@ -413,10 +415,10 @@
         else:
             onward(item, 0, 0)
 
-    begun = []
+    begun, ahead = [], [Z_EARLY]
 
     def refill():
-        while len(begun) < total and plan.free.get(0, 0.0) < plan.now + 0.5:
+        while len(begun) < total and plan.free.get(0, 0.0) < plan.now + ahead[-1]:
             begin_item(len(begun))
             begun.append(True)
 
@@ -555,6 +557,7 @@
             returned[me] = heads_out[who]
 
     steps = list(range(1, narrow)) + [0]
+    ahead.append(Z_LATE)
     plan.need([(-1, 0), (-1, 1)])
     for step in steps:
         plan.work(2.7, functools.partial(weigh, step))
@@ -926,6 +929,28 @@
 
         guarded.append((sender, along(item, sign, hop)))
 
+    def straight(item, step):
+        target = place.along(step)
+        return remote(
+            item,
+            held[item].at[0, target[1]],
+            final[item].at[narrow - step - 1],
+            2 * chips + narrow - step - 1,
+            target,
+        )
+
+    def is_straight(item):
+        return items[item][0] == 0
+
+    def straight_event(item):
+        acc = acc_of(item)
+        acc[...] = held[item][0, me].astype(F32)
+        for step in range(1, narrow):
+            straight(item, step).wait_recv()
+        for slot in range(narrow - 1):
+            acc[...] += final[item][slot].astype(F32)
+        finish(item, acc)
+
     def line_event(item, hop):
         for sign in (1, -1):
             count = narrow - hop - 1
@@ -951,10 +976,9 @@
 
     def line_transfer(item, hop):
         cost = (narrow - hop) * 2 * block_bytes(item) / narrow / LINK
-        event = line_event if hop < narrow else finish
         if hop == narrow:
-            return finish(item)
-        plan.transfer(0 if hop == 1 else 100 + hop, cost, (item, -hop, 0), functools.partial(event, item, hop))
+            return line_end(item)
+        plan.transfer(0 if hop == 1 else 100 + hop, cost, (item, -hop, 0), functools.partial(line_event, item, hop))
 
     def leaves(item, mask):
         bits = bits_of(item)
@@ -1019,6 +1043,12 @@
     def refill():
         while lined and plan.free.get(0, 0.0) < plan.now + Z_AHEAD:
             item = lined.pop(0)
+            if is_straight(item):
+                for step in range(1, narrow):
+                    start(straight(item, step))
+                cost = 2 * (narrow // 2) ** 2 * block_bytes(item) / narrow / LINK
+                plan.transfer(0, cost, (item, -1, 0), functools.partial(straight_event, item))
+                continue
             for sign in (1, -1):
                 send_along(item, sign, 1)
             line_transfer(item, 1)
@@ -1036,9 +1066,11 @@
 
     squares = []
 
-    def finish(item):
-        which, begin, width, _ = items[item]
-        acc = at.acc.at[pl.ds(0, held[item].shape[2]), pl.ds(0, held[item].shape[3])]
+    def acc_of(item):
+        return at.acc.at[pl.ds(0, held[item].shape[2]), pl.ds(0, held[item].shape[3])]
+
+    def line_end(item):
+        acc = acc_of(item)
         acc[...] = held[item][0, me].astype(F32)
 
         @pl.when(me >= 1)
@@ -1049,6 +1081,10 @@
         def _():
             acc[...] += final[item][me].astype(F32)
 
+        finish(item, acc)
+
+    def finish(item, acc):
+        which, begin, width, _ = items[item]
         value = acc[...]
         if which == 1:
             for shift in range(0, width, LANES):
@@ -1086,8 +1122,13 @@
 
         lax.fori_loop(0, tokens // step_rows, one, 0)
 
+    def loop_work(cost, count, pieces, body):
+        for piece in range(pieces):
+            low, high = count * piece // pieces, count * (piece + 1) // pieces
+            plan.work(cost / pieces, functools.partial(lax.fori_loop, low, high, body, 0))
+
     load(at.t5).wait()
-    plan.now += 5.0
+    push(5)
     load_stash(src.last).wait()
     count = D // u_rows
     tall_rows = slope_rows
@@ -1104,12 +1145,18 @@
 
         return carry
 
-    lax.fori_loop(0, count, through_unpatch, 0)
+    loop_work(2.5, count, 1, through_unpatch)
     for index in range(tall):
         ring(src.w4, at.tall, tall_rows, D, index, index * tall_rows).start()
-    norm_back(2, shrink_low, False)
+    plan.work(2.5, lambda: norm_back(2, shrink_low, False))
     load_stash(src.mid).start()
     load(at.hidden).wait()
+
+    def turn_shrink():
+        at.shrink_t[...] = shrink_low[...].T
+
+    plan.work(2.0, turn_shrink)
+    push(4)
     ff = src.w3.shape[1]
     slabs = ff // tall_rows
 
@@ -1128,12 +1175,11 @@
 
         return carry
 
-    lax.fori_loop(0, slabs, through_shrink, 0)
+    loop_work(6.0, slabs, 2, through_shrink)
     owners = [lax.rem(me + step, narrow) for step in list(range(1, narrow)) + [0]]
     for index in range(min(tall, narrow)):
         ring(src.w2, at.tall, head_width, D, index, owners[index] * head_width).start()
     load(at.t3).wait()
-    plan.now += 6.0
 
     def through_expand(index, carry):
         ring(src.w3, at.long, 128, ff, index, index * 128).wait()
@@ -1146,11 +1192,11 @@
 
         return carry
 
-    lax.fori_loop(0, D // 128, through_expand, 0)
+    loop_work(5.0, D // 128, 2, through_expand)
     for index in range(long):
         ring(src.w1, at.long, 128, 3 * D, index, index * 128).start()
     load_stash(src.mid).wait()
-    norm_back(1, merge_low, True)
+    plan.work(2.0, lambda: norm_back(1, merge_low, True))
     load_stash(src.embedded).start()
 
     def swap(src, dst, kind, step):
@@ -1164,14 +1210,13 @@
         )
 
     d_heads, away = at.d_heads, at.away
-    plan.now += 7.0
     piece = 2 * (narrow - 1) * 2 * tokens * head_width / LINK
 
     def head_event():
         for step in range(1, narrow):
             swap(away.at[step - 1], d_heads.at[me], 0, step).wait_recv()
 
-    for index, owner in enumerate(owners):
+    def through_merge(index, owner):
         ring(src.w2, at.tall, head_width, D, index, owner * head_width).wait()
         value = back_mul(merge_low[...], at.tall[index % tall, 0:head_width, :]).astype(BF16)
         if index < narrow - 1:
@@ -1181,14 +1226,13 @@
             d_heads[me] = value
         if index + tall < narrow:
             ring(src.w2, at.tall, head_width, D, index + tall, owners[index + tall] * head_width).start()
-    plan.now += 3.0
+
+    for index, owner in enumerate(owners):
+        plan.work(0.7, functools.partial(through_merge, index, owner))
     plan.transfer(0, piece, (-1, 0, 0), head_event)
     load(at.t2).wait()
-    push(5)
-    at.shrink_t[...] = shrink_low[...].T
-    plan.now += 2.0
-    for which in (4, 3, 2):
-        push(which)
+    push(3)
+    push(2)
     load(at.qkv).wait()
     load(at.heads_out).wait()
     load(at.log_sums).wait()
@@ -1355,7 +1399,7 @@
     head_width = D // narrow
     length = narrow * tokens
     items = backward_plan(widths, head_width // LANES)
-    slots = 2 * chips + 2
+    slots = 2 * chips + narrow + 1
     streamed = dict(w1=kept.w1, w2=kept.w2, w3=kept.w3, w4=kept.w4, w5=kept.w5)
     streamed.update(last=kept.last, mid=kept.mid, embedded=kept.embedded, slopes=kept.slopes)
     loaded = dict(t5=kept.t5, hidden=kept.hidden, t3=kept.t3, t2=kept.t2, t1=kept.t1)

time: 354 us -> 356 us (level)
  no operation moved by 1% of the time
where the time goes in v8:
time: 356 us; the launch traced here: 351 us
  Pallas kernels  339 us (95%)
  local copies, waits for them, and re-layouts  8.28 us (2%)
    pallas_call x1, Pallas kernels, backward_all(): pl.pallas_call(functools.partial(backward_kernel, items, wide, narrow, le...  178 us
    pallas_call x1, Pallas kernels, forward_all(): pl.pallas_call(functools.partial(forward_kernel, items, wide, narrow, lea...  149 us

profile of v8, /device:TPU:0, one launch (start us, length us, event | category | flops | bytes accessed | tf_op | source)
XLA Modules:
  0.0 351.4 jit_solution(12333688810365832065)
XLA Ops:
  0.7 0.0 copy-start.4
  0.7 0.0 copy-start.5
  2.0 1.4 reduce
  3.4 0.2 reshape_squeeze.7
  3.6 0.2 copy.62
  3.8 0.1 reshape.61.mask_ref
  4.0 0.0 copy-done.5
  4.0 0.8 pad.4.refs_7_.refs_18_
  4.8 0.0 copy-done.4
  4.8 0.2 copy.55
  5.0 0.6 reshape_squeeze.6
  5.6 0.4 copy.56
  6.0 0.4 reshape.60.target_ref
  6.5 2.3 copy.59
  8.8 0.0 copy-start.2
  8.8 0.5 reshape.62.weight_ref
  9.3 149.4 %forward.1 = (bf16[1024,3072]{1,0:T(8,128)(2,1)}, bf16[1024,1024]{1,0:T(8,128)(2,1)}, bf16[1024,4096]{1,0:T(8,128)(2,1)}, bf16[4096,1024]{1,0:T(8,128)(2,1)}, bf...) custom-call(f32[32,576]{1,0:T(8,128)} %bitcast.24, ...), custom_call_target="tpu_custom_call" | custom-call | tf_op jit(solution)/shard_map/forward/pallas_call | solution.py:716
  158.7 0.0 copy-done.2
  158.7 0.0 copy-start
  158.7 1.1 copy-done
  159.9 4.9 %render.1 = (bf16[256,768]{1,0:T(8,128)(2,1)S(1)}, f32[8,128]{1,0:T(8,128)S(1)}) custom-call(f32[256,768]{1,0:T(8,128)S(1)} %copy-done, f32[256,768]{1,0:T(8,128)S(1)} %reshape.62.weight_ref, bf16[192,768]{1,0:T(8,128)(2,1)S(1)} %reshape.60.target_ref, s32[64,768]{1,0:T(8,128)S(1)} %reshape.61.mask_ref, s32[2,2048]{1,0:T(2,128)S(1)} %bitcast.19, ...), custom_call_target="tpu_custom_call" | custom-call | tf_op jit(solution)/shard_map/render/pallas_call | solution.py:1581
  164.7 0.0 copy-start.1
  164.7 0.7 copy-done.1
  165.5 0.0 copy-start.3
  165.5 0.6 copy-done.3
  166.1 178.4 %backward.1 = (f32[32,640]{1,0:T(8,128)}, f32[32,3072]{1,0:T(8,128)}, f32[32,1024]{1,0:T(8,128)}, f32[32,4096]{1,0:T(8,128)}, f32[1024,128]{1,0:T(8,128)}, /*index=5*/f32[32,768]{1,0:T(8,128)}, f32[8,128]{1,0:T(8,128)}) custom-call(bf16[1024,3072]{1,0:T(8,128)(2,1)} %get-tuple-element.74.refs_0_, bf16[1024,1024]{1,0:T(8,128)(2,1)} %get-tuple-element.75.refs_1_, ...), custom_call_target="tpu_custom_call" | custom-call | tf_op jit(solution)/shard_map/backward/pallas_call | solution.py:1459
  344.5 6.8 %update.1 = (f32[32,576]{1,0:T(8,128)}, f32[32,576]{1,0:T(8,128)}, f32[32,576]{1,0:T(8,128)}, f32[32,3072]{1,0:T(8,128)}, f32[32,3072]{1,0:T(8,128)}, /*index=5*...) custom-call(s32[1]{0:T(128)S(6)} %copy.64.total_ref, ...), custom_call_target="tpu_custom_call" | custom-call | tf_op jit(solution)/shard_map/update/pallas_call | solution.py:1750
Async XLA Ops:
  0.7 4.1 %copy-start.4 = (bf16[1,12,3,4096]{3,2,1,0:T(4,128)(2,1)S(1)}, bf16[1,12,3,4096]{3,2,1,0:T(4,128)(2,1)}, u32[]{:S(2)}) copy-start(bf16[1,12,3,4096]{3,2,1,0:T(4,128)(2,1)} %param.30) | copy-start | bytes 884740
  0.7 3.3 copy-start.5
  8.8 149.9 %copy-start.2 = (s32[1,2,2048]{2,1,0:T(2,128)S(1)}, s32[1,2,2048]{2,1,0:T(2,128)}, u32[]{:S(2)}) copy-start(s32[1,2,2048]{2,1,0:T(2,128)} %param.32) | copy-start | bytes 49156
  158.7 1.1 copy-start
  164.7 0.7 copy-start.1
  165.5 0.6 copy-start.3

commit v9 on v8

--- a/solution.py
+++ b/solution.py
@@ -240,6 +240,7 @@
 
 LINK = 90e3
 Z_AHEAD = 4.0
+RELAYED = (3, 4)
 Z_EARLY = 1.0
 Z_LATE = 2.0
 TWIN_LINK = 600e3
@@ -300,16 +301,18 @@
     greet(place.neighbours())
     rows_of = [shard.shape[0] for shard in shards]
 
-    def rows_at(which, chip, core, node=None):
+    def slab(which, node):
         rows = rows_of[which]
-        if node is None:
-            return pl.ds(pl.multiple_of((chip * 2 + core) * narrow * rows, rows), narrow * rows)
-        return pl.ds(pl.multiple_of(((chip * 2 + core) * narrow + node) * rows, rows), rows)
+        return pl.ds(pl.multiple_of(node * rows, rows), rows)
+
+    def whole_of(which, columns):
+        part = weights[which][:, :, :, columns]
+        return part.reshape(-1, part.shape[-1])
 
     own = []
     for which in range(6):
         copy = pltpu.make_async_copy(
-            shards[which], weights[which].at[rows_at(which, place.chip, place.core, me), :], own_sem.at[which]
+            shards[which], weights[which].at[place.chip, place.core, slab(which, me), :], own_sem.at[which]
         )
         copy.start()
         own.append(copy)
@@ -326,17 +329,17 @@
 
     def group(item, mask):
         which, begin, width, _ = items[item]
-        return weights[which].at[rows_at(which, flip(place.chip, mask), place.core), pl.ds(begin, width)]
+        return weights[which].at[flip(place.chip, mask), place.core, :, pl.ds(begin, width)]
 
     def along(item, sign, hop):
         which, begin, width, _ = items[item]
         columns = pl.ds(begin, width)
-        rows = rows_at(which, place.chip, place.core, me - sign * (hop - 1))
+        there = weights[which].at[place.chip, place.core, slab(which, me - sign * (hop - 1)), columns]
         return remote(
             item,
-            shards[which].at[:, columns] if hop == 1 else weights[which].at[rows, columns],
-            weights[which].at[rows, columns],
-            2 * chips + hop - 1 + (narrow - 1 if sign < 0 else 0),
+            shards[which].at[:, columns] if hop == 1 else there,
+            there,
+            chips + 1 + hop - 1 + (narrow - 1 if sign < 0 else 0),
             (place.w, me + sign),
         )
 
@@ -359,8 +362,10 @@
     def across(item, mask, bit):
         return remote(item, group(item, mask), group(item, mask), mask ^ bit, place.across(bit))
 
-    def to_twin(item, mask):
-        return remote(item, group(item, mask), group(item, mask), chips + mask, place.twin)
+    def to_twin(item):
+        which, begin, width, _ = items[item]
+        there = weights[which].at[:, place.core, :, pl.ds(begin, width)]
+        return remote(item, there, there, chips, place.twin)
 
     plan = Planner()
     waited = set()
@@ -369,8 +374,10 @@
         which, _, width, _ = items[item]
         return 2 * narrow * rows_of[which] * width
 
-    def twin_event(item, mask):
-        return lambda: to_twin(item, mask).wait_recv()
+    def twin_event(item):
+        to_twin(item).wait_recv()
+
+    here = {}
 
     def onward(item, mask, number):
         bits = bits_of(item)
@@ -381,8 +388,10 @@
             plan.transfer(
                 bits[later], 2 * size / LINK, (item, coming), functools.partial(arrive, item, coming, later)
             )
-        start(to_twin(item, mask))
-        plan.transfer(-1, size / TWIN_LINK, (item, chips + mask), twin_event(item, mask))
+        here[item] = here.get(item, 0) + 1
+        if here[item] == chips:
+            start(to_twin(item))
+            plan.transfer(-1, chips * size / TWIN_LINK, (item, chips), functools.partial(twin_event, item))
 
     def arrive(item, mask, number):
         across(item, mask ^ bits_of(item)[number], bits_of(item)[number]).wait_recv()
@@ -431,7 +440,7 @@
                 (index, key)
                 for index, (owner, begin, width, _) in enumerate(items)
                 if owner == which and (columns is None or (begin < columns[1] and begin + width > columns[0]))
-                for key in range(2 * chips)
+                for key in range(chips + 1)
             ]
         )
 
@@ -463,16 +472,17 @@
         flush(dest)
 
     need(0)
-    width = weights[0].shape[1]
+    width = weights[0].shape[-1]
     kind = lax.broadcasted_iota(jnp.int32, (8, LANES), 0)
     spot = lax.broadcasted_iota(jnp.int32, (8, LANES), 1)
     pick = (spot == kind + lead).astype(F32).astype(BF16)
-    gains[...] = back_mul(pick, weights[0][:, width - LANES :])
+    gains[...] = back_mul(pick, whole_of(0, pl.ds(width - LANES, LANES)))
     flush(gains)
 
     def embed(block):
         cols = pl.ds(block, 256)
-        embedded[:, cols] = back_mul(at.patches[...], weights[0][pl.ds(block, 256), : at.patches.shape[1]])
+        rows = whole_of(0, pl.ds(0, width))[block : block + 256]
+        embedded[:, cols] = back_mul(at.patches[...], rows)
 
     for block in range(0, D, 256):
         plan.work(0.5, functools.partial(embed, block))
@@ -497,7 +507,7 @@
     def project(part, step):
         owner = lax.rem(me + step, narrow)
         offset = pl.multiple_of(part * D + owner * head_width, LANES)
-        value = matmul(normed[...], weights[1][:, pl.ds(offset, head_width)]).astype(BF16)
+        value = matmul(normed[...], whole_of(1, pl.ds(offset, head_width))).astype(BF16)
         if step:
             away[step - 1, part] = value
             start(swap(away.at[step - 1, part], qkv.at[me, part], part, step))
@@ -579,8 +589,9 @@
     def merge(block):
         cols = pl.ds(block, 256)
         value = embedded[:, cols]
+        weight = whole_of(2, cols)
         for source in range(narrow):
-            value = value + matmul(returned[source], weights[2][pl.ds(source * head_width, head_width), cols])
+            value = value + matmul(returned[source], weight[source * head_width : (source + 1) * head_width])
         mid[:, cols] = value
 
     for block in range(0, D, 256):
@@ -598,12 +609,12 @@
     plan.later(2.0, turn_returned)
     turn_second = plan.later(2.0, lambda: turn(at.t3, normed))
 
-    ff = weights[3].shape[1]
+    ff = weights[3].shape[-1]
     tile = wave.shape[1]
     slopes = at.slopes
 
     def expand(block):
-        wave[...] = matmul(normed[...], weights[3][:, pl.ds(block, tile)])
+        wave[...] = matmul(normed[...], whole_of(3, pl.ds(block, tile)))
 
         def bend(step, carry):
             rows = pl.ds(pl.multiple_of(step * 32, 32), 32)
@@ -625,7 +636,7 @@
 
     def shrink(block):
         cols = pl.ds(block, 256)
-        last[:, cols] = mid[:, cols] + matmul(hidden[...], weights[4][:, cols])
+        last[:, cols] = mid[:, cols] + matmul(hidden[...], whole_of(4, cols))
 
     for block in range(0, D, 256):
         need(4, (block, block + 256))
@@ -638,9 +649,9 @@
 
     def unpatch(block):
         cols = pl.ds(block, 256)
-        at.gaussians[:, cols] = matmul(normed[...], weights[5][:, cols])
-
-    for block in range(0, weights[5].shape[1], 256):
+        at.gaussians[:, cols] = matmul(normed[...], whole_of(5, cols))
+
+    for block in range(0, weights[5].shape[-1], 256):
         plan.work(0.7, functools.partial(unpatch, block))
     flush(at.w5)
     flush(at.gaussians)
@@ -663,10 +674,11 @@
     widths = [patches.shape[1]] + [shard.shape[1] for shard in shards[1:]]
     heights = [shard.shape[0] * wide * narrow for shard in shards]
     ff = widths[3]
+    chips = wide // 2
     head_width = D // narrow
     items = forward_plan(widths)
-    slots = wide + 2 * (narrow - 1)
-    full = [((height, width), BF16) for height, width in zip(heights, widths)]
+    slots = chips + 1 + 2 * (narrow - 1)
+    full = [((chips, 2, height // wide, width), BF16) for height, width in zip(heights, widths)]
     shapes = dict(
         w1=full[1],
         w2=full[2],
@@ -691,7 +703,7 @@
     ins = tuple(dict(s0=0, s1=0, s2=0, s3=0, s4=0, s5=0, norm_raw=0, patches=0))
     outs = tuple(shapes)
     extras = dict(
-        first_weight=pltpu.VMEM((heights[0], widths[0]), BF16),
+        first_weight=pltpu.VMEM(*full[0]),
         c0=pltpu.VMEM((shards[0].shape[0], widths[0]), BF16),
         c1=pltpu.VMEM(shards[1].shape, BF16),
         c2=pltpu.VMEM(shards[2].shape, BF16),
@@ -724,21 +736,14 @@
         ),
         name="forward",
     )(*shards, norms, patches)
+    results = [result.reshape(-1, result.shape[-1]) for result in results[:5]] + list(results[5:])
     return Bag(zip(outs, results))
 
 
 def backward_plan(widths, pairs):
     items = []
-    for which, cuts in ((5, 1), (4, 2), (3, 2), (2, 1), (1, pairs), (0, 1)):
+    for which, cuts in ((5, 1), (4, 1), (3, 1), (2, 1), (1, pairs), (0, 1)):
         size = widths[which] // cuts
-        if which == 1:
-            piece = size // 3
-            for cut in range(cuts):
-                start = cut * size
-                items += [(1, start, piece, 0), (1, start + piece, piece, 1)]
-                for side, (shift, width) in enumerate(column_halves(piece)):
-                    items.append((1, start + 2 * piece + shift, width, side))
-            continue
         for cut in range(cuts):
             for side, (start, width) in enumerate(column_halves(size)):
                 items.append((which, cut * size + start, width, side))
@@ -869,15 +874,17 @@
         firsts = [((flip(place.chip, mask) * 2 + core) * narrow) * rows for mask in masks]
         with_extra = which == 0 and begin + width == right.shape[1]
         assert not with_extra or tile == width
-        part, begin = (begin // reach, begin % reach) if which == 1 else (None, begin)
+        if which == 1:
+            tile = LANES * 2
 
         def one(step, carry):
             offset = pl.multiple_of(begin + step * tile, LANES)
             local = pl.multiple_of(step * tile, LANES)
-            if part is None:
+            if which != 1:
                 rhs = right[:, pl.ds(offset, tile)]
             else:
-                rhs = right[part // 3, part % 3, :, pl.ds(offset, tile)]
+                part, inside = offset // reach, pl.multiple_of(offset % reach, LANES)
+                rhs = right[part // 3, part % 3, :, pl.ds(inside, tile)]
             spots = [pl.ds(pl.multiple_of(first, span), span) for first in firsts]
             lhs = jnp.concatenate([left[spot, :] for spot in spots], 0)
             value = jnp.dot(lhs, rhs, preferred_element_type=F32)
@@ -908,7 +915,10 @@
             item, held[item].at[mask], passed[item][number].at[slot], chips + mask, place.across(bit)
         )
 
-    def along(item, sign, hop):
+    def relayed(item):
+        return items[item][0] in RELAYED
+
+    def hopping(item, sign, hop):
         count = narrow - hop
         first = hop if sign > 0 else 0
         node = hop if sign > 0 else narrow - 1 - hop
@@ -920,16 +930,42 @@
             (place.w, node),
         )
 
-    def send_along(item, sign, hop):
+    def send_hop(item, sign, hop):
         sender = me == (hop - 1 if sign > 0 else narrow - hop)
 
         @pl.when(sender)
         def _():
-            along(item, sign, hop).start()
-
-        guarded.append((sender, along(item, sign, hop)))
-
-    def straight(item, step):
+            hopping(item, sign, hop).start()
+
+        guarded.append((sender, hopping(item, sign, hop)))
+
+    def hop_event(item, hop):
+        count = narrow - hop - 1
+        for sign in (1, -1):
+            first = hop + 1 if sign > 0 else 0
+            shift = 1 if sign > 0 else 0
+
+            @pl.when(me == (hop if sign > 0 else narrow - 1 - hop))
+            def _():
+                hopping(item, sign, hop).wait_recv()
+                if count:
+                    mine, theirs = pl.ds(first, count), pl.ds(first + shift, count)
+                    value = held[item][0, mine].astype(F32) + final[item][theirs].astype(F32)
+                    held[item][0, mine] = value.astype(BF16)
+
+            if count:
+                send_hop(item, sign, hop + 1)
+        if count:
+            hop_transfer(item, hop + 1)
+        else:
+            finish(item)
+
+    def hop_transfer(item, hop):
+        cost = (narrow - hop) * 2 * block_bytes(item) / narrow / LINK
+        event = functools.partial(hop_event, item, hop)
+        plan.transfer(0 if hop == 1 else 100 + hop, cost, (item, -hop, 0), event)
+
+    def along(item, step):
         target = place.along(step)
         return remote(
             item,
@@ -938,47 +974,6 @@
             2 * chips + narrow - step - 1,
             target,
         )
-
-    def is_straight(item):
-        return items[item][0] == 0
-
-    def straight_event(item):
-        acc = acc_of(item)
-        acc[...] = held[item][0, me].astype(F32)
-        for step in range(1, narrow):
-            straight(item, step).wait_recv()
-        for slot in range(narrow - 1):
-            acc[...] += final[item][slot].astype(F32)
-        finish(item, acc)
-
-    def line_event(item, hop):
-        for sign in (1, -1):
-            count = narrow - hop - 1
-            first = hop + 1 if sign > 0 else 0
-
-            @pl.when(me == (hop if sign > 0 else narrow - 1 - hop))
-            def _():
-                along(item, sign, hop).wait_recv()
-
-                def one(step, carry):
-                    spot = first + step
-                    value = held[item][0, spot].astype(F32)
-                    value = value + final[item][spot + (1 if sign > 0 else 0)].astype(F32)
-                    held[item][0, spot] = value.astype(BF16)
-                    return carry
-
-                if count:
-                    lax.fori_loop(0, count, one, 0)
-
-            if count:
-                send_along(item, sign, hop + 1)
-        line_transfer(item, hop + 1)
-
-    def line_transfer(item, hop):
-        cost = (narrow - hop) * 2 * block_bytes(item) / narrow / LINK
-        if hop == narrow:
-            return line_end(item)
-        plan.transfer(0 if hop == 1 else 100 + hop, cost, (item, -hop, 0), functools.partial(line_event, item, hop))
 
     def leaves(item, mask):
         bits = bits_of(item)
@@ -1043,15 +1038,15 @@
     def refill():
         while lined and plan.free.get(0, 0.0) < plan.now + Z_AHEAD:
             item = lined.pop(0)
-            if is_straight(item):
-                for step in range(1, narrow):
-                    start(straight(item, step))
-                cost = 2 * (narrow // 2) ** 2 * block_bytes(item) / narrow / LINK
-                plan.transfer(0, cost, (item, -1, 0), functools.partial(straight_event, item))
+            if relayed(item):
+                for sign in (1, -1):
+                    send_hop(item, sign, 1)
+                hop_transfer(item, 1)
                 continue
-            for sign in (1, -1):
-                send_along(item, sign, 1)
-            line_transfer(item, 1)
+            for step in range(1, narrow):
+                start(along(item, step))
+            cost = 2 * (narrow // 2) ** 2 * block_bytes(item) / narrow / LINK
+            plan.transfer(0, cost, (item, -1, 0), functools.partial(finish, item))
 
     plan.refill = refill
 
@@ -1064,28 +1059,21 @@
         plan.now += block_bytes(item) / 8e5
         onward(item, mask, number + 1)
 
-    squares = []
-
-    def acc_of(item):
-        return at.acc.at[pl.ds(0, held[item].shape[2]), pl.ds(0, held[item].shape[3])]
-
-    def line_end(item):
-        acc = acc_of(item)
-        acc[...] = held[item][0, me].astype(F32)
-
-        @pl.when(me >= 1)
-        def _():
-            acc[...] += final[item][me + 1].astype(F32)
-
-        @pl.when(me < narrow - 1)
-        def _():
-            acc[...] += final[item][me].astype(F32)
-
-        finish(item, acc)
-
-    def finish(item, acc):
+    at.squares[...] = jnp.zeros_like(at.squares)
+
+    def finish(item):
         which, begin, width, _ = items[item]
-        value = acc[...]
+        value = held[item][0, me].astype(F32)
+        if relayed(item):
+            value = value + jnp.where(me >= 1, final[item][me + 1].astype(F32), 0.0)
+            value = value + jnp.where(me < narrow - 1, final[item][me].astype(F32), 0.0)
+        else:
+            for step in range(1, narrow):
+                along(item, step).wait_recv()
+            for slot in range(narrow - 1):
+                value = value + final[item][slot].astype(F32)
+        columns = pl.ds(0, value.shape[1])
+        at.squares[:, columns] += jnp.sum(value * value, 0, keepdims=True)
         if which == 1:
             for shift in range(0, width, LANES):
                 part, spot = (begin + shift) // reach, (begin + shift) % reach
@@ -1095,7 +1083,6 @@
             sums[which][pl.ds(begin, width), :] = value
         else:
             sums[which][:, pl.ds(begin, width)] = value
-        squares.append(jnp.sum(value * value))
 
     norms[...] = jnp.zeros_like(norms)
 
@@ -1352,7 +1339,7 @@
 
     rows = lax.broadcasted_iota(jnp.int32, (8, LANES), 0)
     wide_tiles, narrow_tiles = at.wide_tiles, at.narrow_tiles
-    wide_tiles[place.w] = jnp.where(rows == 0, src.term[...], sum(squares))
+    wide_tiles[place.w] = jnp.where(rows == 0, src.term[...], jnp.sum(at.squares[...]))
 
     def tile_copy(buffer, index, slot, peer):
         return pltpu.make_async_remote_copy(
@@ -1399,7 +1386,7 @@
     head_width = D // narrow
     length = narrow * tokens
     items = backward_plan(widths, head_width // LANES)
-    slots = 2 * chips + narrow + 1
+    slots = 2 * chips + max(2, narrow - 1)
     streamed = dict(w1=kept.w1, w2=kept.w2, w3=kept.w3, w4=kept.w4, w5=kept.w5)
     streamed.update(last=kept.last, mid=kept.mid, embedded=kept.embedded, slopes=kept.slopes)
     loaded = dict(t5=kept.t5, hidden=kept.hidden, t3=kept.t3, t2=kept.t2, t1=kept.t1)
@@ -1410,8 +1397,9 @@
     shapes[4] = jax.ShapeDtypeStruct((D, rows[4]), F32)
     shapes.append(jax.ShapeDtypeStruct((8, LANES), F32))
     scratch = {name: pltpu.VMEM(value.shape, value.dtype) for name, value in loaded.items()}
+    blocks = [(width, rows[which]) if which == 4 else (rows[which], width) for which, _, width, _ in items]
     scratch.update(
-        acc=pltpu.VMEM((max(rows[3], D // 4), max(width for _, _, width, _ in items)), F32),
+        squares=pltpu.VMEM((1, max(block[1] for block in blocks)), F32),
         embed_t=pltpu.VMEM((D, tokens), BF16),
         embed_low=pltpu.VMEM((tokens, D), BF16),
         shrink_t=pltpu.VMEM((D, tokens), BF16),
@@ -1445,12 +1433,12 @@
         in_sem=pltpu.SemaphoreType.DMA((9,)),
         ring_sem=pltpu.SemaphoreType.DMA((3, 4)),
     )
-    blocks = [(width, rows[which]) if which == 4 else (rows[which], width) for which, _, width, _ in items]
     lists = [pltpu.VMEM((chips, narrow) + block, BF16) for block in blocks]
     for block in blocks:
         for bit in chip_bits(chips):
             lists.append(pltpu.VMEM((chips // (2 * bit), narrow) + block, BF16))
-    lists += [pltpu.VMEM((narrow + 1,) + block, BF16) for block in blocks]
+    for (which, _, _, _), block in zip(items, blocks):
+        lists.append(pltpu.VMEM((narrow + (1 if which in RELAYED else -1),) + block, BF16))
     for which in range(6):
         widest = max(block for item, block in zip(items, blocks) if item[0] == which)
         lists.append(pltpu.VMEM((chips, narrow) + widest, BF16))

time: 356 us -> 361 us (1.014)
  Pallas kernels: 339 us -> 343 us
    pallas_call x1, Pallas kernels: 178 us -> 190 us  [backward_all(): pl.pallas_call(functools.partial(backward_kernel, items, wide, narrow, le...]
    pallas_call x1, Pallas kernels: 149 us -> 142 us  [forward_all(): pl.pallas_call(functools.partial(forward_kernel, items, wide, narrow, lea...]
where the time goes in v9:
time: 361 us; the launch traced here: 356 us
  Pallas kernels  343 us (95%)
  local copies, waits for them, and re-layouts  8.28 us (2%)
    pallas_call x1, Pallas kernels, backward_all(): pl.pallas_call(functools.partial(backward_kernel, items, wide, narrow, le...  190 us
    pallas_call x1, Pallas kernels, forward_all(): pl.pallas_call(functools.partial(forward_kernel, items, wide, narrow, lea...  142 us

profile of v9, /device:TPU:0, one launch (start us, length us, event | category | flops | bytes accessed | tf_op | source)
XLA Modules:
  0.0 355.7 jit_solution(7494909210283369264)
XLA Ops:
  0.7 0.0 copy-start.4
  0.7 0.0 copy-start.5
  2.0 1.4 reduce
  3.4 0.2 reshape_squeeze.7
  3.6 0.2 copy.62
  3.8 0.1 reshape.81.mask_ref
  4.0 0.0 copy-done.5
  4.0 0.8 pad.4.refs_7_.refs_18_
  4.8 0.0 copy-done.4
  4.8 0.2 copy.55
  5.0 0.6 reshape_squeeze.6
  5.6 0.4 copy.56
  6.0 0.4 reshape.80.target_ref
  6.5 2.3 copy.59
  8.8 0.0 copy-start.2
  8.8 0.5 reshape.82.weight_ref
  9.3 142.2 %forward.1 = (bf16[4,2,128,3072]{3,2,1,0:T(8,128)(2,1)}, bf16[4,2,128,1024]{3,2,1,0:T(8,128)(2,1)}, bf16[4,2,128,4096]{3,2,1,0:T(8,128)(2,1)}, bf16[4,2,512,1024...) custom-call(f32[32,576]{1,0:T(8,128)} %bitcast.34, ...), custom_call_target="tpu_custom_call" | custom-call | tf_op jit(solution)/shard_map/forward/pallas_call | solution.py:728
  151.5 0.0 copy-done.2
  151.5 0.0 copy-start
  151.6 1.1 copy-done
  152.7 4.9 %render.1 = (bf16[256,768]{1,0:T(8,128)(2,1)S(1)}, f32[8,128]{1,0:T(8,128)S(1)}) custom-call(f32[256,768]{1,0:T(8,128)S(1)} %copy-done, f32[256,768]{1,0:T(8,128)S(1)} %reshape.82.weight_ref, bf16[192,768]{1,0:T(8,128)(2,1)S(1)} %reshape.80.target_ref, s32[64,768]{1,0:T(8,128)S(1)} %reshape.81.mask_ref, s32[2,2048]{1,0:T(2,128)S(1)} %bitcast.24, ...), custom_call_target="tpu_custom_call" | custom-call | tf_op jit(solution)/shard_map/render/pallas_call | solution.py:1569
  157.5 0.0 copy-start.1
  157.6 0.7 copy-done.1
  158.3 0.0 copy-start.3
  158.3 0.6 copy-done.3
  158.9 189.6 %backward.1 = (f32[32,640]{1,0:T(8,128)}, f32[32,3072]{1,0:T(8,128)}, f32[32,1024]{1,0:T(8,128)}, f32[32,4096]{1,0:T(8,128)}, f32[1024,128]{1,0:T(8,128)}, /*index=5*/f32[32,768]{1,0:T(8,128)}, f32[8,128]{1,0:T(8,128)}) custom-call(bf16[1024,3072]{1,0:T(8,128)(2,1)} %bitcast.27, bf16[1024,1024]{1,0:T(8,128)(2,1)} %bitcast.29, bf16[1024,4096]{1,0:T(8,128)(2,1)} %bitcast.25, ...), custom_call_target="tpu_custom_call" | custom-call | tf_op jit(solution)/shard_map/backward/pallas_call | solution.py:1447
  348.5 6.8 %update.1 = (f32[32,576]{1,0:T(8,128)}, f32[32,576]{1,0:T(8,128)}, f32[32,576]{1,0:T(8,128)}, f32[32,3072]{1,0:T(8,128)}, f32[32,3072]{1,0:T(8,128)}, /*index=5*...) custom-call(s32[1]{0:T(128)S(6)} %copy.64.total_ref, ...), custom_call_target="tpu_custom_call" | custom-call | tf_op jit(solution)/shard_map/update/pallas_call | solution.py:1738
Async XLA Ops:
  0.7 4.1 %copy-start.4 = (bf16[1,12,3,4096]{3,2,1,0:T(4,128)(2,1)S(1)}, bf16[1,12,3,4096]{3,2,1,0:T(4,128)(2,1)}, u32[]{:S(2)}) copy-start(bf16[1,12,3,4096]{3,2,1,0:T(4,128)(2,1)} %param.30) | copy-start | bytes 884740
  0.7 3.3 copy-start.5
  8.8 142.7 %copy-start.2 = (s32[1,2,2048]{2,1,0:T(2,128)S(1)}, s32[1,2,2048]{2,1,0:T(2,128)}, u32[]{:S(2)}) copy-start(s32[1,2,2048]{2,1,0:T(2,128)} %param.32) | copy-start | bytes 49156
  151.5 1.1 copy-start
  157.5 0.7 copy-start.1
  158.3 0.6 copy-start.3

commit v10 on v9

--- a/solution.py
+++ b/solution.py
@@ -241,6 +241,7 @@
 LINK = 90e3
 Z_AHEAD = 4.0
 RELAYED = (3, 4)
+KEY_ROWS = 512
 Z_EARLY = 1.0
 Z_LATE = 2.0
 TWIN_LINK = 600e3
@@ -742,7 +743,7 @@
 
 def backward_plan(widths, pairs):
     items = []
-    for which, cuts in ((5, 1), (4, 1), (3, 1), (2, 1), (1, pairs), (0, 1)):
+    for which, cuts in ((5, 1), (4, 2), (3, 2), (2, 1), (1, pairs), (0, 1)):
         size = widths[which] // cuts
         for cut in range(cuts):
             for side, (start, width) in enumerate(column_halves(size)):
@@ -813,8 +814,9 @@
     for index in range(tall):
         ring(src.w5, at.tall, u_rows, u_cols, index, index * u_rows).start()
         slope_load(index).start()
+    wide_rows = at.long.shape[1]
     for index in range(long):
-        ring(src.w3, at.long, 128, src.w3.shape[1], index, index * 128).start()
+        ring(src.w3, at.long, wide_rows, src.w3.shape[1], index, index * wide_rows).start()
     for name in loaded:
         load(vars(at)[name]).start()
 
@@ -1169,19 +1171,19 @@
     load(at.t3).wait()
 
     def through_expand(index, carry):
-        ring(src.w3, at.long, 128, ff, index, index * 128).wait()
-        offset = pl.multiple_of(index * 128, 128)
-        d_norm[:, pl.ds(offset, 128)] = back_mul(expand_low[...], at.long[lax.rem(index, long)])
-
-        @pl.when(index + long < D // 128)
+        ring(src.w3, at.long, wide_rows, ff, index, index * wide_rows).wait()
+        offset = pl.multiple_of(index * wide_rows, wide_rows)
+        d_norm[:, pl.ds(offset, wide_rows)] = back_mul(expand_low[...], at.long[lax.rem(index, long)])
+
+        @pl.when(index + long < D // wide_rows)
         def _():
-            ring(src.w3, at.long, 128, ff, index + long, (index + long) * 128).start()
+            ring(src.w3, at.long, wide_rows, ff, index + long, (index + long) * wide_rows).start()
 
         return carry
 
-    loop_work(5.0, D // 128, 2, through_expand)
+    loop_work(5.0, D // wide_rows, 2, through_expand)
     for index in range(long):
-        ring(src.w1, at.long, 128, 3 * D, index, index * 128).start()
+        ring(src.w1, at.long, wide_rows, 3 * D, index, index * wide_rows).start()
     load_stash(src.mid).wait()
     plan.work(2.0, lambda: norm_back(1, merge_low, True))
     load_stash(src.embedded).start()
@@ -1275,9 +1277,12 @@
             delta_row = jnp.concatenate([delta[side : side + 1, :] for side in range(sides)], 1)
             query_acc[...] = jnp.zeros_like(query_acc)
 
-            def block(source, carry):
-                rows = pl.ds(pl.multiple_of(source * tokens, tokens), tokens)
-                key, value = qkv[source, 1, :, lanes], qkv[source, 2, :, lanes]
+            at_once = max(1, KEY_ROWS // tokens)
+            for source in range(0, narrow, at_once):
+                rows = pl.ds(source * tokens, at_once * tokens)
+                some = pl.ds(source, at_once)
+                key = qkv[some, 1, :, lanes].reshape(at_once * tokens, LANES)
+                value = qkv[some, 2, :, lanes].reshape(at_once * tokens, LANES)
                 probs = jnp.exp(back_mul(key, own_query) - log_row)
                 d_probs = back_mul(value, own_upper)
                 d_scores = (probs * (d_probs - delta_row)).astype(BF16)
@@ -1287,9 +1292,7 @@
                 for side in range(sides):
                     spot = slice(side * HD, (side + 1) * HD)
                     query_acc[spot, :] += turned[spot, side * tokens : (side + 1) * tokens]
-                return carry
-
-            lax.fori_loop(0, narrow, block, 0)
+
             parts[who, 0, :, lanes] = (query_acc[...].T * scale).astype(BF16)
         for step in range(narrow):
             plan.work(3.0, functools.partial(one_block, step))
@@ -1312,23 +1315,23 @@
             push(1, pair)
 
     def through_mixer(index, carry):
-        ring(src.w1, at.long, 128, 3 * D, index, index * 128).wait()
+        ring(src.w1, at.long, wide_rows, 3 * D, index, index * wide_rows).wait()
         slot = lax.rem(index, long)
-        value = jnp.zeros((tokens, 128), F32)
+        value = jnp.zeros((tokens, wide_rows), F32)
         for pair in range(head_width // LANES):
             for part in range(3):
                 columns = [part * D + owner * head_width + pair * LANES for owner in range(narrow)]
                 weight = [at.long[slot, :, column : column + LANES] for column in columns]
                 value = value + back_mul(mixed[pair, part], jnp.concatenate(weight, 1))
-        d_norm[:, pl.ds(pl.multiple_of(index * 128, 128), 128)] = value
-
-        @pl.when(index + long < D // 128)
+        d_norm[:, pl.ds(pl.multiple_of(index * wide_rows, wide_rows), wide_rows)] = value
+
+        @pl.when(index + long < D // wide_rows)
         def _():
-            ring(src.w1, at.long, 128, 3 * D, index + long, (index + long) * 128).start()
+            ring(src.w1, at.long, wide_rows, 3 * D, index + long, (index + long) * wide_rows).start()
 
         return carry
 
-    plan.work(4.0, lambda: lax.fori_loop(0, D // 128, through_mixer, 0))
+    plan.work(4.0, lambda: lax.fori_loop(0, D // wide_rows, through_mixer, 0))
     load_stash(src.embedded).wait()
     plan.work(3.0, lambda: norm_back(0, at.embed_low, True))
     at.embed_t[...] = at.embed_low[...].T
@@ -1413,7 +1416,7 @@
         merge_low=pltpu.VMEM((tokens, D), BF16),
         mixed=pltpu.VMEM((head_width // LANES, 3, tokens, narrow * LANES), BF16),
         tall=pltpu.VMEM((4, 256, D), BF16),
-        long=pltpu.VMEM((3, 128, widths[3]), BF16),
+        long=pltpu.VMEM((2, 256, widths[3]), BF16),
         slope_slots=pltpu.VMEM((4, tokens, 256), BF16),
         d_heads=pltpu.VMEM((narrow, tokens, head_width), BF16),
         away=pltpu.VMEM((narrow - 1, tokens, head_width), BF16),

time: 361 us -> 351 us (0.972)
  Pallas kernels: 343 us -> 334 us
    pallas_call x1, Pallas kernels: 190 us -> 180 us  [backward_all(): pl.pallas_call(functools.partial(backward_kernel, items, wide, narrow, le...]
where the time goes in v10:
time: 351 us; the launch traced here: 346 us
  Pallas kernels  334 us (95%)
  local copies, waits for them, and re-layouts  8.28 us (2%)
    pallas_call x1, Pallas kernels, backward_all(): pl.pallas_call(functools.partial(backward_kernel, items, wide, narrow, le...  180 us
    pallas_call x1, Pallas kernels, forward_all(): pl.pallas_call(functools.partial(forward_kernel, items, wide, narrow, lea...  142 us

profile of v10, /device:TPU:0, one launch (start us, length us, event | category | flops | bytes accessed | tf_op | source)
XLA Modules:
  0.0 346.3 jit_solution(6956098172006648112)
XLA Ops:
  0.7 0.0 copy-start.4
  0.7 0.0 copy-start.5
  2.0 1.4 reduce
  3.4 0.2 reshape_squeeze.7
  3.6 0.2 copy.62
  3.8 0.1 reshape.81.mask_ref
  4.0 0.0 copy-done.5
  4.0 0.8 pad.4.refs_7_.refs_18_
  4.8 0.0 copy-done.4
  4.8 0.2 copy.55
  5.0 0.6 reshape_squeeze.6
  5.6 0.4 copy.56
  6.0 0.4 reshape.80.target_ref
  6.5 2.3 copy.59
  8.8 0.0 copy-start.2
  8.8 0.5 reshape.82.weight_ref
  9.3 142.2 %forward.1 = (bf16[4,2,128,3072]{3,2,1,0:T(8,128)(2,1)}, bf16[4,2,128,1024]{3,2,1,0:T(8,128)(2,1)}, bf16[4,2,128,4096]{3,2,1,0:T(8,128)(2,1)}, bf16[4,2,512,1024...) custom-call(f32[32,576]{1,0:T(8,128)} %bitcast.34, ...), custom_call_target="tpu_custom_call" | custom-call | tf_op jit(solution)/shard_map/forward/pallas_call | solution.py:729
  151.5 0.0 copy-done.2
  151.5 0.0 copy-start
  151.5 1.1 copy-done
  152.7 4.9 %render.1 = (bf16[256,768]{1,0:T(8,128)(2,1)S(1)}, f32[8,128]{1,0:T(8,128)S(1)}) custom-call(f32[256,768]{1,0:T(8,128)S(1)} %copy-done, f32[256,768]{1,0:T(8,128)S(1)} %reshape.82.weight_ref, bf16[192,768]{1,0:T(8,128)(2,1)S(1)} %reshape.80.target_ref, s32[64,768]{1,0:T(8,128)S(1)} %reshape.81.mask_ref, s32[2,2048]{1,0:T(2,128)S(1)} %bitcast.24, ...), custom_call_target="tpu_custom_call" | custom-call | tf_op jit(solution)/shard_map/render/pallas_call | solution.py:1572
  157.5 0.0 copy-start.1
  157.6 0.7 copy-done.1
  158.3 0.0 copy-start.3
  158.3 0.6 copy-done.3
  158.9 180.2 %backward.1 = (f32[32,640]{1,0:T(8,128)}, f32[32,3072]{1,0:T(8,128)}, f32[32,1024]{1,0:T(8,128)}, f32[32,4096]{1,0:T(8,128)}, f32[1024,128]{1,0:T(8,128)}, /*index=5*/f32[32,768]{1,0:T(8,128)}, f32[8,128]{1,0:T(8,128)}) custom-call(bf16[1024,3072]{1,0:T(8,128)(2,1)} %bitcast.27, bf16[1024,1024]{1,0:T(8,128)(2,1)} %bitcast.29, bf16[1024,4096]{1,0:T(8,128)(2,1)} %bitcast.25, ...), custom_call_target="tpu_custom_call" | custom-call | tf_op jit(solution)/shard_map/backward/pallas_call | solution.py:1450
  339.1 6.8 %update.1 = (f32[32,576]{1,0:T(8,128)}, f32[32,576]{1,0:T(8,128)}, f32[32,576]{1,0:T(8,128)}, f32[32,3072]{1,0:T(8,128)}, f32[32,3072]{1,0:T(8,128)}, /*index=5*...) custom-call(s32[1]{0:T(128)S(6)} %copy.64.total_ref, ...), custom_call_target="tpu_custom_call" | custom-call | tf_op jit(solution)/shard_map/update/pallas_call | solution.py:1741
Async XLA Ops:
  0.7 4.1 %copy-start.4 = (bf16[1,12,3,4096]{3,2,1,0:T(4,128)(2,1)S(1)}, bf16[1,12,3,4096]{3,2,1,0:T(4,128)(2,1)}, u32[]{:S(2)}) copy-start(bf16[1,12,3,4096]{3,2,1,0:T(4,128)(2,1)} %param.30) | copy-start | bytes 884740
  0.7 3.3 copy-start.5
  8.8 142.7 %copy-start.2 = (s32[1,2,2048]{2,1,0:T(2,128)S(1)}, s32[1,2,2048]{2,1,0:T(2,128)}, u32[]{:S(2)}) copy-start(s32[1,2,2048]{2,1,0:T(2,128)} %param.32) | copy-start | bytes 49156
  151.5 1.1 copy-start
  157.5 0.7 copy-start.1
  158.3 0.6 copy-start.3

commit v11 on v10

--- a/solution.py
+++ b/solution.py
@@ -251,7 +251,7 @@
     barrier = pltpu.get_barrier_semaphore()
     for peer in peers:
         pl.semaphore_signal(barrier, inc=1, device_id=peer, device_id_type=MESH)
-    pl.semaphore_wait(barrier, len(peers))
+    return lambda: pl.semaphore_wait(barrier, len(peers))
 
 
 def normalize(values, gain, shift):
@@ -289,6 +289,7 @@
         copy.start()
         started.append(copy)
 
+    all_here = greet(place.neighbours())
     features = at.s0.shape[1]
     tail = shards[0].shape[1] - LANES
     kinds = at.norm_raw.shape[0]
@@ -297,9 +298,10 @@
     put = (spot == kind + lead).astype(F32).astype(BF16)
     shards[0][:, tail:] = outer_sum(at.norm_raw[...].astype(BF16), put).astype(BF16)
     shards[0][:, 0:features] = at.s0[...].astype(BF16)
-    for source, dest in zip(raw[1:], shards[1:]):
-        dest[...] = source[...].astype(BF16)
-    greet(place.neighbours())
+    shards[1][...] = raw[1][...].astype(BF16)
+    at.padded[...] = jnp.zeros_like(at.padded)
+    at.padded[:, 0:features] = at.patches[...]
+    all_here()
     rows_of = [shard.shape[0] for shard in shards]
 
     def slab(which, node):
@@ -310,13 +312,14 @@
         part = weights[which][:, :, :, columns]
         return part.reshape(-1, part.shape[-1])
 
-    own = []
-    for which in range(6):
-        copy = pltpu.make_async_copy(
+    own = [
+        pltpu.make_async_copy(
             shards[which], weights[which].at[place.chip, place.core, slab(which, me), :], own_sem.at[which]
         )
+        for which in range(6)
+    ]
+    for copy in own[:2]:
         copy.start()
-        own.append(copy)
 
     def remote(item, src, dst, slot, peer):
         return pltpu.make_async_remote_copy(
@@ -434,6 +437,10 @@
 
     plan.refill = refill
     refill()
+    assert all(items[item][0] < 2 for item in range(len(begun)))
+    for which in range(2, 6):
+        shards[which][...] = raw[which][...].astype(BF16)
+        own[which].start()
 
     def need(which, columns=None):
         plan.need(
@@ -472,6 +479,8 @@
         dest[...] = source[...].T
         flush(dest)
 
+    plan.later(2.0, lambda: spread_weights(at.render_w, at.spread))
+    plan.later(3.0, lambda: count_pairs(at.pairs, at.counts))
     need(0)
     width = weights[0].shape[-1]
     kind = lax.broadcasted_iota(jnp.int32, (8, LANES), 0)
@@ -479,11 +488,12 @@
     pick = (spot == kind + lead).astype(F32).astype(BF16)
     gains[...] = back_mul(pick, whole_of(0, pl.ds(width - LANES, LANES)))
     flush(gains)
+    flush(at.padded)
 
     def embed(block):
         cols = pl.ds(block, 256)
         rows = whole_of(0, pl.ds(0, width))[block : block + 256]
-        embedded[:, cols] = back_mul(at.patches[...], rows)
+        embedded[:, cols] = back_mul(at.padded[...], rows)
 
     for block in range(0, D, 256):
         plan.work(0.5, functools.partial(embed, block))
@@ -655,7 +665,17 @@
     for block in range(0, weights[5].shape[-1], 256):
         plan.work(0.7, functools.partial(unpatch, block))
     flush(at.w5)
-    flush(at.gaussians)
+    for entry in list(plan.spare):
+        plan.force(entry)
+
+    def draw():
+        render_block(
+            at.gaussians, at.spread, at.wanted, at.valid, at.counts, at.view, at.total, at.gauss, at.term, at.feat, at.dfeat
+        )
+
+    plan.work(4.0, draw)
+    flush(at.gauss)
+    flush(at.term)
     plan.later(2.0, lambda: turn(at.t5, normed))
     plan.finish()
     for copy in started:
@@ -670,12 +690,15 @@
         copy.wait()
 
 
-def forward_all(shards, norms, patches, lead, wide, narrow):
+def forward_all(shards, norms, patches, scene, wide, narrow):
     tokens = patches.shape[0]
-    widths = [patches.shape[1]] + [shard.shape[1] for shard in shards[1:]]
+    features, kinds = patches.shape[1], norms.shape[0]
+    lead = features % LANES
+    widths = [-(-(features + kinds) // LANES) * LANES] + [shard.shape[1] for shard in shards[1:]]
     heights = [shard.shape[0] * wide * narrow for shard in shards]
     ff = widths[3]
     chips = wide // 2
+    quads, slots_t = tokens // NVIEW, scene[0].shape[0]
     head_width = D // narrow
     items = forward_plan(widths)
     slots = chips + 1 + 2 * (narrow - 1)
@@ -699,9 +722,12 @@
         qkv=((narrow, 3, tokens, head_width), BF16),
         heads_out=((narrow, tokens, head_width), BF16),
         log_sums=((narrow, tokens, LANES), F32),
-        gaussians=((tokens, widths[5]), F32),
+        padded=((tokens, widths[0]), BF16),
+        gauss=((tokens, widths[5]), BF16),
+        term=((8, LANES), F32),
     )
     ins = tuple(dict(s0=0, s1=0, s2=0, s3=0, s4=0, s5=0, norm_raw=0, patches=0))
+    ins += tuple(dict(render_w=0, wanted=0, valid=0, pairs=0, view=0, total=0))
     outs = tuple(shapes)
     extras = dict(
         first_weight=pltpu.VMEM(*full[0]),
@@ -711,6 +737,11 @@
         c3=pltpu.VMEM(shards[3].shape, BF16),
         c4=pltpu.VMEM(shards[4].shape, BF16),
         c5=pltpu.VMEM(shards[5].shape, BF16),
+        gaussians=pltpu.VMEM((tokens, widths[5]), F32),
+        spread=pltpu.VMEM((NVIEW * PP, slots_t * PP), F32),
+        counts=pltpu.VMEM((2 * quads, slots_t * PP), F32),
+        feat=pltpu.VMEM((5 * quads, NVIEW * PP), F32),
+        dfeat=pltpu.VMEM((5 * quads, NVIEW * PP), F32),
         normed=pltpu.VMEM((tokens, D), BF16),
         wave=pltpu.VMEM((tokens, 512), F32),
         away=pltpu.VMEM((narrow - 1, 3, tokens, head_width), BF16),
@@ -729,14 +760,15 @@
     results = pl.pallas_call(
         functools.partial(forward_kernel, items, wide, narrow, lead, ins, outs, scratch),
         out_shape=[jax.ShapeDtypeStruct(*shapes[name]) for name in outs],
-        in_specs=[pl.BlockSpec(memory_space=pltpu.VMEM)] * len(ins),
+        in_specs=[pl.BlockSpec(memory_space=pltpu.VMEM)] * (len(ins) - 2)
+        + [pl.BlockSpec(memory_space=pltpu.SMEM)] * 2,
         out_specs=[anywhere] * len(outs),
         scratch_shapes=[pltpu.VMEM(*shapes[name]) for name in outs] + list(extras.values()),
         compiler_params=pltpu.CompilerParams(
-            collective_id=0, has_side_effects=True, vmem_limit_bytes=60 * MIB
+            collective_id=0, has_side_effects=True, vmem_limit_bytes=63 * MIB
         ),
         name="forward",
-    )(*shards, norms, patches)
+    )(*shards, norms, patches, *scene)
     results = [result.reshape(-1, result.shape[-1]) for result in results[:5]] + list(results[5:])
     return Bag(zip(outs, results))
 
@@ -781,6 +813,10 @@
     stash, d_res, d_norm = at.stash, at.d_res, at.d_norm
     mixed, merge_low, expand_low, shrink_low = at.mixed, at.merge_low, at.expand_low, at.shrink_low
 
+    peers = [(lax.rem(place.w + step, wide), place.n) for step in range(1, wide)]
+    peers += [place.along(step) for step in range(1, narrow)]
+    all_here = greet(peers)
+
     loaded = [name for name in ins if name in scratch]
 
     def load(ref):
@@ -820,9 +856,7 @@
     for name in loaded:
         load(vars(at)[name]).start()
 
-    peers = [(lax.rem(place.w + step, wide), place.n) for step in range(1, wide)]
-    peers += [place.along(step) for step in range(1, narrow)]
-    greet(peers)
+    all_here()
 
     started, guarded = [], []
 
@@ -1460,12 +1494,48 @@
     )(*operands.values())
 
 
+def spread_weights(source, dest):
+    for slot in range(source.shape[0]):
+        for view in range(source.shape[1]):
+            dest[view * PP : (view + 1) * PP, slot * PP : (slot + 1) * PP] = source[slot, view]
+
+
+def count_pairs(pair_ref, counts):
+    quads, span = counts.shape[0] // 2, counts.shape[1]
+    some = 512
+    counts[...] = jnp.zeros_like(counts)
+
+    def one(step, carry):
+        where = pl.ds(pl.multiple_of(step * some, some), some)
+        first, second = pair_ref[0:1, where], pair_ref[1:2, where]
+        least = jnp.minimum(first, second)
+        down = (jnp.abs(first - second) == P_SIZE).astype(jnp.int32)
+        place = quads * PP
+        slot, local = least // place, least % place
+        high = down * quads + local // PP
+        low = slot * PP + local % PP
+        high_hot = (lax.broadcasted_iota(jnp.int32, (2 * quads, some), 0) == high).astype(F32).astype(BF16)
+        low_hot = (lax.broadcasted_iota(jnp.int32, (span, some), 0) == low).astype(F32).astype(BF16)
+        counts[...] += back_mul(high_hot, low_hot)
+        return carry
+
+    lax.fori_loop(0, pair_ref.shape[1] // some, one, 0)
+
+
 def render_kernel(
-    gauss_ref, weight_ref, target_ref, mask_ref, pair_ref, view_ref, total_ref, grad_ref, term_ref, feat, dfeat
+    gauss_ref, weight_ref, target_ref, mask_ref, pair_ref, view_ref, total_ref, grad_ref, term_ref, feat, dfeat, counts
+):
+    count_pairs(pair_ref, counts)
+    render_block(
+        gauss_ref, weight_ref, target_ref, mask_ref, counts, view_ref, total_ref, grad_ref, term_ref, feat, dfeat
+    )
+
+
+def render_block(
+    gauss_ref, weight_ref, target_ref, mask_ref, counts, view_ref, total_ref, grad_ref, term_ref, feat, dfeat
 ):
     quads = gauss_ref.shape[0] // NVIEW
     span = weight_ref.shape[1]
-    pairs = pair_ref.shape[1]
     scale = 1.0 / total_ref[0].astype(F32)
 
     def channel(index):
@@ -1503,16 +1573,6 @@
     below = 1.0 + parts[3]
     depth_out = parts[4] / below
 
-    first, second = pair_ref[0:1, :], pair_ref[1:2, :]
-    least = jnp.minimum(first, second)
-    down = (jnp.abs(first - second) == P_SIZE).astype(jnp.int32)
-    place = quads * PP
-    slot, local = least // place, least % place
-    high = down * quads + local // PP
-    low = slot * PP + local % PP
-    high_hot = (lax.broadcasted_iota(jnp.int32, (2 * quads, pairs), 0) == high).astype(F32).astype(BF16)
-    low_hot = (lax.broadcasted_iota(jnp.int32, (span, pairs), 0) == low).astype(F32).astype(BF16)
-    counts = back_mul(high_hot, low_hot)
     slope = jnp.zeros((quads, span), F32)
     for which, shift in enumerate((1, P_SIZE)):
         count = counts[which * quads : (which + 1) * quads]
@@ -1560,13 +1620,18 @@
         put(index, -2.0 * d_facing * facing / denom * channel(index))
 
 
+def scene_targets(targets, mask, quads):
+    slots = targets.shape[0]
+    wanted = targets.reshape(slots, 3, quads, PP).transpose(1, 2, 0, 3).reshape(3 * quads, slots * PP)
+    valid = mask.reshape(slots, quads, PP).transpose(1, 0, 2).reshape(quads, slots * PP)
+    return wanted, valid
+
+
 def render(gaussians, weights, targets, mask, pairs, view_count, pair_total):
-    rows = gaussians.shape[0]
-    quads = rows // NVIEW
     slots, views = weights.shape[:2]
     spread = weights.transpose(1, 2, 0, 3).reshape(views * PP, slots * PP)
-    wanted = targets.reshape(slots, 3, quads, PP).transpose(1, 2, 0, 3).reshape(3 * quads, slots * PP)
-    valid = mask.reshape(slots, quads, PP).transpose(1, 0, 2).reshape(quads, slots * PP)
+    quads = gaussians.shape[0] // NVIEW
+    wanted, valid = scene_targets(targets, mask, quads)
     vmem = pl.BlockSpec(memory_space=pltpu.VMEM)
     smem = pl.BlockSpec(memory_space=pltpu.SMEM)
     return pl.pallas_call(
@@ -1577,7 +1642,8 @@
         ],
         in_specs=[vmem] * 5 + [smem] * 2,
         out_specs=[vmem] * 2,
-        scratch_shapes=[pltpu.VMEM((5 * quads, views * PP), F32)] * 2,
+        scratch_shapes=[pltpu.VMEM((5 * quads, views * PP), F32)] * 2
+        + [pltpu.VMEM((2 * quads, slots * PP), F32)],
         compiler_params=pltpu.CompilerParams(vmem_limit_bytes=48 * MIB),
         name="render",
     )(gaussians, spread, wanted, valid, pairs, view_count, pair_total)
@@ -1798,12 +1864,23 @@
     by_kernel = mixer_weight.shape[0] % 16 == 0 and shrink_weight.shape[0] % LANES == 0
 
     patches = views.reshape(-1, features)
-    rows = patches.shape[0]
-    patches = jnp.pad(patches, ((0, 0), (0, padded - features)))
     if by_kernel:
         raw = (embed_weight.T,) + masters[1:6]
-        kept = forward_all(raw, norm_params, patches, features % LANES, wide_count, groups)
+        wanted, valid = scene_targets(targets[0], pix_mask[0], patches.shape[0] // NVIEW)
+        scene = (render_w[0], wanted, valid, pairs[0], view_count, pair_total)
+        kept = forward_all(raw, norm_params, patches, scene, wide_count, groups)
+        *sums, totals = backward_all(
+            kept, kept.padded, kept.gauss, kept.term, features % LANES, wide_count, groups
+        )
+        olds = []
+        for triple in zip(masters, firsts, seconds):
+            olds += triple
+        olds[:3] = [old.T for old in olds[:3]]
+        *news, loss, grad_norm = update_all(olds, sums, totals, pair_total, features)
+        news[:3] = [new.T for new in news[:3]]
+        return tuple(news) + (loss[0, 0], grad_norm[0, 0])
     else:
+        patches = jnp.pad(patches, ((0, 0), (0, padded - features)))
         first_shard = jnp.concatenate([embed_weight.T, norm_params.T], 1)
         first_shard = jnp.pad(first_shard.astype(BF16), ((0, 0), (0, fill)))
         shards = [first_shard] + [weight.astype(BF16) for weight in masters[1:6]]
@@ -1812,17 +1889,6 @@
     gauss_low, term = render(
         kept.gaussians, render_w[0], targets[0], pix_mask[0], pairs[0], view_count, pair_total
     )
-    if by_kernel:
-        *sums, totals = backward_all(
-            kept, patches, gauss_low, term, features % LANES, wide_count, groups
-        )
-        olds = []
-        for triple in zip(masters, firsts, seconds):
-            olds += triple
-        olds[:3] = [old.T for old in olds[:3]]
-        *news, loss, grad_norm = update_all(olds, sums, totals, pair_total, features)
-        news[:3] = [new.T for new in news[:3]]
-        return tuple(news) + (loss[0, 0], grad_norm[0, 0])
     sums, loss_sum, square_sum = backward_plain(kept, patches, gauss_low, term, features, kinds)
     first_sum = sums[0].T
     grads = [first_sum[:features]] + list(sums[1:]) + [first_sum[features : features + kinds]]

time: 351 us -> 346 us (0.986)
  local copies, waits for them, and re-layouts: 8.28 us -> 3.6 us
    pallas_call x1 -> x0, Pallas kernels: 4.87 us -> none  [render(): pl.pallas_call(render_kernel, out_shape=[jax.ShapeDtypeStruct(gaussians.s...]
    pallas_call x1, Pallas kernels: 142 us -> 147 us  [forward_all(): pl.pallas_call(functools.partial(forward_kernel, items, wide, narrow, lea...]
where the time goes in v11:
time: 346 us; the launch traced here: 342 us
  Pallas kernels  334 us (97%)
  local copies, waits for them, and re-layouts  3.6 us (1%)
    pallas_call x1, Pallas kernels, backward_all(): pl.pallas_call(functools.partial(backward_kernel, items, wide, narrow, le...  181 us
    pallas_call x1, Pallas kernels, forward_all(): pl.pallas_call(functools.partial(forward_kernel, items, wide, narrow, lea...  147 us

profile of v11, /device:TPU:0, one launch (start us, length us, event | category | flops | bytes accessed | tf_op | source)
XLA Modules:
  0.0 341.8 jit_solution(5961917856415597891)
XLA Ops:
  0.7 0.0 copy-start
  2.0 1.4 reduce
  3.4 0.2 reshape_squeeze.7
  3.6 0.2 copy.57
  3.8 0.8 reshape.72.refs_10_
  4.6 0.0 copy-done
  4.6 0.2 copy.53
  4.9 0.6 reshape_squeeze.6
  5.5 0.4 copy.54
  5.9 1.2 reshape.71.refs_9_
  7.0 146.5 %forward.1 = (bf16[4,2,128,3072]{3,2,1,0:T(8,128)(2,1)}, bf16[4,2,128,1024]{3,2,1,0:T(8,128)(2,1)}, bf16[4,2,128,4096]{3,2,1,0:T(8,128)(2,1)}, bf16[4,2,512,1024...) custom-call(f32[32,576]{1,0:T(8,128)} %bitcast.31, ...), custom_call_target="tpu_custom_call" | custom-call | tf_op jit(solution)/shard_map/forward/pallas_call | solution.py:760
  153.6 181.2 %backward.1 = (f32[32,640]{1,0:T(8,128)}, f32[32,3072]{1,0:T(8,128)}, f32[32,1024]{1,0:T(8,128)}, f32[32,4096]{1,0:T(8,128)}, f32[1024,128]{1,0:T(8,128)}, /*index=5*/f32[32,768]{1,0:T(8,128)}, f32[8,128]{1,0:T(8,128)}) custom-call(bf16[1024,3072]{1,0:T(8,128)(2,1)} %bitcast.24, bf16[1024,1024]{1,0:T(8,128)(2,1)} %bitcast.26, bf16[1024,4096]{1,0:T(8,128)(2,1)} %bitcast.22, ...), custom_call_target="tpu_custom_call" | custom-call | tf_op jit(solution)/shard_map/backward/pallas_call | solution.py:1484
  334.7 6.8 %update.1 = (f32[32,576]{1,0:T(8,128)}, f32[32,576]{1,0:T(8,128)}, f32[32,576]{1,0:T(8,128)}, f32[32,3072]{1,0:T(8,128)}, f32[32,3072]{1,0:T(8,128)}, /*index=5*...) custom-call(s32[1]{0:T(128)S(6)} %copy.59.refs_13_.total_ref, ...), custom_call_target="tpu_custom_call" | custom-call | tf_op jit(solution)/shard_map/update/pallas_call | solution.py:1807
Async XLA Ops:
  0.7 4.0 %copy-start = (bf16[1,12,3,4096]{3,2,1,0:T(4,128)(2,1)S(1)}, bf16[1,12,3,4096]{3,2,1,0:T(4,128)(2,1)}, u32[]{:S(2)}) copy-start(bf16[1,12,3,4096]{3,2,1,0:T(4,128)(2,1)} %param.30) | copy-start | bytes 884740

commit v12 on v11

--- a/solution.py
+++ b/solution.py
@@ -214,8 +214,8 @@
             if not self.fill(self.events[0][0]):
                 self.step()
 
-    def work(self, cost, work):
-        while self.events and self.events[0][0] <= self.now:
+    def work(self, cost, work, rush=False):
+        while not rush and self.events and self.events[0][0] <= self.now:
             self.step()
         self.refill()
         work()
@@ -241,7 +241,7 @@
 LINK = 90e3
 Z_AHEAD = 4.0
 RELAYED = (3, 4)
-KEY_ROWS = 512
+KEY_ROWS = 1024
 Z_EARLY = 1.0
 Z_LATE = 2.0
 TWIN_LINK = 600e3
@@ -1329,7 +1329,7 @@
 
             parts[who, 0, :, lanes] = (query_acc[...].T * scale).astype(BF16)
         for step in range(narrow):
-            plan.work(3.0, functools.partial(one_block, step))
+            plan.work(4.0, functools.partial(one_block, step), step > 0)
             for earlier in range(pair):
                 if earlier not in pushed_pairs and (-2, 0, earlier) in plan.done:
                     pushed_pairs.append(earlier)

time: 346 us -> 345 us (level)
  no operation moved by 1% of the time
where the time goes in v12:
time: 345 us; the launch traced here: 341 us
  Pallas kernels  333 us (97%)
  local copies, waits for them, and re-layouts  3.6 us (1%)
    pallas_call x1, Pallas kernels, backward_all(): pl.pallas_call(functools.partial(backward_kernel, items, wide, narrow, le...  180 us
    pallas_call x1, Pallas kernels, forward_all(): pl.pallas_call(functools.partial(forward_kernel, items, wide, narrow, lea...  147 us

profile of v12, /device:TPU:0, one launch (start us, length us, event | category | flops | bytes accessed | tf_op | source)
XLA Modules:
  0.0 340.5 jit_solution(6118507127149285075)
XLA Ops:
  0.7 0.0 copy-start
  2.0 1.4 reduce
  3.4 0.2 reshape_squeeze.7
  3.6 0.2 copy.57
  3.8 0.8 reshape.72.refs_10_
  4.6 0.0 copy-done
  4.6 0.2 copy.53
  4.9 0.6 reshape_squeeze.6
  5.5 0.4 copy.54
  5.9 1.2 reshape.71.refs_9_
  7.0 146.5 %forward.1 = (bf16[4,2,128,3072]{3,2,1,0:T(8,128)(2,1)}, bf16[4,2,128,1024]{3,2,1,0:T(8,128)(2,1)}, bf16[4,2,128,4096]{3,2,1,0:T(8,128)(2,1)}, bf16[4,2,512,1024...) custom-call(f32[32,576]{1,0:T(8,128)} %bitcast.31, ...), custom_call_target="tpu_custom_call" | custom-call | tf_op jit(solution)/shard_map/forward/pallas_call | solution.py:760
  153.6 179.9 %backward.1 = (f32[32,640]{1,0:T(8,128)}, f32[32,3072]{1,0:T(8,128)}, f32[32,1024]{1,0:T(8,128)}, f32[32,4096]{1,0:T(8,128)}, f32[1024,128]{1,0:T(8,128)}, /*index=5*/f32[32,768]{1,0:T(8,128)}, f32[8,128]{1,0:T(8,128)}) custom-call(bf16[1024,3072]{1,0:T(8,128)(2,1)} %bitcast.24, bf16[1024,1024]{1,0:T(8,128)(2,1)} %bitcast.26, bf16[1024,4096]{1,0:T(8,128)(2,1)} %bitcast.22, ...), custom_call_target="tpu_custom_call" | custom-call | tf_op jit(solution)/shard_map/backward/pallas_call | solution.py:1484
  333.5 6.8 %update.1 = (f32[32,576]{1,0:T(8,128)}, f32[32,576]{1,0:T(8,128)}, f32[32,576]{1,0:T(8,128)}, f32[32,3072]{1,0:T(8,128)}, f32[32,3072]{1,0:T(8,128)}, /*index=5*...) custom-call(s32[1]{0:T(128)S(6)} %copy.59.refs_13_.total_ref, ...), custom_call_target="tpu_custom_call" | custom-call | tf_op jit(solution)/shard_map/update/pallas_call | solution.py:1807
Async XLA Ops:
  0.7 4.0 %copy-start = (bf16[1,12,3,4096]{3,2,1,0:T(4,128)(2,1)S(1)}, bf16[1,12,3,4096]{3,2,1,0:T(4,128)(2,1)}, u32[]{:S(2)}) copy-start(bf16[1,12,3,4096]{3,2,1,0:T(4,128)(2,1)} %param.30) | copy-start | bytes 884740

commit v13 on v12

--- a/solution.py
+++ b/solution.py
@@ -241,7 +241,7 @@
 LINK = 90e3
 Z_AHEAD = 4.0
 RELAYED = (3, 4)
-KEY_ROWS = 1024
+KEY_ROWS = 512
 Z_EARLY = 1.0
 Z_LATE = 2.0
 TWIN_LINK = 600e3

time: 345 us -> 345 us (level)
  no operation moved by 1% of the time
where the time goes in v13:
time: 345 us; the launch traced here: 341 us
  Pallas kernels  333 us (97%)
  local copies, waits for them, and re-layouts  3.6 us (1%)
    pallas_call x1, Pallas kernels, backward_all(): pl.pallas_call(functools.partial(backward_kernel, items, wide, narrow, le...  180 us
    pallas_call x1, Pallas kernels, forward_all(): pl.pallas_call(functools.partial(forward_kernel, items, wide, narrow, lea...  147 us

profile of v13, /device:TPU:0, one launch (start us, length us, event | category | flops | bytes accessed | tf_op | source)
XLA Modules:
  0.0 340.8 jit_solution(255524103408997498)
XLA Ops:
  0.7 0.0 copy-start
  2.0 1.4 reduce
  3.4 0.2 reshape_squeeze.7
  3.6 0.2 copy.57
  3.8 0.8 reshape.72.refs_10_
  4.6 0.0 copy-done
  4.6 0.2 copy.53
  4.9 0.6 reshape_squeeze.6
  5.5 0.4 copy.54
  5.9 1.2 reshape.71.refs_9_
  7.0 146.5 %forward.1 = (bf16[4,2,128,3072]{3,2,1,0:T(8,128)(2,1)}, bf16[4,2,128,1024]{3,2,1,0:T(8,128)(2,1)}, bf16[4,2,128,4096]{3,2,1,0:T(8,128)(2,1)}, bf16[4,2,512,1024...) custom-call(f32[32,576]{1,0:T(8,128)} %bitcast.31, ...), custom_call_target="tpu_custom_call" | custom-call | tf_op jit(solution)/shard_map/forward/pallas_call | solution.py:760
  153.6 180.2 %backward.1 = (f32[32,640]{1,0:T(8,128)}, f32[32,3072]{1,0:T(8,128)}, f32[32,1024]{1,0:T(8,128)}, f32[32,4096]{1,0:T(8,128)}, f32[1024,128]{1,0:T(8,128)}, /*index=5*/f32[32,768]{1,0:T(8,128)}, f32[8,128]{1,0:T(8,128)}) custom-call(bf16[1024,3072]{1,0:T(8,128)(2,1)} %bitcast.24, bf16[1024,1024]{1,0:T(8,128)(2,1)} %bitcast.26, bf16[1024,4096]{1,0:T(8,128)(2,1)} %bitcast.22, ...), custom_call_target="tpu_custom_call" | custom-call | tf_op jit(solution)/shard_map/backward/pallas_call | solution.py:1484
  333.8 6.8 %update.1 = (f32[32,576]{1,0:T(8,128)}, f32[32,576]{1,0:T(8,128)}, f32[32,576]{1,0:T(8,128)}, f32[32,3072]{1,0:T(8,128)}, f32[32,3072]{1,0:T(8,128)}, /*index=5*...) custom-call(s32[1]{0:T(128)S(6)} %copy.59.refs_13_.total_ref, ...), custom_call_target="tpu_custom_call" | custom-call | tf_op jit(solution)/shard_map/update/pallas_call | solution.py:1807
Async XLA Ops:
  0.7 4.0 %copy-start = (bf16[1,12,3,4096]{3,2,1,0:T(4,128)(2,1)S(1)}, bf16[1,12,3,4096]{3,2,1,0:T(4,128)(2,1)}, u32[]{:S(2)}) copy-start(bf16[1,12,3,4096]{3,2,1,0:T(4,128)(2,1)} %param.30) | copy-start | bytes 884740
